TPU v7x, 32 devices: a whole 2x2x4 slice. The times are simulated.
32 devices in a mesh: grp: 2 (over y), row: 8 (over z, x), col: 2 (over core).
Axes of the slice: x: 2, y: 2, z: 4, core: 2. Of those that a mesh axis runs over, the one named last changes fastest.
Arguments:
- acts: bfloat16 [32, 8192], P(('grp', 'row'), 'col'), parts along dimension 0, may hold values from -6 to 6
- grads: bfloat16 [32, 10240], P(('grp', 'row'), 'col'), parts along dimension 0, may hold values from -6 to 6
- eigen_a: bfloat16 [2, 4096, 8192], P('col', 'row'), may hold values from -0.0625 to 0.0625
- eigen_s_rows: bfloat16 [10240, 10240], P('row', 'col'), may hold values from -0.0625 to 0.0625
- doc_lengths: int32 [24], P('grp'), parts along dimension 0, may hold values from 1 to 4, 16 in all
- doc_plan: int32 [24], P('grp'), parts along dimension 0, may hold values from 0 to 5, as said below
Outputs:
- correction: float32 [20480, 8192], P(('grp', 'row'), 'col'), parts along dimension 0
There are 2 independent parts, one for each index of `grp`. A program takes and returns all parts, laid end to end along the dimension named above; an argument that names none is the same for every part. Nothing has to cross between parts.
Inputs may be any that keep to these rules, and one draw needn't show every extreme that they name: `doc_plan`: every one of the 6 sequences receives at least one document.
All inputs are finite; a program needn't handle non-finite values.
Results may differ from a plain program's by a relative error of at most 0.006.
Values may be sent and summed in bfloat16 or wider, within the bound.
No kernel may reach another device: no remote copies, remote signals or barrier semaphores. Data moves between devices by JAX's collectives and lax.ppermute only.
A program may use at most 128 MiB of HBM per device.

v0:
```python
import jax
import jax.numpy as jnp
from jax import lax
from jax.sharding import PartitionSpec as P

N_SEQ = 6


def sequence_index(doc_lengths, doc_plan, total_tokens):
    positions = jnp.arange(total_tokens, dtype=jnp.int32)
    doc_ends = jnp.cumsum(doc_lengths)
    doc_index = jnp.sum((positions[:, None] >= doc_ends[None, :]).astype(jnp.int32), axis=1)
    doc_onehot = (
        doc_index[:, None] == jnp.arange(doc_lengths.shape[0], dtype=jnp.int32)[None, :]
    ).astype(jnp.int32)
    return jnp.sum(doc_onehot * doc_plan[None, :], axis=1)


def body(acts, grads, eigen_a, eigen_s_rows, doc_lengths, doc_plan):
    basis_tile = eigen_a[0]
    act_rows = lax.all_gather(acts, "row", axis=0, tiled=True)
    rotated = lax.dot_general(
        basis_tile,
        lax.all_gather(act_rows, "col", axis=1, tiled=True),
        (((1,), (1,)), ((), ())),
        preferred_element_type=jnp.float32,
    )
    a_block = rotated.astype(jnp.bfloat16)
    a_rot = lax.all_gather(a_block, "row", axis=0, tiled=True)
    grad_terms = lax.dot_general(
        eigen_s_rows,
        lax.all_gather(grads, "row", axis=0, tiled=True),
        (((1,), (1,)), ((), ())),
        preferred_element_type=jnp.float32,
    )
    g_rot = lax.psum(grad_terms, "col").astype(jnp.bfloat16)
    total_tokens = g_rot.shape[1]
    seq_index = sequence_index(doc_lengths, doc_plan, total_tokens)
    order = jnp.argsort(seq_index, stable=True)
    seq_sorted = seq_index[order]
    block_rows = 128
    padding = -total_tokens % block_rows
    g_sorted = jnp.pad(jnp.take(g_rot, order, axis=1), ((0, 0), (0, padding)))
    a_sorted = jnp.pad(jnp.take(a_rot, order, axis=1), ((0, 0), (0, padding)))
    positions = jnp.arange(total_tokens, dtype=jnp.int32)
    previous_seq = jnp.concatenate([seq_sorted[:1], seq_sorted[:-1]])
    is_start = (positions % block_rows == 0) | (seq_sorted != previous_seq)
    segment_total = (total_tokens + block_rows - 1) // block_rows + N_SEQ - 1
    starts = jnp.nonzero(is_start, size=segment_total, fill_value=total_tokens)[0].astype(jnp.int32)
    ends = jnp.concatenate([starts[1:], jnp.array([total_tokens], jnp.int32)])
    segment_seq = seq_sorted[jnp.minimum(starts, total_tokens - 1)]
    block_iota = jnp.arange(block_rows, dtype=jnp.int32)

    def add_segment(step, carry):
        running, correction, last_seq = carry
        start = starts[step]
        finish = ends[step]
        block_first = jnp.minimum(start, total_tokens - 1) // block_rows * block_rows
        g_block = lax.dynamic_slice_in_dim(g_sorted, block_first, block_rows, 1)
        a_block_cols = lax.dynamic_slice_in_dim(a_sorted, block_first, block_rows, 1)
        spot = block_first + block_iota
        inside = ((spot >= start) & (spot < finish)).astype(jnp.bfloat16)
        term = lax.dot_general(
            g_block * inside[None, :],
            a_block_cols,
            (((1,), (1,)), ((), ())),
            preferred_element_type=jnp.float32,
        )
        changed = segment_seq[step] != last_seq
        correction = correction + jnp.where(changed, running * running, jnp.zeros_like(running))
        running = jnp.where(changed, jnp.zeros_like(running), running) + term
        return (running, correction, segment_seq[step])

    zero_grid = jnp.zeros((g_rot.shape[0], a_rot.shape[0]), jnp.float32)
    running, correction, last_seq = lax.fori_loop(
        0, segment_total, add_segment, (zero_grid, zero_grid, segment_seq[0])
    )
    correction = correction + running * running
    return correction / total_tokens


def solution(mesh):
    return jax.shard_map(
        body,
        mesh=mesh,
        in_specs=(
            P(("grp", "row"), "col"),
            P(("grp", "row"), "col"),
            P("col", "row", None),
            P("row", "col"),
            P("grp"),
            P("grp"),
        ),
        out_specs=P(("grp", "row"), "col"),
        check_vma=False,
    )
```

profile of v0, /device:TPU:0, one launch (start us, length us, event | category | flops | bytes accessed | tf_op | source)
XLA Modules:
  0.0 374.1 jit_solution(2561750320197521835)
XLA Ops:
  7.9 32.5 %all-gather.1 = bf16[8,2,4096]{2,1,0:T(2,128)(2,1)S(1)} all-gather(bf16[1,2,4096]{2,1,0:T(2,128)(2,1)} %bitcast.44), channel_id=1, replica_groups=mesh['grp'=2,'row'=8,'col'=2] {'row'}, dimensions={0}, use_global_device_ids=true | all-gather | bytes 147456 | tf_op jit(solution)/shard_map/all_gather | solution.py:21
  40.5 2.0 all_gather.14
  42.5 5.6 %fusion.6 = bf16[512,16]{0,1:T(8,128)(2,1)S(1)} fusion(bf16[16,8192]{1,0:T(8,128)(2,1)S(1)} %all_gather.14, bf16[1,512,8192]{2,1,0:T(8,128)(2,1)} %param.11), kind=kOutput, calls=%fused_computation.15 | convolution fusion | flops 134225920 | bytes 8667136 | tf_op jit(solution)/shard_map/dot_general | solution.py:22
  48.2 30.5 %all_gather.15 = bf16[4096,16]{0,1:T(8,128)(2,1)S(1)} all-gather(bf16[512,16]{0,1:T(8,128)(2,1)S(1)} %fusion.6), channel_id=1, replica_groups=mesh['grp'=2,'row'=8,'col'=2] {'row'}, dimensions={0}, use_global_device_ids=true | all-gather | bytes 147456 | tf_op jit(solution)/shard_map/all_gather | solution.py:29
  79.4 30.8 %all-gather = bf16[8,2,5120]{2,1,0:T(2,128)(2,1)S(1)} all-gather(bf16[1,2,5120]{2,1,0:T(2,128)(2,1)} %bitcast.43), channel_id=1, replica_groups=mesh['grp'=2,'row'=8,'col'=2] {'row'}, dimensions={0}, use_global_device_ids=true | all-gather | bytes 184320 | tf_op jit(solution)/shard_map/all_gather | solution.py:32
  110.3 8.2 %fusion.23 = f32[1280,16]{0,1:T(8,128)S(1)} fusion(bf16[1280,5120]{1,0:T(8,128)(2,1)} %param.12, bf16[16,5120]{1,0:T(8,128)(2,1)S(1)} %reshape.241), kind=kOutput, calls=%fused_computation.57 | convolution fusion | flops 209715200 | bytes 13352960 | tf_op jit(solution)/shard_map/dot_general | solution.py:30
  118.5 3.6 psum.7
  123.8 228.2 %while.20 = (s32[]{:T(128)}, f32[1280,4096]{1,0:T(8,128)}, f32[1280,4096]{1,0:T(8,128)}, s32[]{:T(128)}, s32[6]{0:T(128)S(1)}, /*index=5*/s32[6]{0:T(128)S(1)}, ...) while((s32[]{:T(128)}, f32[1280,4096]{1,0:T(8,128)}, ...), condition=%wide.region_10.11_spmd.clone, body=%wide.region_9.10_spmd.clone.sunk | while | flops 1384284800 | bytes 106234776 | solution.py:75
  127.0 1.3 and_convert_fusion.2
  128.2 9.3 %select_add_fusion.5 = f32[1280,4096]{1,0:T(8,128)} fusion(f32[1280,4096]{1,0:T(8,128)} %get-tuple-element.414, f32[1280,4096]{1,0:T(8,128)} %get-tuple-element.413, pred[]{:T(512)S(6)} %compare.31, pred[]{:T(512)S(6)} %ne.132), kind=kLoop, calls=%fused_computation.6.clone.1 | loop fusion | flops 26214400 | bytes 62914560 | tf_op jit(solution)/shard_map/while/body/eval_jaxpr/add | solution.py:70
  137.5 9.1 %select_add_fusion.4 = f32[1280,4096]{1,0:T(8,128)} fusion(f32[1280,4096]{1,0:T(8,128)} %get-tuple-element.413, bf16[4096,128]{1,0:T(8,128)(2,1)S(1)} %get-tuple-element.436, pred[]{:T(512)S(6)} %compare.31, pred[]{:T(512)S(6)} %ne.132, bf16[1280,128]{1,0:T(8,128)(2,1)S(1)} %get-tuple-element.435, bf16[128]{0:T(256)(128)(2,1)S(1)} %and_convert_fusion.2), kind=kOutput, calls=%fused_computation.7.clone.1 | convolution fusion | flops 1358069760 | bytes 43319552 | tf_op jit(solution)/shard_map/while/body/eval_jaxpr/dot_general | solution.py:63
  150.3 1.3 and_convert_fusion.2
  151.6 22.3 %select_add_fusion.5 = f32[1280,4096]{1,0:T(8,128)} fusion(f32[1280,4096]{1,0:T(8,128)} %get-tuple-element.414, f32[1280,4096]{1,0:T(8,128)} %get-tuple-element.413, pred[]{:T(512)S(6)} %compare.31, pred[]{:T(512)S(6)} %ne.132), kind=kLoop, calls=%fused_computation.6.clone.1 | loop fusion | flops 26214400 | bytes 62914560 | tf_op jit(solution)/shard_map/while/body/eval_jaxpr/add | solution.py:70
  173.9 13.7 %select_add_fusion.4 = f32[1280,4096]{1,0:T(8,128)} fusion(f32[1280,4096]{1,0:T(8,128)} %get-tuple-element.413, bf16[4096,128]{1,0:T(8,128)(2,1)S(1)} %get-tuple-element.436, pred[]{:T(512)S(6)} %compare.31, pred[]{:T(512)S(6)} %ne.132, bf16[1280,128]{1,0:T(8,128)(2,1)S(1)} %get-tuple-element.435, bf16[128]{0:T(256)(128)(2,1)S(1)} %and_convert_fusion.2), kind=kOutput, calls=%fused_computation.7.clone.1 | convolution fusion | flops 1358069760 | bytes 43319552 | tf_op jit(solution)/shard_map/while/body/eval_jaxpr/dot_general | solution.py:63
  192.5 22.3 %select_add_fusion.5 = f32[1280,4096]{1,0:T(8,128)} fusion(f32[1280,4096]{1,0:T(8,128)} %get-tuple-element.414, f32[1280,4096]{1,0:T(8,128)} %get-tuple-element.413, pred[]{:T(512)S(6)} %compare.31, pred[]{:T(512)S(6)} %ne.132), kind=kLoop, calls=%fused_computation.6.clone.1 | loop fusion | flops 26214400 | bytes 62914560 | tf_op jit(solution)/shard_map/while/body/eval_jaxpr/add | solution.py:70
  214.8 13.7 %select_add_fusion.4 = f32[1280,4096]{1,0:T(8,128)} fusion(f32[1280,4096]{1,0:T(8,128)} %get-tuple-element.413, bf16[4096,128]{1,0:T(8,128)(2,1)S(1)} %get-tuple-element.436, pred[]{:T(512)S(6)} %compare.31, pred[]{:T(512)S(6)} %ne.132, bf16[1280,128]{1,0:T(8,128)(2,1)S(1)} %get-tuple-element.435, bf16[128]{0:T(256)(128)(2,1)S(1)} %and_convert_fusion.2), kind=kOutput, calls=%fused_computation.7.clone.1 | convolution fusion | flops 1358069760 | bytes 43319552 | tf_op jit(solution)/shard_map/while/body/eval_jaxpr/dot_general | solution.py:63
  232.2 1.3 and_convert_fusion.2
  233.5 22.3 %select_add_fusion.5 = f32[1280,4096]{1,0:T(8,128)} fusion(f32[1280,4096]{1,0:T(8,128)} %get-tuple-element.414, f32[1280,4096]{1,0:T(8,128)} %get-tuple-element.413, pred[]{:T(512)S(6)} %compare.31, pred[]{:T(512)S(6)} %ne.132), kind=kLoop, calls=%fused_computation.6.clone.1 | loop fusion | flops 26214400 | bytes 62914560 | tf_op jit(solution)/shard_map/while/body/eval_jaxpr/add | solution.py:70
  255.8 13.7 %select_add_fusion.4 = f32[1280,4096]{1,0:T(8,128)} fusion(f32[1280,4096]{1,0:T(8,128)} %get-tuple-element.413, bf16[4096,128]{1,0:T(8,128)(2,1)S(1)} %get-tuple-element.436, pred[]{:T(512)S(6)} %compare.31, pred[]{:T(512)S(6)} %ne.132, bf16[1280,128]{1,0:T(8,128)(2,1)S(1)} %get-tuple-element.435, bf16[128]{0:T(256)(128)(2,1)S(1)} %and_convert_fusion.2), kind=kOutput, calls=%fused_computation.7.clone.1 | convolution fusion | flops 1358069760 | bytes 43319552 | tf_op jit(solution)/shard_map/while/body/eval_jaxpr/dot_general | solution.py:63
  274.5 22.3 %select_add_fusion.5 = f32[1280,4096]{1,0:T(8,128)} fusion(f32[1280,4096]{1,0:T(8,128)} %get-tuple-element.414, f32[1280,4096]{1,0:T(8,128)} %get-tuple-element.413, pred[]{:T(512)S(6)} %compare.31, pred[]{:T(512)S(6)} %ne.132), kind=kLoop, calls=%fused_computation.6.clone.1 | loop fusion | flops 26214400 | bytes 62914560 | tf_op jit(solution)/shard_map/while/body/eval_jaxpr/add | solution.py:70
  296.8 13.7 %select_add_fusion.4 = f32[1280,4096]{1,0:T(8,128)} fusion(f32[1280,4096]{1,0:T(8,128)} %get-tuple-element.413, bf16[4096,128]{1,0:T(8,128)(2,1)S(1)} %get-tuple-element.436, pred[]{:T(512)S(6)} %compare.31, pred[]{:T(512)S(6)} %ne.132, bf16[1280,128]{1,0:T(8,128)(2,1)S(1)} %get-tuple-element.435, bf16[128]{0:T(256)(128)(2,1)S(1)} %and_convert_fusion.2), kind=kOutput, calls=%fused_computation.7.clone.1 | convolution fusion | flops 1358069760 | bytes 43319552 | tf_op jit(solution)/shard_map/while/body/eval_jaxpr/dot_general | solution.py:63
  315.5 22.3 %select_add_fusion.5 = f32[1280,4096]{1,0:T(8,128)} fusion(f32[1280,4096]{1,0:T(8,128)} %get-tuple-element.414, f32[1280,4096]{1,0:T(8,128)} %get-tuple-element.413, pred[]{:T(512)S(6)} %compare.31, pred[]{:T(512)S(6)} %ne.132), kind=kLoop, calls=%fused_computation.6.clone.1 | loop fusion | flops 26214400 | bytes 62914560 | tf_op jit(solution)/shard_map/while/body/eval_jaxpr/add | solution.py:70
  337.7 13.7 %select_add_fusion.4 = f32[1280,4096]{1,0:T(8,128)} fusion(f32[1280,4096]{1,0:T(8,128)} %get-tuple-element.413, bf16[4096,128]{1,0:T(8,128)(2,1)S(1)} %get-tuple-element.436, pred[]{:T(512)S(6)} %compare.31, pred[]{:T(512)S(6)} %ne.132, bf16[1280,128]{1,0:T(8,128)(2,1)S(1)} %get-tuple-element.435, bf16[128]{0:T(256)(128)(2,1)S(1)} %and_convert_fusion.2), kind=kOutput, calls=%fused_computation.7.clone.1 | convolution fusion | flops 1358069760 | bytes 43319552 | tf_op jit(solution)/shard_map/while/body/eval_jaxpr/dot_general | solution.py:63
  352.0 22.1 %add_multiply_fusion = f32[1280,4096]{1,0:T(8,128)} fusion(f32[1280,4096]{1,0:T(8,128)} %get-tuple-element.251, f32[1280,4096]{1,0:T(8,128)} %get-tuple-element.252), kind=kLoop, calls=%fused_computation.12 | loop fusion | flops 15728640 | bytes 62914560 | tf_op jit(solution)/shard_map/div | solution.py:79
  (59 shorter events, 25.3 us)
where the time goes:
time: 375 us; the launch traced here: 374 us
  other arithmetic  157 us (42%)
  blocking collectives  99.5 us (27%)
  matrix products  91.3 us (24%)
  local copies, waits for them, and re-layouts  15 us (4%)
  loops' own time  11.2 us (3%)
    add x6, other arithmetic, add_segment(): correction + jnp.where(changed, running * running, jnp.zeros_like(running))  121 us
    dot_general x6, matrix products, add_segment(): lax.dot_general(g_block * inside[None, :], a_block_cols, (((1,), (1,)), (...  77.5 us
    all_gather x1, blocking collectives, body(): act_rows = lax.all_gather(acts, 'row', axis=0, tiled=True)  32.5 us
    all_gather x1, blocking collectives, body(): lax.all_gather(grads, 'row', axis=0, tiled=True)  30.8 us
    all_gather x1, blocking collectives, body(): a_rot = lax.all_gather(a_block, 'row', axis=0, tiled=True)  30.5 us
    div x1, other arithmetic, body(): return correction / total_tokens  22.1 us
    another operation x1, loops' own time, body(): lax.fori_loop(0, segment_total, add_segment, (zero_grid, zero_grid, segme...  11.2 us
    dot_general x1, matrix products, body(): lax.dot_general(eigen_s_rows, lax.all_gather(grads, 'row', axis=0, tiled=...  8.2 us

commit v1 on v0

v1 whole, which is shorter than its diff:
```python
import functools
import jax
import jax.numpy as jnp
from jax import lax
from jax.experimental import pallas as pl
from jax.experimental.pallas import tpu as pltpu
from jax.sharding import PartitionSpec as P

N_SEQ = 6
PAIR_ROWS = 80
BF16 = jnp.bfloat16
F32 = jnp.float32
I32 = jnp.int32
NT = (((1,), (1,)), ((), ()))
VMEM_LIMIT = 50 * 1024 * 1024


def iota(shape, dim):
    return lax.broadcasted_iota(I32, shape, dim)


def dot(a, b, dims=(((1,), (0,)), ((), ()))):
    return lax.dot_general(a, b, dims, preferred_element_type=F32)


def sequence_index(doc_lengths, doc_plan, total_tokens):
    positions = jnp.arange(total_tokens, dtype=I32)
    doc_ends = jnp.cumsum(doc_lengths)
    doc_index = jnp.sum((positions[:, None] >= doc_ends[None, :]).astype(I32), axis=1)
    doc_onehot = (doc_index[:, None] == jnp.arange(doc_lengths.shape[0], dtype=I32)[None, :]).astype(I32)
    return jnp.sum(doc_onehot * doc_plan[None, :], axis=1)


def general_body(acts, grads, eigen_a, eigen_s_rows, doc_lengths, doc_plan):
    act_rows = lax.all_gather(acts, "row", axis=0, tiled=True)
    act_full = lax.all_gather(act_rows, "col", axis=1, tiled=True)
    a_block = dot(eigen_a[0], act_full, NT).astype(BF16)
    a_rot = lax.all_gather(a_block, "row", axis=0, tiled=True)
    grad_terms = dot(eigen_s_rows, lax.all_gather(grads, "row", axis=0, tiled=True), NT)
    g_rot = lax.psum(grad_terms, "col").astype(BF16)
    total_tokens = g_rot.shape[1]
    seq_index = sequence_index(doc_lengths, doc_plan, total_tokens)
    correction = jnp.zeros((g_rot.shape[0], a_rot.shape[0]), F32)
    for sequence in range(N_SEQ):
        inside = (seq_index == sequence).astype(BF16)
        term = dot(g_rot * inside[None, :], a_rot, NT)
        correction = correction + term * term
    return correction / total_tokens


def pairs_kernel(row_ref, len_ref, plan_ref, s1a_ref, s2a_ref, s1g_ref, s2g_ref, perm_ref):
    docs = len_ref.shape[1]
    tokens = perm_ref.shape[0]
    grid_pairs = tokens * tokens
    me = row_ref[0]
    upper = (iota((docs, docs), 0) <= iota((docs, docs), 1)).astype(F32)
    ends = dot(jnp.broadcast_to(len_ref[...].astype(F32), (8, docs)), upper)[0:1]
    position = iota((tokens, docs), 0).astype(F32)
    doc = jnp.sum((ends <= position).astype(F32), axis=1, keepdims=True)
    onehot = doc == iota((tokens, docs), 1).astype(F32)
    seq = jnp.sum(jnp.where(onehot, plan_ref[...].astype(F32), 0.0), axis=1, keepdims=True)
    p_lane = iota((tokens, grid_pairs), 1)
    t_sub = iota((tokens, grid_pairs), 0)
    first = lax.div(p_lane, tokens)
    second = lax.rem(p_lane, tokens)
    seq_first = jnp.sum(jnp.where(first == t_sub, seq, 0.0), axis=0, keepdims=True)
    seq_second = jnp.sum(jnp.where(second == t_sub, seq, 0.0), axis=0, keepdims=True)
    valid = (seq_first == seq_second) & (first[0:1] <= second[0:1])
    before = (iota((grid_pairs, grid_pairs), 0) < iota((grid_pairs, grid_pairs), 1)).astype(BF16)
    rank = dot(jnp.broadcast_to(valid.astype(F32), (8, grid_pairs)).astype(BF16), before)[0:1]
    place = jnp.where(valid, rank, -1.0)
    pick = (iota((PAIR_ROWS, grid_pairs), 0).astype(F32) == place).astype(BF16)
    p_sub = iota((grid_pairs, tokens), 0)
    t_lane = iota((grid_pairs, tokens), 1)
    is_first = lax.div(p_sub, tokens) == t_lane
    is_second = lax.rem(p_sub, tokens) == t_lane
    factor = jnp.where(lax.div(p_sub, tokens) == lax.rem(p_sub, tokens), 1.0, 2.0)
    s1 = dot(pick, jnp.where(is_first, 1.0, 0.0).astype(BF16)).astype(BF16)
    s1_scaled = dot(pick, jnp.where(is_first, factor, 0.0).astype(BF16)).astype(BF16)
    s2 = dot(pick, jnp.where(is_second, 1.0, 0.0).astype(BF16)).astype(BF16)
    token = iota((tokens, tokens), 0)
    slot = iota((tokens, tokens), 1)
    source = ((me + 8 - 2 * (slot >> 2)) & 7) ^ ((slot >> 1) & 1)
    perm = (token == 2 * source + (slot & 1)).astype(BF16)
    s1a_ref[...] = s1
    s2a_ref[...] = s2
    s1g_ref[...] = dot(s1_scaled, perm).astype(BF16)
    s2g_ref[...] = dot(s2, perm).astype(BF16)
    perm_ref[...] = perm


def make_pairs(me, doc_lengths, doc_plan, tokens):
    vmem = pl.BlockSpec(memory_space=pltpu.VMEM)
    sel = jax.ShapeDtypeStruct((PAIR_ROWS, tokens), BF16)
    return pl.pallas_call(
        pairs_kernel,
        out_shape=(sel, sel, sel, sel, jax.ShapeDtypeStruct((tokens, tokens), BF16)),
        in_specs=[pl.BlockSpec(memory_space=pltpu.SMEM), vmem, vmem],
        out_specs=(vmem,) * 5,
        cost_estimate=pl.CostEstimate(flops=2_000_000, bytes_accessed=40_000, transcendentals=0),
        name="pairs",
    )(me, doc_lengths[None, :], doc_plan[None, :])


def assemble_kernel(width, p0, p1, p2, p3, acts_ref, grads_ref):
    rows = []
    for piece in (p0, p1, p2, p3):
        for side in range(2):
            rows.append(piece[side].astype(F32))
    whole = jnp.concatenate(rows, axis=0).astype(BF16)
    acts_ref[...] = whole[:, :width]
    grads_ref[...] = whole[:, width:]


def assemble(pieces, width):
    tokens = sum(p.shape[0] * p.shape[1] for p in pieces)
    total = pieces[0].shape[2]
    vmem = pl.BlockSpec(memory_space=pltpu.VMEM)
    return pl.pallas_call(
        functools.partial(assemble_kernel, width),
        out_shape=(
            jax.ShapeDtypeStruct((tokens, width), BF16),
            jax.ShapeDtypeStruct((tokens, total - width), BF16),
        ),
        in_specs=[vmem] * 4,
        out_specs=(vmem, vmem),
        cost_estimate=pl.CostEstimate(flops=1_000_000, bytes_accessed=600_000, transcendentals=0),
        name="assemble",
    )(*pieces)


def rotate_first_kernel(half_ref, w_ref, x_ref, o_ref):
    o_ref[...] = dot(w_ref[0], x_ref[...], NT)


def rotate_second_kernel(half_ref, w_ref, x_ref, part_ref, perm_ref, o_ref):
    total = (dot(w_ref[0], x_ref[...], NT) + part_ref[...]).astype(BF16)
    mine = dot(perm_ref[...], total, NT).astype(BF16)
    for row in range(o_ref.shape[0]):
        o_ref[row] = mine


def rotate_acts(eigen_a, half, x, part=None, perm=None, copies=0, block=128):
    _, features, _ = eigen_a.shape
    tokens, depth = x.shape
    w_spec = pl.BlockSpec((1, block, depth), lambda i, h: (0, i, h[0]))
    x_spec = pl.BlockSpec((tokens, depth), lambda i, h: (0, 0))
    part_spec = pl.BlockSpec((block, tokens), lambda i, h: (i, 0))
    cost = pl.CostEstimate(
        flops=2 * features * depth * 256, bytes_accessed=features * depth * 2, transcendentals=0
    )
    params = pltpu.CompilerParams(vmem_limit_bytes=24 * 1024 * 1024)
    if part is None:
        return pl.pallas_call(
            rotate_first_kernel,
            out_shape=jax.ShapeDtypeStruct((features, tokens), F32),
            grid_spec=pltpu.PrefetchScalarGridSpec(
                num_scalar_prefetch=1,
                grid=(features // block,),
                in_specs=[w_spec, x_spec],
                out_specs=part_spec,
            ),
            compiler_params=params,
            cost_estimate=cost,
            name="rotate_first",
        )(half, eigen_a, x)
    return pl.pallas_call(
        rotate_second_kernel,
        out_shape=jax.ShapeDtypeStruct((copies, tokens, features), BF16),
        grid_spec=pltpu.PrefetchScalarGridSpec(
            num_scalar_prefetch=1,
            grid=(features // block,),
            in_specs=[w_spec, x_spec, part_spec, pl.BlockSpec((tokens, tokens), lambda i, h: (0, 0))],
            out_specs=pl.BlockSpec((copies, tokens, block), lambda i, h: (0, 0, i)),
        ),
        compiler_params=params,
        cost_estimate=cost,
        name="rotate_second",
    )(half, eigen_a, x, part, perm)


def rotate_grads_kernel(w_ref, x_ref, o_ref):
    o_ref[...] = dot(w_ref[...], x_ref[...], NT).T


def rotate_grads(eigen_s, x, block=128):
    features, depth = eigen_s.shape
    tokens = x.shape[0]
    return pl.pallas_call(
        rotate_grads_kernel,
        out_shape=jax.ShapeDtypeStruct((tokens, features), F32),
        grid=(features // block,),
        in_specs=[
            pl.BlockSpec((block, depth), lambda i: (i, 0)),
            pl.BlockSpec((tokens, depth), lambda i: (0, 0)),
        ],
        out_specs=pl.BlockSpec((tokens, block), lambda i: (0, i)),
        compiler_params=pltpu.CompilerParams(vmem_limit_bytes=24 * 1024 * 1024),
        cost_estimate=pl.CostEstimate(
            flops=2 * features * depth * 256, bytes_accessed=features * depth * 2, transcendentals=0
        ),
        name="rotate_grads",
    )(eigen_s, x)


def split(x):
    high = x.astype(BF16)
    low = (x - high.astype(F32)).astype(BF16)
    return high, low


def correct_kernel(tokens, own_ref, other_ref, a_ref, s1a_ref, s2a_ref, s1g_ref, s2g_ref, o_ref, g_pairs):
    @pl.when(pl.program_id(0) == 0)
    def _():
        g_rot = (own_ref[...] + other_ref[...]).astype(BF16)
        product = dot(s1g_ref[...], g_rot) * dot(s2g_ref[...], g_rot) * (1.0 / tokens)
        high, low = split(product)
        g_pairs[...] = jnp.concatenate([high, high, low], axis=0).T

    a_rot = a_ref[0]
    high, low = split(dot(s1a_ref[...], a_rot) * dot(s2a_ref[...], a_rot))
    a_pairs = jnp.concatenate([high, low, high], axis=0)
    o_ref[...] = dot(g_pairs[...], a_pairs)


def correct(own, other, a_all, s1a, s2a, s1g, s2g):
    tokens, rows = own.shape
    n_row, _, width = a_all.shape
    block = 256
    per = width // block
    g_spec = pl.BlockSpec((tokens, rows), lambda i: (0, 0))
    s_spec = pl.BlockSpec((PAIR_ROWS, tokens), lambda i: (0, 0))
    return pl.pallas_call(
        functools.partial(correct_kernel, tokens),
        out_shape=jax.ShapeDtypeStruct((rows, n_row * width), F32),
        grid=(n_row * per,),
        in_specs=[
            g_spec,
            g_spec,
            pl.BlockSpec((1, tokens, block), lambda i: (i // per, 0, i % per)),
            s_spec,
            s_spec,
            s_spec,
            s_spec,
        ],
        out_specs=pl.BlockSpec((rows, block), lambda i: (0, i)),
        scratch_shapes=[pltpu.VMEM((rows, 3 * PAIR_ROWS), BF16)],
        compiler_params=pltpu.CompilerParams(vmem_limit_bytes=VMEM_LIMIT),
        cost_estimate=pl.CostEstimate(
            flops=2 * rows * n_row * width * 256, bytes_accessed=rows * n_row * width * 4, transcendentals=0
        ),
        name="correct",
    )(own, other, a_all, s1a, s2a, s1g, s2g)


def few_tokens_body(acts, grads, eigen_a, eigen_s_rows, doc_lengths, doc_plan):
    n_row = 8
    tokens = n_row * acts.shape[0]
    me = lax.axis_index("row").astype(I32)[None]
    col = lax.axis_index("col").astype(I32)[None]
    width = acts.shape[1]

    payload = jnp.concatenate([acts, grads], axis=1)
    beside = lax.ppermute(payload, "row", [(i, i ^ 1) for i in range(n_row)])
    both = jnp.stack([payload, beside])
    pieces = [both] + [
        lax.ppermute(both, "row", [(i, (i + 2 * k) % n_row) for i in range(n_row)]) for k in range(1, 4)
    ]
    s1a, s2a, s1g, s2g, perm = make_pairs(me, doc_lengths, doc_plan, tokens)
    acts_own, grads_own = assemble(pieces, width)
    acts_other = lax.ppermute(acts_own, "col", [(0, 1), (1, 0)])
    part = rotate_acts(eigen_a, col, acts_own)
    copies = rotate_acts(eigen_a, 1 - col, acts_other, part, perm, n_row)
    a_all = lax.all_to_all(copies, "row", 0, 0)
    g_own = rotate_grads(eigen_s_rows, grads_own)
    g_other = lax.ppermute(g_own, "col", [(0, 1), (1, 0)])
    return correct(g_own, g_other, a_all, s1a, s2a, s1g, s2g)


def solution(mesh):
    def body(acts, *rest):
        n_row = mesh.shape["row"]
        tokens = n_row * acts.shape[0]
        most = tokens - (N_SEQ - 1)
        pairs = most * (most + 1) // 2 + N_SEQ - 1
        few = n_row == 8 and acts.shape[0] == 2 and mesh.shape["col"] == 2 and pairs <= PAIR_ROWS
        return (few_tokens_body if few else general_body)(acts, *rest)

    return jax.shard_map(
        body,
        mesh=mesh,
        in_specs=(
            P(("grp", "row"), "col"),
            P(("grp", "row"), "col"),
            P("col", "row", None),
            P("row", "col"),
            P("grp"),
            P("grp"),
        ),
        out_specs=P(("grp", "row"), "col"),
        check_vma=False,
    )
```

time: 375 us -> 62.2 us (0.17)
  other arithmetic: 157 us -> 0.1 us
  blocking collectives: 99.5 us -> 0 us
  matrix products: 91.3 us -> 0 us
  Pallas kernels: 0 us -> 27.2 us
  starting transfers between devices: 0 us -> 13.1 us
  loops' own time: 11.2 us -> 0 us
  waiting for transfers between devices: 0 us -> 8.1 us
    add x6 -> x0, other arithmetic: 121 us -> none  [add_segment(): correction + jnp.where(changed, running * running, jnp.zeros_like(running))]
    all_gather x4 -> x0, blocking collectives: 95.8 us -> none  [the longest x1 32.5 us: body(): act_rows = lax.all_gather(acts, 'row', axis=0, tiled=True)]
    dot_general x8 -> x0, matrix products: 91.3 us -> none  [the longest x6 77.5 us: add_segment(): lax.dot_general(g_block * inside[None, :], a_block_cols, (((1,), (1,)), (...]
    pallas_call x0 -> x6, Pallas kernels: none -> 27.2 us  [the longest x1 13.2 us: correct(): pl.pallas_call(functools.partial(correct_kernel, tokens), out_shape=jax.S...]
    div x1 -> x0, other arithmetic: 22.1 us -> none  [body(): return correction / total_tokens]
    unnamed x4 -> x29, local copies, waits for them, and re-layouts: 0.81 us -> 12.4 us
    another operation x1 -> x0, loops' own time: 11.2 us -> none  [body(): lax.fori_loop(0, segment_total, add_segment, (zero_grid, zero_grid, segme...]
    dynamic_slice x18 -> x0, local copies, waits for them, and re-layouts: 11.2 us -> none  [the longest x6 3.96 us: add_segment(): start = starts[step]]
  transfers between devices with their start and end apart: 0 -> 7, of which waited for: 0 -> 5; matrix products, arithmetic and copies ran while one was open for 0% -> 0% of each run, Pallas kernels for 0% -> 15%
where the time goes in v1:
time: 62.2 us; the launch traced here: 61.7 us
  Pallas kernels  27.2 us (44%)
  local copies, waits for them, and re-layouts  13.2 us (21%)
  starting transfers between devices  13.1 us (21%)
  waiting for transfers between devices  8.1 us (13%)
    pallas_call x1, Pallas kernels, correct(): pl.pallas_call(functools.partial(correct_kernel, tokens), out_shape=jax.S...  13.2 us
    unnamed x29, local copies, waits for them, and re-layouts  12.4 us
    ppermute x3, starting transfers between devices, few_tokens_body(): lax.ppermute(both, 'row', [(i, (i + 2 * k) % n_row) for i in range(n_row)])  5.2 us
    pallas_call x1, Pallas kernels, rotate_grads(): pl.pallas_call(rotate_grads_kernel, out_shape=jax.ShapeDtypeStruct((token...  5.17 us
    ppermute x3, waiting for transfers between devices, few_tokens_body(): lax.ppermute(both, 'row', [(i, (i + 2 * k) % n_row) for i in range(n_row)])  5.13 us
    all_to_all x1, starting transfers between devices, few_tokens_body(): a_all = lax.all_to_all(copies, 'row', 0, 0)  4.54 us
    pallas_call x1, Pallas kernels, rotate_acts(): pl.pallas_call(rotate_second_kernel, out_shape=jax.ShapeDtypeStruct((copi...  3.03 us
    ppermute x1, starting transfers between devices, few_tokens_body(): beside = lax.ppermute(payload, 'row', [(i, i ^ 1) for i in range(n_row)])  3 us
  transfers between devices with their start and end apart: 7, of which 5 were waited for; matrix products, arithmetic and copies ran while one was open for 0% of the time, Pallas kernels for 15%

profile of v1, /device:TPU:0, one launch (start us, length us, event | category | flops | bytes accessed | tf_op | source)
XLA Modules:
  0.0 61.7 jit_solution(1055634995999629109)
XLA Ops:
  0.0 0.7 %constant_dynamic-update-slice_fusion.1 = bf16[2,9216]{1,0:T(2,128)(2,1)S(1)} fusion(bf16[2,4096]{1,0:T(2,128)(2,1)} %param.6), kind=kLoop, calls=%fused_computation.2 | loop fusion | bytes 32768
  0.7 0.8 %constant_dynamic-update-slice_fusion = bf16[2,9216]{1,0:T(2,128)(2,1)S(1)} fusion(bf16[2,9216]{1,0:T(2,128)(2,1)S(1)} %constant_dynamic-update-slice_fusion.1, bf16[2,5120]{1,0:T(2,128)(2,1)} %param.7), kind=kLoop, calls=%fused_computation.1 | loop fusion | bytes 40960 | tf_op jit(solution)/shard_map/concatenate | solution.py:263
  1.5 3.0 %collective-permute-start = (bf16[2,9216]{1,0:T(2,128)(2,1)S(1)}, bf16[2,9216]{1,0:T(2,128)(2,1)S(1)}, u32[]{:S(2)}, u32[]{:S(2)}) collective-permute-start(bf16[2,9216]{1,0:T(2,128)(2,1)S(1)} %constant_dynamic-update-slice_fusion), channel_id=1, source_target_pairs={{0,2},{2,0},{4,6},{6,4},{8,10},{10,8},{12,14},{14,12},{1,3},{3,1},... | collective-permute-start | bytes 110600 | tf_op jit(solution)/shard_map/ppermute | solution.py:264
  4.5 1.9 %collective-permute-done = bf16[2,9216]{1,0:T(2,128)(2,1)S(1)} collective-permute-done((bf16[2,9216]{1,0:T(2,128)(2,1)S(1)}, bf16[2,9216]{1,0:T(2,128)(2,1)S(1)}, u32[]{:S(2)}, u32[]{:S(2)}) %collective-permute-start) | collective-permute-done | bytes 36896 | tf_op jit(solution)/shard_map/ppermute | solution.py:264
  6.5 4.2 %collective-permute-start.3 = (bf16[2,2,9216]{2,1,0:T(2,128)(2,1)S(1)}, bf16[2,2,9216]{2,1,0:T(2,128)(2,1)S(1)}, u32[]{:S(2)}, u32[]{:S(2)}) collective-permute-start(bf16[2,2,9216]{2,1,0:T(2,128)(2,1)S(1)} %pad_maximum_fusion.p0), channel_id=1, source_target_pairs={{0,12},{2,14},{4,0},{6,2},{8,4},{10,6},{12,8},{14,10},{1,13},{3,15... | collective-permute-start | bytes 221192 | tf_op jit(solution)/shard_map/ppermute | solution.py:267
  10.7 1.0 %collective-permute-start.1 = (bf16[2,2,9216]{2,1,0:T(2,128)(2,1)S(1)}, bf16[2,2,9216]{2,1,0:T(2,128)(2,1)S(1)}, u32[]{:S(2)}, u32[]{:S(2)}) collective-permute-start(bf16[2,2,9216]{2,1,0:T(2,128)(2,1)S(1)} %pad_maximum_fusion.p0), channel_id=1, source_target_pairs={{0,4},{2,6},{4,8},{6,10},{8,12},{10,14},{12,0},{14,2},{1,5},{3,7},... | collective-permute-start | bytes 221192 | tf_op jit(solution)/shard_map/ppermute | solution.py:267
  11.7 1.0 %collective-permute-done.3.p3 = bf16[2,2,9216]{2,1,0:T(2,128)(2,1)S(1)} collective-permute-done((bf16[2,2,9216]{2,1,0:T(2,128)(2,1)S(1)}, bf16[2,2,9216]{2,1,0:T(2,128)(2,1)S(1)}, u32[]{:S(2)}, u32[]{:S(2)}) %collective-permute-start.3) | collective-permute-done | bytes 73760 | tf_op jit(solution)/shard_map/ppermute | solution.py:267
  12.7 3.3 %collective-permute-done.2.p2 = bf16[2,2,9216]{2,1,0:T(2,128)(2,1)S(1)} collective-permute-done((bf16[2,2,9216]{2,1,0:T(2,128)(2,1)S(1)}, bf16[2,2,9216]{2,1,0:T(2,128)(2,1)S(1)}, u32[]{:S(2)}, u32[]{:S(2)}) %collective-permute-start.2) | collective-permute-done | bytes 73760 | tf_op jit(solution)/shard_map/ppermute | solution.py:267
  16.0 0.9 %collective-permute-done.1.p1 = bf16[2,2,9216]{2,1,0:T(2,128)(2,1)S(1)} collective-permute-done((bf16[2,2,9216]{2,1,0:T(2,128)(2,1)S(1)}, bf16[2,2,9216]{2,1,0:T(2,128)(2,1)S(1)}, u32[]{:S(2)}, u32[]{:S(2)}) %collective-permute-start.1) | collective-permute-done | bytes 73760 | tf_op jit(solution)/shard_map/ppermute | solution.py:267
  16.9 0.6 %copy-done.13 = bf16[2,2,9216]{2,1,0:T(2,128)(2,1)} copy-done((bf16[2,2,9216]{2,1,0:T(2,128)(2,1)}, bf16[2,2,9216]{2,1,0:T(2,128)(2,1)S(1)}, u32[]{:S(2)}) %copy-start.13) | copy-done | bytes 73752
  17.5 1.8 %assemble.1 = (bf16[16,4096]{1,0:T(8,128)(2,1)}, bf16[16,5120]{1,0:T(8,128)(2,1)}) custom-call(bf16[2,2,9216]{2,1,0:T(2,128)(2,1)} %copy-done.10, bf16[2,2,9216]{2,1,0:T(2,128)(2,1)} %copy-done.13, bf16[2,2,9216]{2,1,0:T(2,128)(2,1)} %copy-done.12, bf16[2,2,9216]{2,1,0:T(2,128)(2,1)} %copy-done.11), custom_call_target="tpu_custom_call" | custom-call | flops 1000000 | bytes 600000 | tf_op jit(solution)/shard_map/assemble/pallas_call | solution.py:119
  19.4 2.0 %pairs.1 = (bf16[80,16]{1,0:T(8,128)(2,1)}, bf16[80,16]{1,0:T(8,128)(2,1)}, bf16[80,16]{1,0:T(8,128)(2,1)}, bf16[80,16]{1,0:T(8,128)(2,1)}, bf16[16,16]{1,0:T(8,128)(2,1)}) custom-call(s32[1]{0:T(128)} %bitcast.3.row_ref, s32[1,12]{1,0:T(1,128)} %bitcast.8, s32[1,12]{1,0:T(1,128)} %bitcast.9), custom_call_target="tpu_custom_call" | custom-call | flops 2000000 | bytes 40000 | tf_op jit(solution)/shard_map/pairs/pallas_call | solution.py:95
  21.4 3.4 %copy-done = bf16[1,512,8192]{2,1,0:T(8,128)(2,1)S(1)} copy-done((bf16[1,512,8192]{2,1,0:T(8,128)(2,1)S(1)}, bf16[1,512,8192]{2,1,0:T(8,128)(2,1)}, u32[]{:S(2)}) %copy-start) | copy-done | bytes 8388632
  24.7 0.9 %copy-done.4 = bf16[16,4096]{1,0:T(8,128)(2,1)S(1)} copy-done((bf16[16,4096]{1,0:T(8,128)(2,1)S(1)}, bf16[16,4096]{1,0:T(8,128)(2,1)}, u32[]{:S(2)}) %copy-start.4) | copy-done | bytes 131096
  25.6 2.0 %rotate_first.1.part_ref = f32[512,16]{1,0:T(8,128)S(1)} custom-call(s32[1]{0:T(128)} %bitcast.2.half_ref, bf16[1,512,8192]{2,1,0:T(8,128)(2,1)S(1)} %copy-done, bf16[16,4096]{1,0:T(8,128)(2,1)S(1)} %copy-done.4), custom_call_target="tpu_custom_call" | custom-call | flops 1073741824 | bytes 4194304 | tf_op jit(solution)/shard_map/rotate_first/pallas_call | solution.py:154
  27.7 1.3 %copy-done.1 = bf16[1,512,8192]{2,1,0:T(8,128)(2,1)S(1)} copy-done((bf16[1,512,8192]{2,1,0:T(8,128)(2,1)S(1)}, bf16[1,512,8192]{2,1,0:T(8,128)(2,1)}, u32[]{:S(2)}) %copy-start.1) | copy-done | bytes 8388632
  29.0 0.7 %copy-done.9 = bf16[16,16]{1,0:T(8,128)(2,1)S(1)} copy-done((bf16[16,16]{1,0:T(8,128)(2,1)S(1)}, bf16[16,16]{1,0:T(8,128)(2,1)}, u32[]{:S(2)}) %copy-start.9) | copy-done | bytes 536
  29.7 3.0 %rotate_second.1 = bf16[8,16,512]{2,1,0:T(8,128)(2,1)} custom-call(s32[1]{0:T(128)S(6)} %sub.3.half_ref, bf16[1,512,8192]{2,1,0:T(8,128)(2,1)S(1)} %copy-done.1, bf16[16,4096]{1,0:T(8,128)(2,1)S(1)} %collective-permute-done.5.x_ref, f32[512,16]{1,0:T(8,128)S(1)} %rotate_first.1.part_ref, bf16[16,16]{1,0:T(8,128)(2,1)S(1)} %copy-done.9), custom_call_target="tpu_custom_call" | custom-call | flops 1073741824 | bytes 4194304 | tf_op jit(solution)/shard_map/rotate_second/pallas_call | solution.py:167
  32.7 4.5 %all-to-all-start = ((bf16[8,16,512]{2,1,0:T(8,128)(2,1)}), bf16[8,16,512]{2,1,0:T(8,128)(2,1)S(1)}, u32[]{:S(2)}, u32[]{:S(2)}) async-start(bf16[8,16,512]{2,1,0:T(8,128)(2,1)} %rotate_second.1), calls=%async_computation | async-start | bytes 262144 | tf_op jit(solution)/shard_map/all_to_all | solution.py:274
  37.3 4.7 %copy-done.2 = bf16[1280,5120]{1,0:T(8,128)(2,1)S(1)} copy-done((bf16[1280,5120]{1,0:T(8,128)(2,1)S(1)}, bf16[1280,5120]{1,0:T(8,128)(2,1)}, u32[]{:S(2)}) %copy-start.2) | copy-done | bytes 13107224
  42.0 5.2 %rotate_grads.1.own_ref = f32[16,1280]{1,0:T(8,128)S(1)} custom-call(bf16[1280,5120]{1,0:T(8,128)(2,1)S(1)} %copy-done.2, bf16[16,5120]{1,0:T(8,128)(2,1)S(1)} %copy-done.3), custom_call_target="tpu_custom_call" | custom-call | flops 3355443200 | bytes 13107200 | tf_op jit(solution)/shard_map/rotate_grads/pallas_call | solution.py:189
  47.2 0.3 collective-permute-start.4
  47.5 1.0 %collective-permute-done.4.other_ref = f32[16,1280]{1,0:T(8,128)S(1)} collective-permute-done((f32[16,1280]{1,0:T(8,128)S(1)}, f32[16,1280]{1,0:T(8,128)S(1)}, u32[]{:S(2)}, u32[]{:S(2)}) %collective-permute-start.4) | collective-permute-done | bytes 81952 | tf_op jit(solution)/shard_map/ppermute | solution.py:276
  48.5 13.2 %correct.1 = f32[1280,4096]{1,0:T(8,128)} custom-call(f32[16,1280]{1,0:T(8,128)S(1)} %rotate_grads.1.own_ref, f32[16,1280]{1,0:T(8,128)S(1)} %collective-permute-done.4.other_ref, bf16[8,16,512]{2,1,0:T(8,128)(2,1)S(1)} %all-to-all-done.a_ref, bf16[80,16]{1,0:T(8,128)(2,1)S(1)} %copy-done.5, bf16[80,16]{1,0:T(8,128)(2,1)S(1)} %copy-done.6, ...), custom_call_target="tpu_custom_call" | custom-call | flops 2684354560 | bytes 20971520 | tf_op jit(solution)/shard_map/correct/pallas_call | solution.py:233
  (27 shorter events, 0.2 us)
Async XLA Ops:
  1.5 4.9 %collective-permute-start = (bf16[2,9216]{1,0:T(2,128)(2,1)S(1)}, bf16[2,9216]{1,0:T(2,128)(2,1)S(1)}, u32[]{:S(2)}, u32[]{:S(2)}) collective-permute-start(bf16[2,9216]{1,0:T(2,128)(2,1)S(1)} %constant_dynamic-update-slice_fusion), channel_id=1, source_target_pairs={{0,2},{2,0},{4,6},{6,4},{8,10},{10,8},{12,14},{14,12},{1,3},{3,1},... | collective-permute-start | bytes 110600 | tf_op jit(solution)/shard_map/ppermute | solution.py:264
  6.5 10.4 %copy-start.10 = (bf16[2,2,9216]{2,1,0:T(2,128)(2,1)}, bf16[2,2,9216]{2,1,0:T(2,128)(2,1)S(1)}, u32[]{:S(2)}) copy-start(bf16[2,2,9216]{2,1,0:T(2,128)(2,1)S(1)} %pad_maximum_fusion.p0) | copy-start | bytes 221188
  6.5 6.2 %collective-permute-start.3 = (bf16[2,2,9216]{2,1,0:T(2,128)(2,1)S(1)}, bf16[2,2,9216]{2,1,0:T(2,128)(2,1)S(1)}, u32[]{:S(2)}, u32[]{:S(2)}) collective-permute-start(bf16[2,2,9216]{2,1,0:T(2,128)(2,1)S(1)} %pad_maximum_fusion.p0), channel_id=1, source_target_pairs={{0,12},{2,14},{4,0},{6,2},{8,4},{10,6},{12,8},{14,10},{1,13},{3,15... | collective-permute-start | bytes 221192 | tf_op jit(solution)/shard_map/ppermute | solution.py:267
  10.7 5.3 %collective-permute-start.2 = (bf16[2,2,9216]{2,1,0:T(2,128)(2,1)S(1)}, bf16[2,2,9216]{2,1,0:T(2,128)(2,1)S(1)}, u32[]{:S(2)}, u32[]{:S(2)}) collective-permute-start(bf16[2,2,9216]{2,1,0:T(2,128)(2,1)S(1)} %pad_maximum_fusion.p0), channel_id=1, source_target_pairs={{0,8},{2,10},{4,12},{6,14},{8,0},{10,2},{12,4},{14,6},{1,9},{3,11}... | collective-permute-start | bytes 221192 | tf_op jit(solution)/shard_map/ppermute | solution.py:267
  10.7 6.2 %collective-permute-start.1 = (bf16[2,2,9216]{2,1,0:T(2,128)(2,1)S(1)}, bf16[2,2,9216]{2,1,0:T(2,128)(2,1)S(1)}, u32[]{:S(2)}, u32[]{:S(2)}) collective-permute-start(bf16[2,2,9216]{2,1,0:T(2,128)(2,1)S(1)} %pad_maximum_fusion.p0), channel_id=1, source_target_pairs={{0,4},{2,6},{4,8},{6,10},{8,12},{10,14},{12,0},{14,2},{1,5},{3,7},... | collective-permute-start | bytes 221192 | tf_op jit(solution)/shard_map/ppermute | solution.py:267
  12.7 4.2 %copy-start.11 = (bf16[2,2,9216]{2,1,0:T(2,128)(2,1)}, bf16[2,2,9216]{2,1,0:T(2,128)(2,1)S(1)}, u32[]{:S(2)}) copy-start(bf16[2,2,9216]{2,1,0:T(2,128)(2,1)S(1)} %collective-permute-done.3.p3) | copy-start | bytes 221188
  16.0 0.9 %copy-start.12 = (bf16[2,2,9216]{2,1,0:T(2,128)(2,1)}, bf16[2,2,9216]{2,1,0:T(2,128)(2,1)S(1)}, u32[]{:S(2)}) copy-start(bf16[2,2,9216]{2,1,0:T(2,128)(2,1)S(1)} %collective-permute-done.2.p2) | copy-start | bytes 221188
  16.9 0.6 %copy-start.13 = (bf16[2,2,9216]{2,1,0:T(2,128)(2,1)}, bf16[2,2,9216]{2,1,0:T(2,128)(2,1)S(1)}, u32[]{:S(2)}) copy-start(bf16[2,2,9216]{2,1,0:T(2,128)(2,1)S(1)} %collective-permute-done.1.p1) | copy-start | bytes 221188
  19.4 8.3 %collective-permute-start.5 = (bf16[16,4096]{1,0:T(8,128)(2,1)}, bf16[16,4096]{1,0:T(8,128)(2,1)S(1)}, u32[]{:S(2)}, u32[]{:S(2)}) collective-permute-start(bf16[16,4096]{1,0:T(8,128)(2,1)} %get-tuple-element.13.x_ref), channel_id=1, source_target_pairs={{0,1},{1,0},{2,3},{3,2},{4,5},{5,4},{6,7},{7,6},{8,9},{9,8},{10,11... | collective-permute-start | bytes 393224 | tf_op jit(solution)/shard_map/ppermute | solution.py:271
  21.4 3.4 %copy-start = (bf16[1,512,8192]{2,1,0:T(8,128)(2,1)S(1)}, bf16[1,512,8192]{2,1,0:T(8,128)(2,1)}, u32[]{:S(2)}) copy-start(bf16[1,512,8192]{2,1,0:T(8,128)(2,1)} %w_ref.5) | copy-start | bytes 25165828
  24.7 0.9 %copy-start.4 = (bf16[16,4096]{1,0:T(8,128)(2,1)S(1)}, bf16[16,4096]{1,0:T(8,128)(2,1)}, u32[]{:S(2)}) copy-start(bf16[16,4096]{1,0:T(8,128)(2,1)} %get-tuple-element.13.x_ref) | copy-start | bytes 393220
  25.6 3.4 %copy-start.1 = (bf16[1,512,8192]{2,1,0:T(8,128)(2,1)S(1)}, bf16[1,512,8192]{2,1,0:T(8,128)(2,1)}, u32[]{:S(2)}) copy-start(bf16[1,512,8192]{2,1,0:T(8,128)(2,1)} %w_ref.5) | copy-start | bytes 25165828
  25.6 11.6 %copy-start.3 = (bf16[16,5120]{1,0:T(8,128)(2,1)S(1)}, bf16[16,5120]{1,0:T(8,128)(2,1)}, u32[]{:S(2)}) copy-start(bf16[16,5120]{1,0:T(8,128)(2,1)} %get-tuple-element.12.x_ref) | copy-start | bytes 491524
  27.6 20.9 %copy-start.5 = (bf16[80,16]{1,0:T(8,128)(2,1)S(1)}, bf16[80,16]{1,0:T(8,128)(2,1)}, u32[]{:S(2)}) copy-start(bf16[80,16]{1,0:T(8,128)(2,1)} %get-tuple-element.15.s1a_ref) | copy-start | bytes 7684
  27.6 20.9 %copy-start.6 = (bf16[80,16]{1,0:T(8,128)(2,1)S(1)}, bf16[80,16]{1,0:T(8,128)(2,1)}, u32[]{:S(2)}) copy-start(bf16[80,16]{1,0:T(8,128)(2,1)} %get-tuple-element.16.s2a_ref) | copy-start | bytes 7684
  27.6 20.9 %copy-start.7 = (bf16[80,16]{1,0:T(8,128)(2,1)S(1)}, bf16[80,16]{1,0:T(8,128)(2,1)}, u32[]{:S(2)}) copy-start(bf16[80,16]{1,0:T(8,128)(2,1)} %get-tuple-element.17.s1g_ref) | copy-start | bytes 7684
  27.7 20.9 %copy-start.8 = (bf16[80,16]{1,0:T(8,128)(2,1)S(1)}, bf16[80,16]{1,0:T(8,128)(2,1)}, u32[]{:S(2)}) copy-start(bf16[80,16]{1,0:T(8,128)(2,1)} %get-tuple-element.18.s2g_ref) | copy-start | bytes 7684
  29.0 0.7 %copy-start.9 = (bf16[16,16]{1,0:T(8,128)(2,1)S(1)}, bf16[16,16]{1,0:T(8,128)(2,1)}, u32[]{:S(2)}) copy-start(bf16[16,16]{1,0:T(8,128)(2,1)} %get-tuple-element.14.perm_ref) | copy-start | bytes 1540
  32.7 15.8 %all-to-all-start = ((bf16[8,16,512]{2,1,0:T(8,128)(2,1)}), bf16[8,16,512]{2,1,0:T(8,128)(2,1)S(1)}, u32[]{:S(2)}, u32[]{:S(2)}) async-start(bf16[8,16,512]{2,1,0:T(8,128)(2,1)} %rotate_second.1), calls=%async_computation | async-start | bytes 262144 | tf_op jit(solution)/shard_map/all_to_all | solution.py:274
  37.3 4.7 %copy-start.2 = (bf16[1280,5120]{1,0:T(8,128)(2,1)S(1)}, bf16[1280,5120]{1,0:T(8,128)(2,1)}, u32[]{:S(2)}) copy-start(bf16[1280,5120]{1,0:T(8,128)(2,1)} %w_ref.3) | copy-start | bytes 39321604
  47.2 1.3 %collective-permute-start.4 = (f32[16,1280]{1,0:T(8,128)S(1)}, f32[16,1280]{1,0:T(8,128)S(1)}, u32[]{:S(2)}, u32[]{:S(2)}) collective-permute-start(f32[16,1280]{1,0:T(8,128)S(1)} %rotate_grads.1.own_ref), channel_id=1, source_target_pairs={{0,1},{1,0},{2,3},{3,2},{4,5},{5,4},{6,7},{7,6},{8,9},{9,8},{10,11... | collective-permute-start | bytes 245768 | tf_op jit(solution)/shard_map/ppermute | solution.py:276

commit v2 on v1

v2 whole, which is shorter than its diff:
```python
import functools
import jax
import jax.numpy as jnp
from jax import lax
from jax.experimental import pallas as pl
from jax.experimental.pallas import tpu as pltpu
from jax.sharding import PartitionSpec as P

N_SEQ = 6
PAIR_ROWS = 80
BF16 = jnp.bfloat16
F32 = jnp.float32
I32 = jnp.int32
NT = (((1,), (1,)), ((), ()))
MIB = 1024 * 1024
HBM = pl.BlockSpec(memory_space=pltpu.HBM)
SMEM = pl.BlockSpec(memory_space=pltpu.SMEM)
VMEM = pl.BlockSpec(memory_space=pltpu.VMEM)


def iota(shape, dim):
    return lax.broadcasted_iota(I32, shape, dim)


def dot(a, b, dims=(((1,), (0,)), ((), ()))):
    return lax.dot_general(a, b, dims, preferred_element_type=F32)


def sequence_index(doc_lengths, doc_plan, total_tokens):
    positions = jnp.arange(total_tokens, dtype=I32)
    doc_ends = jnp.cumsum(doc_lengths)
    doc_index = jnp.sum((positions[:, None] >= doc_ends[None, :]).astype(I32), axis=1)
    doc_onehot = (doc_index[:, None] == jnp.arange(doc_lengths.shape[0], dtype=I32)[None, :]).astype(I32)
    return jnp.sum(doc_onehot * doc_plan[None, :], axis=1)


def general_body(acts, grads, eigen_a, eigen_s_rows, doc_lengths, doc_plan):
    act_rows = lax.all_gather(acts, "row", axis=0, tiled=True)
    act_full = lax.all_gather(act_rows, "col", axis=1, tiled=True)
    a_block = dot(eigen_a[0], act_full, NT).astype(BF16)
    a_rot = lax.all_gather(a_block, "row", axis=0, tiled=True)
    grad_terms = dot(eigen_s_rows, lax.all_gather(grads, "row", axis=0, tiled=True), NT)
    g_rot = lax.psum(grad_terms, "col").astype(BF16)
    total_tokens = g_rot.shape[1]
    seq_index = sequence_index(doc_lengths, doc_plan, total_tokens)
    correction = jnp.zeros((g_rot.shape[0], a_rot.shape[0]), F32)
    for sequence in range(N_SEQ):
        inside = (seq_index == sequence).astype(BF16)
        term = dot(g_rot * inside[None, :], a_rot, NT)
        correction = correction + term * term
    return correction / total_tokens


def pairs_kernel(ids_ref, len_ref, plan_ref, s1a_ref, s2a_ref, s1g_ref, s2g_ref, perm_ref):
    docs = len_ref.shape[1]
    tokens = perm_ref.shape[0]
    grid_pairs = tokens * tokens
    me = ids_ref[0]
    upper = (iota((docs, docs), 0) <= iota((docs, docs), 1)).astype(F32)
    ends = dot(jnp.broadcast_to(len_ref[...].astype(F32), (8, docs)), upper)[0:1]
    position = iota((tokens, docs), 0).astype(F32)
    doc = jnp.sum((ends <= position).astype(F32), axis=1, keepdims=True)
    onehot = doc == iota((tokens, docs), 1).astype(F32)
    seq = jnp.sum(jnp.where(onehot, plan_ref[...].astype(F32), 0.0), axis=1, keepdims=True)
    p_lane = iota((tokens, grid_pairs), 1)
    t_sub = iota((tokens, grid_pairs), 0)
    first = lax.div(p_lane, tokens)
    second = lax.rem(p_lane, tokens)
    seq_first = jnp.sum(jnp.where(first == t_sub, seq, 0.0), axis=0, keepdims=True)
    seq_second = jnp.sum(jnp.where(second == t_sub, seq, 0.0), axis=0, keepdims=True)
    valid = (seq_first == seq_second) & (first[0:1] <= second[0:1])
    before = (iota((grid_pairs, grid_pairs), 0) < iota((grid_pairs, grid_pairs), 1)).astype(BF16)
    rank = dot(jnp.broadcast_to(valid.astype(F32), (8, grid_pairs)).astype(BF16), before)[0:1]
    place = jnp.where(valid, rank, -1.0)
    pick = (iota((PAIR_ROWS, grid_pairs), 0).astype(F32) == place).astype(BF16)
    p_sub = iota((grid_pairs, tokens), 0)
    t_lane = iota((grid_pairs, tokens), 1)
    is_first = lax.div(p_sub, tokens) == t_lane
    is_second = lax.rem(p_sub, tokens) == t_lane
    factor = jnp.where(lax.div(p_sub, tokens) == lax.rem(p_sub, tokens), 1.0, 2.0)
    s1 = dot(pick, jnp.where(is_first, 1.0, 0.0).astype(BF16)).astype(BF16)
    s1_scaled = dot(pick, jnp.where(is_first, factor, 0.0).astype(BF16)).astype(BF16)
    s2 = dot(pick, jnp.where(is_second, 1.0, 0.0).astype(BF16)).astype(BF16)
    token = iota((tokens, tokens), 0)
    slot = iota((tokens, tokens), 1)
    source = ((me + 8 - 2 * (slot >> 2)) & 7) ^ ((slot >> 1) & 1)
    perm = (token == 2 * source + (slot & 1)).astype(BF16)
    s1a_ref[...] = s1
    s2a_ref[...] = s2
    s1g_ref[...] = dot(s1_scaled, perm).astype(BF16)
    s2g_ref[...] = dot(s2, perm).astype(BF16)
    perm_ref[...] = perm


def make_pairs(ids, doc_lengths, doc_plan, tokens):
    sel = jax.ShapeDtypeStruct((PAIR_ROWS, tokens), BF16)
    return pl.pallas_call(
        pairs_kernel,
        out_shape=(sel, sel, sel, sel, jax.ShapeDtypeStruct((tokens, tokens), BF16)),
        in_specs=[SMEM, VMEM, VMEM],
        out_specs=(VMEM,) * 5,
        compiler_params=pltpu.CompilerParams(vmem_limit_bytes=2 * MIB),
        cost_estimate=pl.CostEstimate(flops=2_000_000, bytes_accessed=40_000, transcendentals=0),
        name="pairs",
    )(ids, doc_lengths[None, :], doc_plan[None, :])


def pack_kernel(ids_ref, acts_ref, grads_ref, acts_beside_ref, grads_beside_ref, o_ref):
    width = acts_ref.shape[1]
    o_ref[0, :, :width] = acts_ref[...]
    o_ref[0, :, width:] = grads_ref[...]
    o_ref[1, :, :width] = acts_beside_ref[...]
    o_ref[1, :, width:] = grads_beside_ref[...]


def pack(ids, acts, grads, acts_beside, grads_beside):
    rows, width = acts.shape
    return pl.pallas_call(
        pack_kernel,
        out_shape=jax.ShapeDtypeStruct((2, rows, width + grads.shape[1]), BF16),
        in_specs=[SMEM] + [VMEM] * 4,
        out_specs=VMEM,
        compiler_params=pltpu.CompilerParams(vmem_limit_bytes=2 * MIB),
        cost_estimate=pl.CostEstimate(flops=10_000, bytes_accessed=200_000, transcendentals=0),
        name="pack",
    )(ids, acts, grads, acts_beside, grads_beside)


def assemble_kernel(width, p0, p1, p2, p3, basis_ref, perm_ref, acts_ref, grads_ref):
    rows = []
    for piece in (p0, p1, p2, p3):
        for side in range(2):
            rows.append(piece[side].astype(F32))
    whole = jnp.concatenate(rows, axis=0).astype(BF16)
    acts_ref[...] = whole[:, :width]
    grads_ref[...] = whole[:, width:]


def assemble(pieces, basis, perm, width):
    tokens = sum(p.shape[0] * p.shape[1] for p in pieces)
    total = pieces[0].shape[2]
    return pl.pallas_call(
        functools.partial(assemble_kernel, width),
        out_shape=(
            jax.ShapeDtypeStruct((tokens, width), BF16),
            jax.ShapeDtypeStruct((tokens, total - width), BF16),
        ),
        in_specs=[VMEM] * 6,
        out_specs=(VMEM, VMEM),
        compiler_params=pltpu.CompilerParams(vmem_limit_bytes=4 * MIB),
        cost_estimate=pl.CostEstimate(flops=1_000_000, bytes_accessed=600_000, transcendentals=0),
        name="assemble",
    )(*pieces, basis, perm)


def load_kernel(w_ref, o_ref, sem):
    copy = pltpu.make_async_copy(w_ref, o_ref, sem)
    copy.start()
    copy.wait()


def load(w):
    return pl.pallas_call(
        load_kernel,
        out_shape=jax.ShapeDtypeStruct(w.shape, w.dtype),
        in_specs=[HBM],
        out_specs=VMEM,
        scratch_shapes=[pltpu.SemaphoreType.DMA],
        compiler_params=pltpu.CompilerParams(vmem_limit_bytes=42 * MIB),
        cost_estimate=pl.CostEstimate(flops=0, bytes_accessed=w.size * 2, transcendentals=0),
        name="load",
    )(w)


def half_dot(half, w_ref, x_ref):
    depth = x_ref.shape[1]
    columns = pl.ds(pl.multiple_of(half * depth, depth), depth)
    return dot(w_ref[0, :, columns], x_ref[...], NT)


def rotate_first_kernel(ids_ref, w_ref, x_ref, o_ref):
    o_ref[...] = half_dot(ids_ref[1], w_ref, x_ref)


def rotate_second_kernel(ids_ref, w_ref, x_ref, part_ref, perm_ref, o_ref):
    total = (half_dot(1 - ids_ref[1], w_ref, x_ref) + part_ref[...]).astype(BF16)
    mine = dot(perm_ref[...], total, NT).astype(BF16)
    for row in range(o_ref.shape[0]):
        o_ref[row] = mine


def rotate_acts(eigen_a, ids, x, part=None, perm=None, copies=0):
    _, features, _ = eigen_a.shape
    tokens, depth = x.shape
    cost = pl.CostEstimate(
        flops=2 * features * depth * 256, bytes_accessed=features * depth * 2, transcendentals=0
    )
    params = pltpu.CompilerParams(vmem_limit_bytes=4 * MIB)
    if part is None:
        return pl.pallas_call(
            rotate_first_kernel,
            out_shape=jax.ShapeDtypeStruct((features, tokens), F32),
            in_specs=[SMEM, VMEM, VMEM],
            out_specs=VMEM,
            compiler_params=params,
            cost_estimate=cost,
            name="rotate_first",
        )(ids, eigen_a, x)
    return pl.pallas_call(
        rotate_second_kernel,
        out_shape=jax.ShapeDtypeStruct((copies, tokens, features), BF16),
        in_specs=[SMEM, VMEM, VMEM, VMEM, VMEM],
        out_specs=VMEM,
        compiler_params=params,
        cost_estimate=cost,
        name="rotate_second",
    )(ids, eigen_a, x, part, perm)


def rotate_grads_kernel(w_ref, x_ref, o_ref, held, sems):
    parts = sems.shape[0]
    block = w_ref.shape[0] // parts
    copies = []
    for part in range(parts):
        rows = slice(part * block, (part + 1) * block)
        copies.append(pltpu.make_async_copy(w_ref.at[rows, :], held.at[rows, :], sems.at[part]))
        copies[-1].start()
    for part in range(parts):
        rows = slice(part * block, (part + 1) * block)
        copies[part].wait()
        o_ref[:, rows] = dot(held[rows, :], x_ref[...], NT).T


def rotate_grads(eigen_s, x):
    features, depth = eigen_s.shape
    tokens = x.shape[0]
    parts = features // 256
    return pl.pallas_call(
        rotate_grads_kernel,
        out_shape=jax.ShapeDtypeStruct((tokens, features), F32),
        in_specs=[HBM, VMEM],
        out_specs=VMEM,
        scratch_shapes=[pltpu.VMEM((features, depth), BF16), pltpu.SemaphoreType.DMA((parts,))],
        compiler_params=pltpu.CompilerParams(vmem_limit_bytes=52 * MIB),
        cost_estimate=pl.CostEstimate(
            flops=2 * features * depth * 256, bytes_accessed=features * depth * 2, transcendentals=0
        ),
        name="rotate_grads",
    )(eigen_s, x)


def split(x):
    high = x.astype(BF16)
    low = (x - high.astype(F32)).astype(BF16)
    return high, low


def correct_kernel(own_ref, other_ref, a_ref, s1a_ref, s2a_ref, s1g_ref, s2g_ref, o_ref, buffer, g_pairs, sems):
    tokens = own_ref.shape[0]
    n_block, _, width = a_ref.shape
    g_rot = (own_ref[...] + other_ref[...]).astype(BF16)
    product = dot(s1g_ref[...], g_rot) * dot(s2g_ref[...], g_rot) * (1.0 / tokens)
    high, low = split(product)
    g_pairs[...] = jnp.concatenate([high, high, low], axis=0).T
    copies = []
    for block in range(n_block):
        a_rot = a_ref[block]
        high, low = split(dot(s1a_ref[...], a_rot) * dot(s2a_ref[...], a_rot))
        columns = slice(block * width, (block + 1) * width)
        buffer[:, columns] = dot(g_pairs[...], jnp.concatenate([high, low, high], axis=0))
        copies.append(pltpu.make_async_copy(buffer.at[:, columns], o_ref.at[:, columns], sems.at[block]))
        copies[-1].start()
    for copy in copies:
        copy.wait()


def correct(own, other, a_all, s1a, s2a, s1g, s2g):
    tokens, rows = own.shape
    n_row, _, width = a_all.shape
    return pl.pallas_call(
        correct_kernel,
        out_shape=jax.ShapeDtypeStruct((rows, n_row * width), F32),
        in_specs=[VMEM] * 7,
        out_specs=pl.BlockSpec(memory_space=pl.ANY),
        scratch_shapes=[
            pltpu.VMEM((rows, n_row * width), F32),
            pltpu.VMEM((rows, 3 * PAIR_ROWS), BF16),
            pltpu.SemaphoreType.DMA((n_row,)),
        ],
        compiler_params=pltpu.CompilerParams(vmem_limit_bytes=32 * MIB),
        cost_estimate=pl.CostEstimate(
            flops=2 * rows * n_row * width * 256, bytes_accessed=rows * n_row * width * 4, transcendentals=0
        ),
        name="correct",
    )(own, other, a_all, s1a, s2a, s1g, s2g)


def few_tokens_body(acts, grads, eigen_a, eigen_s_rows, doc_lengths, doc_plan):
    n_row = 8
    tokens = n_row * acts.shape[0]
    ids = jnp.stack([lax.axis_index("row"), lax.axis_index("col")]).astype(I32)
    width = acts.shape[1]

    across = [(i, i ^ 1) for i in range(n_row)]
    acts_beside = lax.ppermute(acts, "row", across)
    grads_beside = lax.ppermute(grads, "row", across)
    both = pack(ids, acts, grads, acts_beside, grads_beside)
    pieces = [both] + [
        lax.ppermute(both, "row", [(i, (i + 2 * k) % n_row) for i in range(n_row)]) for k in range(1, 4)
    ]
    s1a, s2a, s1g, s2g, perm = make_pairs(ids, doc_lengths, doc_plan, tokens)
    basis = load(eigen_a)
    acts_own, grads_own = assemble(pieces, basis, perm, width)
    acts_other = lax.ppermute(acts_own, "col", [(0, 1), (1, 0)])
    part = rotate_acts(basis, ids, acts_own)
    copies = rotate_acts(basis, ids, acts_other, part, perm, n_row)
    a_all = lax.all_to_all(copies, "row", 0, 0)
    g_own = rotate_grads(eigen_s_rows, grads_own)
    g_other = lax.ppermute(g_own, "col", [(0, 1), (1, 0)])
    return correct(g_own, g_other, a_all, s1a, s2a, s1g, s2g)


def solution(mesh):
    def body(acts, *rest):
        n_row = mesh.shape["row"]
        tokens = n_row * acts.shape[0]
        most = tokens - (N_SEQ - 1)
        pairs = most * (most + 1) // 2 + N_SEQ - 1
        few = n_row == 8 and acts.shape[0] == 2 and mesh.shape["col"] == 2 and pairs <= PAIR_ROWS
        return (few_tokens_body if few else general_body)(acts, *rest)

    return jax.shard_map(
        body,
        mesh=mesh,
        in_specs=(
            P(("grp", "row"), "col"),
            P(("grp", "row"), "col"),
            P("col", "row", None),
            P("row", "col"),
            P("grp"),
            P("grp"),
        ),
        out_specs=P(("grp", "row"), "col"),
        check_vma=False,
    )
```

time: 62.2 us -> 45.4 us (0.73)
  local copies, waits for them, and re-layouts: 13.2 us -> 1.45 us
  waiting for transfers between devices: 8.1 us -> 5.36 us
  starting transfers between devices: 13.1 us -> 11.7 us
  Pallas kernels: 27.2 us -> 26.4 us
    unnamed x29 -> x8, local copies, waits for them, and re-layouts: 12.4 us -> 1.45 us
    ppermute x3, waiting for transfers between devices: 5.13 us -> 0.46 us  [few_tokens_body(): lax.ppermute(both, 'row', [(i, (i + 2 * k) % n_row) for i in range(n_row)])]
    pallas_call x1, Pallas kernels: 5.17 us -> 8.66 us  [rotate_grads(): pl.pallas_call(rotate_grads_kernel, out_shape=jax.ShapeDtypeStruct((token...]
    ppermute x1 -> x2, waiting for transfers between devices: 1.94 us -> 3.84 us  [the longest x1 2.07 us: few_tokens_body(): grads_beside = lax.ppermute(grads, 'row', across)]
    pallas_call x1, Pallas kernels: 1.84 us -> 0.18 us  [assemble(): pl.pallas_call(functools.partial(assemble_kernel, width), out_shape=(jax....]
    pallas_call x1 -> x3, Pallas kernels: 13.2 us -> 12 us  [the longest x1 8.03 us: correct(): pl.pallas_call(correct_kernel, out_shape=jax.ShapeDtypeStruct((rows, n_ro...]
    all_to_all x1, starting transfers between devices: 4.54 us -> 3.65 us  [few_tokens_body(): a_all = lax.all_to_all(copies, 'row', 0, 0)]
    concatenate x1 -> x0, local copies, waits for them, and re-layouts: 0.75 us -> none  [few_tokens_body(): payload = jnp.concatenate([acts, grads], axis=1)]
  transfers between devices with their start and end apart: 7 -> 8, of which waited for: 5 -> 4; matrix products, arithmetic and copies ran while one was open for 0% -> 0% of each run, Pallas kernels for 15% -> 33%
where the time goes in v2:
time: 45.4 us; the launch traced here: 45.1 us
  Pallas kernels  26.4 us (58%)
  starting transfers between devices  11.7 us (26%)
  waiting for transfers between devices  5.36 us (12%)
  local copies, waits for them, and re-layouts  1.45 us (3%)
    pallas_call x1, Pallas kernels, rotate_grads(): pl.pallas_call(rotate_grads_kernel, out_shape=jax.ShapeDtypeStruct((token...  8.66 us
    pallas_call x1, Pallas kernels, correct(): pl.pallas_call(correct_kernel, out_shape=jax.ShapeDtypeStruct((rows, n_ro...  8.03 us
    ppermute x3, starting transfers between devices, few_tokens_body(): lax.ppermute(both, 'row', [(i, (i + 2 * k) % n_row) for i in range(n_row)])  4.67 us
    all_to_all x1, starting transfers between devices, few_tokens_body(): a_all = lax.all_to_all(copies, 'row', 0, 0)  3.65 us
    pallas_call x1, Pallas kernels, load(): pl.pallas_call(load_kernel, out_shape=jax.ShapeDtypeStruct(w.shape, w.dty...  3.39 us
    ppermute x1, starting transfers between devices, few_tokens_body(): acts_beside = lax.ppermute(acts, 'row', across)  2.94 us
    pallas_call x1, Pallas kernels, rotate_acts(): pl.pallas_call(rotate_second_kernel, out_shape=jax.ShapeDtypeStruct((copi...  2.57 us
    ppermute x1, waiting for transfers between devices, few_tokens_body(): grads_beside = lax.ppermute(grads, 'row', across)  2.07 us
  transfers between devices with their start and end apart: 8, of which 4 were waited for; matrix products, arithmetic and copies ran while one was open for 0% of the time, Pallas kernels for 33%

profile of v2, /device:TPU:0, one launch (start us, length us, event | category | flops | bytes accessed | tf_op | source)
XLA Modules:
  0.0 45.1 jit_solution(16565364172548563112)
XLA Ops:
  0.0 2.9 %collective-permute-start = (bf16[2,4096]{1,0:T(2,128)(2,1)}, bf16[2,4096]{1,0:T(2,128)(2,1)S(1)}, u32[]{:S(2)}, u32[]{:S(2)}) collective-permute-start(bf16[2,4096]{1,0:T(2,128)(2,1)} %acts_ref.1), channel_id=1, source_target_pairs={{0,2},{2,0},{4,6},{6,4},{8,10},{10,8},{12,14},{14,12},{1,3},{3,1},... | collective-permute-start | bytes 49160 | tf_op jit(solution)/shard_map/ppermute | solution.py:305
  2.9 0.1 collective-permute-start.1
  3.0 0.1 pad_add_fusion.ids_ref
  3.1 1.8 %collective-permute-done.acts_beside_ref = bf16[2,4096]{1,0:T(2,128)(2,1)S(1)} collective-permute-done((bf16[2,4096]{1,0:T(2,128)(2,1)}, bf16[2,4096]{1,0:T(2,128)(2,1)S(1)}, u32[]{:S(2)}, u32[]{:S(2)}) %collective-permute-start) | collective-permute-done | bytes 16416 | tf_op jit(solution)/shard_map/ppermute | solution.py:305
  4.9 2.1 %collective-permute-done.1.grads_beside_ref = bf16[2,5120]{1,0:T(2,128)(2,1)S(1)} collective-permute-done((bf16[2,5120]{1,0:T(2,128)(2,1)}, bf16[2,5120]{1,0:T(2,128)(2,1)S(1)}, u32[]{:S(2)}, u32[]{:S(2)}) %collective-permute-start.1) | collective-permute-done | bytes 20512 | tf_op jit(solution)/shard_map/ppermute | solution.py:306
  6.9 0.7 %copy-done = bf16[2,5120]{1,0:T(2,128)(2,1)S(1)} copy-done((bf16[2,5120]{1,0:T(2,128)(2,1)S(1)}, bf16[2,5120]{1,0:T(2,128)(2,1)}, u32[]{:S(2)}) %copy-start) | copy-done | bytes 20504
  7.7 0.7 %copy-done.1 = bf16[2,4096]{1,0:T(2,128)(2,1)S(1)} copy-done((bf16[2,4096]{1,0:T(2,128)(2,1)S(1)}, bf16[2,4096]{1,0:T(2,128)(2,1)}, u32[]{:S(2)}) %copy-start.1) | copy-done | bytes 16408
  8.4 0.5 %pack.1.p0 = bf16[2,2,9216]{2,1,0:T(2,128)(2,1)S(1)} custom-call(s32[2]{0:T(128)S(1)} %pad_add_fusion.ids_ref, bf16[2,4096]{1,0:T(2,128)(2,1)S(1)} %copy-done.1, bf16[2,5120]{1,0:T(2,128)(2,1)S(1)} %copy-done, bf16[2,4096]{1,0:T(2,128)(2,1)S(1)} %collective-permute-done.acts_beside_ref, bf16[2,5120]{1,0:T(2,128)(2,1)S(1)} %collective-permute-done.1.grads_beside_ref), custom_call_target="tpu_custom_call" | custom-call | flops 10000 | bytes 200000 | tf_op jit(solution)/shard_map/pack/pallas_call | solution.py:118
  8.9 3.7 %collective-permute-start.4 = (bf16[2,2,9216]{2,1,0:T(2,128)(2,1)S(1)}, bf16[2,2,9216]{2,1,0:T(2,128)(2,1)S(1)}, u32[]{:S(2)}, u32[]{:S(2)}) collective-permute-start(bf16[2,2,9216]{2,1,0:T(2,128)(2,1)S(1)} %pack.1.p0), channel_id=1, source_target_pairs={{0,12},{2,14},{4,0},{6,2},{8,4},{10,6},{12,8},{14,10},{1,13},{3,15... | collective-permute-start | bytes 221192 | tf_op jit(solution)/shard_map/ppermute | solution.py:309
  12.6 0.0 collective-permute-start.3
  12.6 1.0 %collective-permute-start.2 = (bf16[2,2,9216]{2,1,0:T(2,128)(2,1)S(1)}, bf16[2,2,9216]{2,1,0:T(2,128)(2,1)S(1)}, u32[]{:S(2)}, u32[]{:S(2)}) collective-permute-start(bf16[2,2,9216]{2,1,0:T(2,128)(2,1)S(1)} %pack.1.p0), channel_id=1, source_target_pairs={{0,4},{2,6},{4,8},{6,10},{8,12},{10,14},{12,0},{14,2},{1,5},{3,7},... | collective-permute-start | bytes 221192 | tf_op jit(solution)/shard_map/ppermute | solution.py:309
  13.6 3.4 %load.1.basis_ref.w_ref = bf16[1,512,8192]{2,1,0:T(8,128)(2,1)S(1)} custom-call(bf16[1,512,8192]{2,1,0:T(8,128)(2,1)} %w_ref.2), custom_call_target="tpu_custom_call" | custom-call | bytes 8388608 | tf_op jit(solution)/shard_map/load/pallas_call | solution.py:163
  17.0 1.2 %pairs.1 = (bf16[80,16]{1,0:T(8,128)(2,1)S(1)}, bf16[80,16]{1,0:T(8,128)(2,1)S(1)}, bf16[80,16]{1,0:T(8,128)(2,1)S(1)}, bf16[80,16]{1,0:T(8,128)(2,1)S(1)}, bf16[16,16]{1,0:T(8,128)(2,1)S(1)}) custom-call(s32[2]{0:T(128)S(1)} %pad_add_fusion.ids_ref, s32[1,12]{1,0:T(1,128)S(1)} %bitcast.4, s32[1,12]{1,0:T(1,128)S(1)} %bitcast.5), custom_call_target="tpu_custom_call" | custom-call | flops 2000000 | bytes 40000 | tf_op jit(solution)/shard_map/pairs/pallas_call | solution.py:97
  18.3 0.0 collective-permute-done.4.p3
  18.3 0.5 %collective-permute-done.2.p1 = bf16[2,2,9216]{2,1,0:T(2,128)(2,1)S(1)} collective-permute-done((bf16[2,2,9216]{2,1,0:T(2,128)(2,1)S(1)}, bf16[2,2,9216]{2,1,0:T(2,128)(2,1)S(1)}, u32[]{:S(2)}, u32[]{:S(2)}) %collective-permute-start.2) | collective-permute-done | bytes 73760 | tf_op jit(solution)/shard_map/ppermute | solution.py:309
  18.7 0.2 assemble.1
  18.9 0.1 collective-permute-start.6
  19.0 1.8 %rotate_first.1.part_ref = f32[512,16]{1,0:T(8,128)S(1)} custom-call(s32[2]{0:T(128)S(1)} %pad_add_fusion.ids_ref, bf16[1,512,8192]{2,1,0:T(8,128)(2,1)S(1)} %load.1.basis_ref.w_ref, bf16[16,4096]{1,0:T(8,128)(2,1)S(1)} %get-tuple-element.14.x_ref), custom_call_target="tpu_custom_call" | custom-call | flops 1073741824 | bytes 4194304 | tf_op jit(solution)/shard_map/rotate_first/pallas_call | solution.py:200
  20.8 2.6 %rotate_second.1 = bf16[8,16,512]{2,1,0:T(8,128)(2,1)} custom-call(s32[2]{0:T(128)S(1)} %pad_add_fusion.ids_ref, bf16[1,512,8192]{2,1,0:T(8,128)(2,1)S(1)} %load.1.basis_ref.w_ref, bf16[16,4096]{1,0:T(8,128)(2,1)S(1)} %collective-permute-done.6.x_ref, f32[512,16]{1,0:T(8,128)S(1)} %rotate_first.1.part_ref, bf16[16,16]{1,0:T(8,128)(2,1)S(1)} %get-tuple-element.12.perm_ref), custom_call_target="tpu_custom_call" | custom-call | flops 1073741824 | bytes 4194304 | tf_op jit(solution)/shard_map/rotate_second/pallas_call | solution.py:209
  23.4 3.7 %all-to-all-start = ((bf16[8,16,512]{2,1,0:T(8,128)(2,1)}), bf16[8,16,512]{2,1,0:T(8,128)(2,1)S(1)}, u32[]{:S(2)}, u32[]{:S(2)}) async-start(bf16[8,16,512]{2,1,0:T(8,128)(2,1)} %rotate_second.1), calls=%async_computation | async-start | bytes 262144 | tf_op jit(solution)/shard_map/all_to_all | solution.py:317
  27.0 8.7 %rotate_grads.1.own_ref = f32[16,1280]{1,0:T(8,128)S(1)} custom-call(bf16[1280,5120]{1,0:T(8,128)(2,1)} %w_ref.3, bf16[16,5120]{1,0:T(8,128)(2,1)S(1)} %get-tuple-element.13.x_ref), custom_call_target="tpu_custom_call" | custom-call | flops 3355443200 | bytes 13107200 | tf_op jit(solution)/shard_map/rotate_grads/pallas_call | solution.py:238
  35.7 0.3 collective-permute-start.5
  36.0 1.1 %collective-permute-done.5.other_ref = f32[16,1280]{1,0:T(8,128)S(1)} collective-permute-done((f32[16,1280]{1,0:T(8,128)S(1)}, f32[16,1280]{1,0:T(8,128)S(1)}, u32[]{:S(2)}, u32[]{:S(2)}) %collective-permute-start.5) | collective-permute-done | bytes 81952 | tf_op jit(solution)/shard_map/ppermute | solution.py:319
  37.0 8.0 %correct.1 = f32[1280,4096]{1,0:T(8,128)} custom-call(f32[16,1280]{1,0:T(8,128)S(1)} %rotate_grads.1.own_ref, f32[16,1280]{1,0:T(8,128)S(1)} %collective-permute-done.5.other_ref, bf16[8,16,512]{2,1,0:T(8,128)(2,1)S(1)} %all-to-all-done.a_ref, bf16[80,16]{1,0:T(8,128)(2,1)S(1)} %get-tuple-element.15.s1a_ref, bf16[80,16]{1,0:T(8,128)(2,1)S(1)} %get-tuple-element.16.s2a_ref, ...), custom_call_target="tpu_custom_call" | custom-call | flops 2684354560 | bytes 20971520 | tf_op jit(solution)/shard_map/correct/pallas_call | solution.py:280
  (9 shorter events, 0.0 us)
Async XLA Ops:
  0.0 17.0 %copy-start.3 = (s32[12]{0:T(128)S(1)}, s32[12]{0:T(128)}, u32[]{:S(2)}) copy-start(s32[12]{0:T(128)} %param.11) | copy-start | bytes 148
  0.0 17.0 %copy-start.2 = (s32[12]{0:T(128)S(1)}, s32[12]{0:T(128)}, u32[]{:S(2)}) copy-start(s32[12]{0:T(128)} %param.10) | copy-start | bytes 148
  0.0 4.9 %collective-permute-start = (bf16[2,4096]{1,0:T(2,128)(2,1)}, bf16[2,4096]{1,0:T(2,128)(2,1)S(1)}, u32[]{:S(2)}, u32[]{:S(2)}) collective-permute-start(bf16[2,4096]{1,0:T(2,128)(2,1)} %acts_ref.1), channel_id=1, source_target_pairs={{0,2},{2,0},{4,6},{6,4},{8,10},{10,8},{12,14},{14,12},{1,3},{3,1},... | collective-permute-start | bytes 49160 | tf_op jit(solution)/shard_map/ppermute | solution.py:305
  2.9 4.0 %collective-permute-start.1 = (bf16[2,5120]{1,0:T(2,128)(2,1)}, bf16[2,5120]{1,0:T(2,128)(2,1)S(1)}, u32[]{:S(2)}, u32[]{:S(2)}) collective-permute-start(bf16[2,5120]{1,0:T(2,128)(2,1)} %grads_ref.1), channel_id=1, source_target_pairs={{0,2},{2,0},{4,6},{6,4},{8,10},{10,8},{12,14},{14,12},{1,3},{3,1},... | collective-permute-start | bytes 61448 | tf_op jit(solution)/shard_map/ppermute | solution.py:306
  6.9 0.7 %copy-start = (bf16[2,5120]{1,0:T(2,128)(2,1)S(1)}, bf16[2,5120]{1,0:T(2,128)(2,1)}, u32[]{:S(2)}) copy-start(bf16[2,5120]{1,0:T(2,128)(2,1)} %grads_ref.1) | copy-start | bytes 61444
  7.7 0.7 %copy-start.1 = (bf16[2,4096]{1,0:T(2,128)(2,1)S(1)}, bf16[2,4096]{1,0:T(2,128)(2,1)}, u32[]{:S(2)}) copy-start(bf16[2,4096]{1,0:T(2,128)(2,1)} %acts_ref.1) | copy-start | bytes 49156
  8.9 9.3 %collective-permute-start.4 = (bf16[2,2,9216]{2,1,0:T(2,128)(2,1)S(1)}, bf16[2,2,9216]{2,1,0:T(2,128)(2,1)S(1)}, u32[]{:S(2)}, u32[]{:S(2)}) collective-permute-start(bf16[2,2,9216]{2,1,0:T(2,128)(2,1)S(1)} %pack.1.p0), channel_id=1, source_target_pairs={{0,12},{2,14},{4,0},{6,2},{8,4},{10,6},{12,8},{14,10},{1,13},{3,15... | collective-permute-start | bytes 221192 | tf_op jit(solution)/shard_map/ppermute | solution.py:309
  12.6 5.7 %collective-permute-start.3 = (bf16[2,2,9216]{2,1,0:T(2,128)(2,1)S(1)}, bf16[2,2,9216]{2,1,0:T(2,128)(2,1)S(1)}, u32[]{:S(2)}, u32[]{:S(2)}) collective-permute-start(bf16[2,2,9216]{2,1,0:T(2,128)(2,1)S(1)} %pack.1.p0), channel_id=1, source_target_pairs={{0,8},{2,10},{4,12},{6,14},{8,0},{10,2},{12,4},{14,6},{1,9},{3,11}... | collective-permute-start | bytes 221192 | tf_op jit(solution)/shard_map/ppermute | solution.py:309
  12.6 6.2 %collective-permute-start.2 = (bf16[2,2,9216]{2,1,0:T(2,128)(2,1)S(1)}, bf16[2,2,9216]{2,1,0:T(2,128)(2,1)S(1)}, u32[]{:S(2)}, u32[]{:S(2)}) collective-permute-start(bf16[2,2,9216]{2,1,0:T(2,128)(2,1)S(1)} %pack.1.p0), channel_id=1, source_target_pairs={{0,4},{2,6},{4,8},{6,10},{8,12},{10,14},{12,0},{14,2},{1,5},{3,7},... | collective-permute-start | bytes 221192 | tf_op jit(solution)/shard_map/ppermute | solution.py:309
  18.9 1.9 %collective-permute-start.6 = (bf16[16,4096]{1,0:T(8,128)(2,1)S(1)}, bf16[16,4096]{1,0:T(8,128)(2,1)S(1)}, u32[]{:S(2)}, u32[]{:S(2)}) collective-permute-start(bf16[16,4096]{1,0:T(8,128)(2,1)S(1)} %get-tuple-element.14.x_ref), channel_id=1, source_target_pairs={{0,1},{1,0},{2,3},{3,2},{4,5},{5,4},{6,7},{7,6},{8,9},{9,8},{10,11... | collective-permute-start | bytes 393224 | tf_op jit(solution)/shard_map/ppermute | solution.py:314
  23.4 13.7 %all-to-all-start = ((bf16[8,16,512]{2,1,0:T(8,128)(2,1)}), bf16[8,16,512]{2,1,0:T(8,128)(2,1)S(1)}, u32[]{:S(2)}, u32[]{:S(2)}) async-start(bf16[8,16,512]{2,1,0:T(8,128)(2,1)} %rotate_second.1), calls=%async_computation | async-start | bytes 262144 | tf_op jit(solution)/shard_map/all_to_all | solution.py:317
  35.7 1.3 %collective-permute-start.5 = (f32[16,1280]{1,0:T(8,128)S(1)}, f32[16,1280]{1,0:T(8,128)S(1)}, u32[]{:S(2)}, u32[]{:S(2)}) collective-permute-start(f32[16,1280]{1,0:T(8,128)S(1)} %rotate_grads.1.own_ref), channel_id=1, source_target_pairs={{0,1},{1,0},{2,3},{3,2},{4,5},{5,4},{6,7},{7,6},{8,9},{9,8},{10,11... | collective-permute-start | bytes 245768 | tf_op jit(solution)/shard_map/ppermute | solution.py:319

commit v3 on v2

--- a/solution.py
+++ b/solution.py
@@ -14,7 +14,6 @@
 NT = (((1,), (1,)), ((), ()))
 MIB = 1024 * 1024
 HBM = pl.BlockSpec(memory_space=pltpu.HBM)
-SMEM = pl.BlockSpec(memory_space=pltpu.SMEM)
 VMEM = pl.BlockSpec(memory_space=pltpu.VMEM)
 
 
@@ -51,11 +50,11 @@
     return correction / total_tokens
 
 
-def pairs_kernel(ids_ref, len_ref, plan_ref, s1a_ref, s2a_ref, s1g_ref, s2g_ref, perm_ref):
+def pairs_kernel(len_ref, plan_ref, s1a_ref, s2a_ref, s1g_ref, s2g_ref, perm_ref):
     docs = len_ref.shape[1]
     tokens = perm_ref.shape[0]
     grid_pairs = tokens * tokens
-    me = ids_ref[0]
+    me = lax.axis_index("row")
     upper = (iota((docs, docs), 0) <= iota((docs, docs), 1)).astype(F32)
     ends = dot(jnp.broadcast_to(len_ref[...].astype(F32), (8, docs)), upper)[0:1]
     position = iota((tokens, docs), 0).astype(F32)
@@ -92,38 +91,75 @@
     perm_ref[...] = perm
 
 
-def make_pairs(ids, doc_lengths, doc_plan, tokens):
+def make_pairs(doc_lengths, doc_plan, tokens):
     sel = jax.ShapeDtypeStruct((PAIR_ROWS, tokens), BF16)
     return pl.pallas_call(
         pairs_kernel,
         out_shape=(sel, sel, sel, sel, jax.ShapeDtypeStruct((tokens, tokens), BF16)),
-        in_specs=[SMEM, VMEM, VMEM],
+        in_specs=[VMEM, VMEM],
         out_specs=(VMEM,) * 5,
         compiler_params=pltpu.CompilerParams(vmem_limit_bytes=2 * MIB),
         cost_estimate=pl.CostEstimate(flops=2_000_000, bytes_accessed=40_000, transcendentals=0),
         name="pairs",
-    )(ids, doc_lengths[None, :], doc_plan[None, :])
-
-
-def pack_kernel(ids_ref, acts_ref, grads_ref, acts_beside_ref, grads_beside_ref, o_ref):
+    )(doc_lengths[None, :], doc_plan[None, :])
+
+
+def pack_kernel(acts_ref, grads_ref, o_ref, sems):
     width = acts_ref.shape[1]
-    o_ref[0, :, :width] = acts_ref[...]
-    o_ref[0, :, width:] = grads_ref[...]
-    o_ref[1, :, :width] = acts_beside_ref[...]
-    o_ref[1, :, width:] = grads_beside_ref[...]
-
-
-def pack(ids, acts, grads, acts_beside, grads_beside):
+    copies = (
+        pltpu.make_async_copy(acts_ref, o_ref.at[:, :width], sems.at[0]),
+        pltpu.make_async_copy(grads_ref, o_ref.at[:, width:], sems.at[1]),
+    )
+    for copy in copies:
+        copy.start()
+    for copy in copies:
+        copy.wait()
+
+
+def pack(acts, grads):
     rows, width = acts.shape
     return pl.pallas_call(
         pack_kernel,
-        out_shape=jax.ShapeDtypeStruct((2, rows, width + grads.shape[1]), BF16),
-        in_specs=[SMEM] + [VMEM] * 4,
+        out_shape=jax.ShapeDtypeStruct((rows, width + grads.shape[1]), BF16),
+        in_specs=[HBM, HBM],
+        out_specs=VMEM,
+        scratch_shapes=[pltpu.SemaphoreType.DMA((2,))],
+        cost_estimate=pl.CostEstimate(flops=0, bytes_accessed=80_000, transcendentals=0),
+        name="pack",
+    )(acts, grads)
+
+
+def stage_kernel(own_ref, o_ref):
+    o_ref[...] = own_ref[...]
+
+
+def stage(own):
+    return pl.pallas_call(
+        stage_kernel,
+        out_shape=jax.ShapeDtypeStruct(own.shape, BF16),
+        in_specs=[VMEM],
         out_specs=VMEM,
         compiler_params=pltpu.CompilerParams(vmem_limit_bytes=2 * MIB),
-        cost_estimate=pl.CostEstimate(flops=10_000, bytes_accessed=200_000, transcendentals=0),
-        name="pack",
-    )(ids, acts, grads, acts_beside, grads_beside)
+        cost_estimate=pl.CostEstimate(flops=10_000, bytes_accessed=2_000_000, transcendentals=0),
+        name="stage",
+    )(own)
+
+
+def merge_kernel(own_ref, beside_ref, o_ref):
+    o_ref[0] = own_ref[...]
+    o_ref[1] = beside_ref[...]
+
+
+def merge(own, beside):
+    return pl.pallas_call(
+        merge_kernel,
+        out_shape=jax.ShapeDtypeStruct((2,) + own.shape, BF16),
+        in_specs=[VMEM] * 2,
+        out_specs=VMEM,
+        compiler_params=pltpu.CompilerParams(vmem_limit_bytes=2 * MIB),
+        cost_estimate=pl.CostEstimate(flops=10_000, bytes_accessed=150_000, transcendentals=0),
+        name="merge",
+    )(own, beside)
 
 
 def assemble_kernel(width, p0, p1, p2, p3, basis_ref, perm_ref, acts_ref, grads_ref):
@@ -178,18 +214,18 @@
     return dot(w_ref[0, :, columns], x_ref[...], NT)
 
 
-def rotate_first_kernel(ids_ref, w_ref, x_ref, o_ref):
-    o_ref[...] = half_dot(ids_ref[1], w_ref, x_ref)
-
-
-def rotate_second_kernel(ids_ref, w_ref, x_ref, part_ref, perm_ref, o_ref):
-    total = (half_dot(1 - ids_ref[1], w_ref, x_ref) + part_ref[...]).astype(BF16)
+def rotate_first_kernel(w_ref, x_ref, o_ref):
+    o_ref[...] = half_dot(lax.axis_index("col"), w_ref, x_ref)
+
+
+def rotate_second_kernel(w_ref, x_ref, part_ref, perm_ref, o_ref):
+    total = (half_dot(1 - lax.axis_index("col"), w_ref, x_ref) + part_ref[...]).astype(BF16)
     mine = dot(perm_ref[...], total, NT).astype(BF16)
     for row in range(o_ref.shape[0]):
         o_ref[row] = mine
 
 
-def rotate_acts(eigen_a, ids, x, part=None, perm=None, copies=0):
+def rotate_acts(eigen_a, x, part=None, perm=None, copies=0):
     _, features, _ = eigen_a.shape
     tokens, depth = x.shape
     cost = pl.CostEstimate(
@@ -200,43 +236,45 @@
         return pl.pallas_call(
             rotate_first_kernel,
             out_shape=jax.ShapeDtypeStruct((features, tokens), F32),
-            in_specs=[SMEM, VMEM, VMEM],
+            in_specs=[VMEM, VMEM],
             out_specs=VMEM,
             compiler_params=params,
             cost_estimate=cost,
             name="rotate_first",
-        )(ids, eigen_a, x)
+        )(eigen_a, x)
     return pl.pallas_call(
         rotate_second_kernel,
         out_shape=jax.ShapeDtypeStruct((copies, tokens, features), BF16),
-        in_specs=[SMEM, VMEM, VMEM, VMEM, VMEM],
+        in_specs=[VMEM] * 4,
         out_specs=VMEM,
         compiler_params=params,
         cost_estimate=cost,
         name="rotate_second",
-    )(ids, eigen_a, x, part, perm)
-
-
-def rotate_grads_kernel(w_ref, x_ref, o_ref, held, sems):
+    )(eigen_a, x, part, perm)
+
+
+def rotate_grads_kernel(ahead, w_ref, x_ref, o_ref, held, sems):
     parts = sems.shape[0]
     block = w_ref.shape[0] // parts
-    copies = []
-    for part in range(parts):
-        rows = slice(part * block, (part + 1) * block)
-        copies.append(pltpu.make_async_copy(w_ref.at[rows, :], held.at[rows, :], sems.at[part]))
-        copies[-1].start()
-    for part in range(parts):
-        rows = slice(part * block, (part + 1) * block)
+    spans = [slice(part * block, (part + 1) * block) for part in range(parts)]
+    copies = [
+        pltpu.make_async_copy(w_ref.at[rows, :], held.at[rows, :], sems.at[part]) for part, rows in enumerate(spans)
+    ]
+    for part in range(ahead):
+        copies[part].start()
+    for part, rows in enumerate(spans):
         copies[part].wait()
+        if part + ahead < parts:
+            copies[part + ahead].start()
         o_ref[:, rows] = dot(held[rows, :], x_ref[...], NT).T
 
 
 def rotate_grads(eigen_s, x):
     features, depth = eigen_s.shape
     tokens = x.shape[0]
-    parts = features // 256
-    return pl.pallas_call(
-        rotate_grads_kernel,
+    parts = features // 128
+    return pl.pallas_call(
+        functools.partial(rotate_grads_kernel, 3),
         out_shape=jax.ShapeDtypeStruct((tokens, features), F32),
         in_specs=[HBM, VMEM],
         out_specs=VMEM,
@@ -298,22 +336,20 @@
 def few_tokens_body(acts, grads, eigen_a, eigen_s_rows, doc_lengths, doc_plan):
     n_row = 8
     tokens = n_row * acts.shape[0]
-    ids = jnp.stack([lax.axis_index("row"), lax.axis_index("col")]).astype(I32)
     width = acts.shape[1]
 
-    across = [(i, i ^ 1) for i in range(n_row)]
-    acts_beside = lax.ppermute(acts, "row", across)
-    grads_beside = lax.ppermute(grads, "row", across)
-    both = pack(ids, acts, grads, acts_beside, grads_beside)
+    own = pack(acts, grads)
+    beside = lax.ppermute(own, "row", [(i, i ^ 1) for i in range(n_row)])
+    both = merge(stage(own), beside)
     pieces = [both] + [
         lax.ppermute(both, "row", [(i, (i + 2 * k) % n_row) for i in range(n_row)]) for k in range(1, 4)
     ]
-    s1a, s2a, s1g, s2g, perm = make_pairs(ids, doc_lengths, doc_plan, tokens)
     basis = load(eigen_a)
+    s1a, s2a, s1g, s2g, perm = make_pairs(doc_lengths, doc_plan, tokens)
     acts_own, grads_own = assemble(pieces, basis, perm, width)
     acts_other = lax.ppermute(acts_own, "col", [(0, 1), (1, 0)])
-    part = rotate_acts(basis, ids, acts_own)
-    copies = rotate_acts(basis, ids, acts_other, part, perm, n_row)
+    part = rotate_acts(basis, acts_own)
+    copies = rotate_acts(basis, acts_other, part, perm, n_row)
     a_all = lax.all_to_all(copies, "row", 0, 0)
     g_own = rotate_grads(eigen_s_rows, grads_own)
     g_other = lax.ppermute(g_own, "col", [(0, 1), (1, 0)])

time: 45.4 us -> 44 us (0.969)
  waiting for transfers between devices: 5.36 us -> 3.58 us
  starting transfers between devices: 11.7 us -> 12.5 us
  local copies, waits for them, and re-layouts: 1.45 us -> 0.81 us
    ppermute x2 -> x1, waiting for transfers between devices: 3.84 us -> 1.34 us  [few_tokens_body(): beside = lax.ppermute(own, 'row', [(i, i ^ 1) for i in range(n_row)])]
    pallas_call x2 -> x4, Pallas kernels: 9.2 us -> 11.1 us  [the longest x1 9.73 us: rotate_grads(): pl.pallas_call(functools.partial(rotate_grads_kernel, 3), out_shape=jax.S...]
    unnamed x8 -> x6, local copies, waits for them, and re-layouts: 1.45 us -> 0.81 us
    ppermute x3, waiting for transfers between devices: 0.46 us -> 1.01 us  [few_tokens_body(): lax.ppermute(both, 'row', [(i, (i + 2 * k) % n_row) for i in range(n_row)])]
    pallas_call x1, Pallas kernels: 2.57 us -> 2.03 us  [rotate_acts(): pl.pallas_call(rotate_second_kernel, out_shape=jax.ShapeDtypeStruct((copi...]
    pallas_call x1, Pallas kernels: 1.24 us -> 0.7 us  [make_pairs(): pl.pallas_call(pairs_kernel, out_shape=(sel, sel, sel, sel, jax.ShapeDtyp...]
    pallas_call x1, Pallas kernels: 1.76 us -> 1.23 us  [rotate_acts(): pl.pallas_call(rotate_first_kernel, out_shape=jax.ShapeDtypeStruct((featu...]
    ppermute x3, starting transfers between devices: 4.67 us -> 5.14 us  [few_tokens_body(): lax.ppermute(both, 'row', [(i, (i + 2 * k) % n_row) for i in range(n_row)])]
  transfers between devices with their start and end apart: 8 -> 7, of which waited for: 4 -> 5; matrix products, arithmetic and copies ran while one was open for 0% -> 0% of each run, Pallas kernels for 33% -> 35%
where the time goes in v3:
time: 44 us; the launch traced here: 43.6 us
  Pallas kernels  26.7 us (61%)
  starting transfers between devices  12.5 us (28%)
  waiting for transfers between devices  3.58 us (8%)
  local copies, waits for them, and re-layouts  0.81 us (2%)
    pallas_call x1, Pallas kernels, rotate_grads(): pl.pallas_call(functools.partial(rotate_grads_kernel, 3), out_shape=jax.S...  9.73 us
    pallas_call x1, Pallas kernels, correct(): pl.pallas_call(correct_kernel, out_shape=jax.ShapeDtypeStruct((rows, n_ro...  8.02 us
    ppermute x3, starting transfers between devices, few_tokens_body(): lax.ppermute(both, 'row', [(i, (i + 2 * k) % n_row) for i in range(n_row)])  5.14 us
    all_to_all x1, starting transfers between devices, few_tokens_body(): a_all = lax.all_to_all(copies, 'row', 0, 0)  4.04 us
    pallas_call x1, Pallas kernels, load(): pl.pallas_call(load_kernel, out_shape=jax.ShapeDtypeStruct(w.shape, w.dty...  3.39 us
    ppermute x1, starting transfers between devices, few_tokens_body(): beside = lax.ppermute(own, 'row', [(i, i ^ 1) for i in range(n_row)])  3 us
    pallas_call x1, Pallas kernels, rotate_acts(): pl.pallas_call(rotate_second_kernel, out_shape=jax.ShapeDtypeStruct((copi...  2.03 us
    pallas_call x1, Pallas kernels, pack(): pl.pallas_call(pack_kernel, out_shape=jax.ShapeDtypeStruct((rows, width +...  1.4 us
  transfers between devices with their start and end apart: 7, of which 5 were waited for; matrix products, arithmetic and copies ran while one was open for 0% of the time, Pallas kernels for 35%

profile of v3, /device:TPU:0, one launch (start us, length us, event | category | flops | bytes accessed | tf_op | source)
XLA Modules:
  0.0 43.6 jit_solution(6992472054280479102)
XLA Ops:
  0.0 1.4 %pack.1.own_ref = bf16[2,9216]{1,0:T(2,128)(2,1)} custom-call(bf16[2,4096]{1,0:T(2,128)(2,1)} %acts_ref.1, bf16[2,5120]{1,0:T(2,128)(2,1)} %grads_ref.1), custom_call_target="tpu_custom_call" | custom-call | bytes 80000 | tf_op jit(solution)/shard_map/pack/pallas_call | solution.py:121
  1.4 3.0 %collective-permute-start = (bf16[2,9216]{1,0:T(2,128)(2,1)}, bf16[2,9216]{1,0:T(2,128)(2,1)S(1)}, u32[]{:S(2)}, u32[]{:S(2)}) collective-permute-start(bf16[2,9216]{1,0:T(2,128)(2,1)} %pack.1.own_ref), channel_id=1, source_target_pairs={{0,2},{2,0},{4,6},{6,4},{8,10},{10,8},{12,14},{14,12},{1,3},{3,1},... | collective-permute-start | bytes 110600 | tf_op jit(solution)/shard_map/ppermute | solution.py:342
  4.4 0.8 %copy-done = bf16[2,9216]{1,0:T(2,128)(2,1)S(1)} copy-done((bf16[2,9216]{1,0:T(2,128)(2,1)S(1)}, bf16[2,9216]{1,0:T(2,128)(2,1)}, u32[]{:S(2)}) %copy-start) | copy-done | bytes 36888
  5.2 1.3 %collective-permute-done.beside_ref = bf16[2,9216]{1,0:T(2,128)(2,1)S(1)} collective-permute-done((bf16[2,9216]{1,0:T(2,128)(2,1)}, bf16[2,9216]{1,0:T(2,128)(2,1)S(1)}, u32[]{:S(2)}, u32[]{:S(2)}) %collective-permute-start) | collective-permute-done | bytes 36896 | tf_op jit(solution)/shard_map/ppermute | solution.py:342
  6.6 4.1 %collective-permute-start.3 = (bf16[2,2,9216]{2,1,0:T(2,128)(2,1)S(1)}, bf16[2,2,9216]{2,1,0:T(2,128)(2,1)S(1)}, u32[]{:S(2)}, u32[]{:S(2)}) collective-permute-start(bf16[2,2,9216]{2,1,0:T(2,128)(2,1)S(1)} %merge.1.p0), channel_id=1, source_target_pairs={{0,12},{2,14},{4,0},{6,2},{8,4},{10,6},{12,8},{14,10},{1,13},{3,15... | collective-permute-start | bytes 221192 | tf_op jit(solution)/shard_map/ppermute | solution.py:345
  10.7 0.0 collective-permute-start.2
  10.7 1.0 %collective-permute-start.1 = (bf16[2,2,9216]{2,1,0:T(2,128)(2,1)S(1)}, bf16[2,2,9216]{2,1,0:T(2,128)(2,1)S(1)}, u32[]{:S(2)}, u32[]{:S(2)}) collective-permute-start(bf16[2,2,9216]{2,1,0:T(2,128)(2,1)S(1)} %merge.1.p0), channel_id=1, source_target_pairs={{0,4},{2,6},{4,8},{6,10},{8,12},{10,14},{12,0},{14,2},{1,5},{3,7},... | collective-permute-start | bytes 221192 | tf_op jit(solution)/shard_map/ppermute | solution.py:345
  11.7 3.4 %load.1.basis_ref.w_ref = bf16[1,512,8192]{2,1,0:T(8,128)(2,1)S(1)} custom-call(bf16[1,512,8192]{2,1,0:T(8,128)(2,1)} %w_ref.2), custom_call_target="tpu_custom_call" | custom-call | bytes 8388608 | tf_op jit(solution)/shard_map/load/pallas_call | solution.py:199
  15.1 0.0 copy-done.2
  15.1 0.7 %pairs.1 = (bf16[80,16]{1,0:T(8,128)(2,1)S(1)}, bf16[80,16]{1,0:T(8,128)(2,1)S(1)}, bf16[80,16]{1,0:T(8,128)(2,1)S(1)}, bf16[80,16]{1,0:T(8,128)(2,1)S(1)}, bf16[16,16]{1,0:T(8,128)(2,1)S(1)}) custom-call(s32[1,12]{1,0:T(1,128)S(1)} %bitcast.2, s32[1,12]{1,0:T(1,128)S(1)} %bitcast.3), custom_call_target="tpu_custom_call" | custom-call | flops 2000000 | bytes 40000 | tf_op jit(solution)/shard_map/pairs/pallas_call | solution.py:96
  15.8 0.0 collective-permute-done.3.p3
  15.9 0.1 collective-permute-done.2.p2
  16.0 0.9 %collective-permute-done.1.p1 = bf16[2,2,9216]{2,1,0:T(2,128)(2,1)S(1)} collective-permute-done((bf16[2,2,9216]{2,1,0:T(2,128)(2,1)S(1)}, bf16[2,2,9216]{2,1,0:T(2,128)(2,1)S(1)}, u32[]{:S(2)}, u32[]{:S(2)}) %collective-permute-start.1) | collective-permute-done | bytes 73760 | tf_op jit(solution)/shard_map/ppermute | solution.py:345
  16.9 0.2 assemble.1
  17.0 0.1 collective-permute-start.5
  17.1 1.2 %rotate_first.1.part_ref = f32[512,16]{1,0:T(8,128)S(1)} custom-call(bf16[1,512,8192]{2,1,0:T(8,128)(2,1)S(1)} %load.1.basis_ref.w_ref, bf16[16,4096]{1,0:T(8,128)(2,1)S(1)} %get-tuple-element.14.x_ref), custom_call_target="tpu_custom_call" | custom-call | flops 1073741824 | bytes 4194304 | tf_op jit(solution)/shard_map/rotate_first/pallas_call | solution.py:236
  18.4 0.1 collective-permute-done.5.x_ref
  18.5 2.0 %rotate_second.1 = bf16[8,16,512]{2,1,0:T(8,128)(2,1)} custom-call(bf16[1,512,8192]{2,1,0:T(8,128)(2,1)S(1)} %load.1.basis_ref.w_ref, bf16[16,4096]{1,0:T(8,128)(2,1)S(1)} %collective-permute-done.5.x_ref, f32[512,16]{1,0:T(8,128)S(1)} %rotate_first.1.part_ref, bf16[16,16]{1,0:T(8,128)(2,1)S(1)} %get-tuple-element.12.perm_ref), custom_call_target="tpu_custom_call" | custom-call | flops 1073741824 | bytes 4194304 | tf_op jit(solution)/shard_map/rotate_second/pallas_call | solution.py:245
  20.5 4.0 %all-to-all-start = ((bf16[8,16,512]{2,1,0:T(8,128)(2,1)}), bf16[8,16,512]{2,1,0:T(8,128)(2,1)S(1)}, u32[]{:S(2)}, u32[]{:S(2)}) async-start(bf16[8,16,512]{2,1,0:T(8,128)(2,1)} %rotate_second.1), calls=%async_computation | async-start | bytes 262144 | tf_op jit(solution)/shard_map/all_to_all | solution.py:353
  24.5 9.7 %rotate_grads.1.own_ref = f32[16,1280]{1,0:T(8,128)S(1)} custom-call(bf16[1280,5120]{1,0:T(8,128)(2,1)} %w_ref.3, bf16[16,5120]{1,0:T(8,128)(2,1)S(1)} %get-tuple-element.13.x_ref), custom_call_target="tpu_custom_call" | custom-call | flops 3355443200 | bytes 13107200 | tf_op jit(solution)/shard_map/rotate_grads/pallas_call | solution.py:276
  34.3 0.2 collective-permute-start.4
  34.5 1.1 %collective-permute-done.4.other_ref = f32[16,1280]{1,0:T(8,128)S(1)} collective-permute-done((f32[16,1280]{1,0:T(8,128)S(1)}, f32[16,1280]{1,0:T(8,128)S(1)}, u32[]{:S(2)}, u32[]{:S(2)}) %collective-permute-start.4) | collective-permute-done | bytes 81952 | tf_op jit(solution)/shard_map/ppermute | solution.py:355
  35.6 0.0 all-to-all-done.a_ref
  35.6 8.0 %correct.1 = f32[1280,4096]{1,0:T(8,128)} custom-call(f32[16,1280]{1,0:T(8,128)S(1)} %rotate_grads.1.own_ref, f32[16,1280]{1,0:T(8,128)S(1)} %collective-permute-done.4.other_ref, bf16[8,16,512]{2,1,0:T(8,128)(2,1)S(1)} %all-to-all-done.a_ref, bf16[80,16]{1,0:T(8,128)(2,1)S(1)} %get-tuple-element.15.s1a_ref, bf16[80,16]{1,0:T(8,128)(2,1)S(1)} %get-tuple-element.16.s2a_ref, ...), custom_call_target="tpu_custom_call" | custom-call | flops 2684354560 | bytes 20971520 | tf_op jit(solution)/shard_map/correct/pallas_call | solution.py:318
  (6 shorter events, 0.0 us)
Async XLA Ops:
  0.0 15.1 %copy-start.2 = (s32[12]{0:T(128)S(1)}, s32[12]{0:T(128)}, u32[]{:S(2)}) copy-start(s32[12]{0:T(128)} %param.11) | copy-start | bytes 148
  0.0 15.1 %copy-start.1 = (s32[12]{0:T(128)S(1)}, s32[12]{0:T(128)}, u32[]{:S(2)}) copy-start(s32[12]{0:T(128)} %param.10) | copy-start | bytes 148
  1.4 5.2 %collective-permute-start = (bf16[2,9216]{1,0:T(2,128)(2,1)}, bf16[2,9216]{1,0:T(2,128)(2,1)S(1)}, u32[]{:S(2)}, u32[]{:S(2)}) collective-permute-start(bf16[2,9216]{1,0:T(2,128)(2,1)} %pack.1.own_ref), channel_id=1, source_target_pairs={{0,2},{2,0},{4,6},{6,4},{8,10},{10,8},{12,14},{14,12},{1,3},{3,1},... | collective-permute-start | bytes 110600 | tf_op jit(solution)/shard_map/ppermute | solution.py:342
  4.4 0.8 %copy-start = (bf16[2,9216]{1,0:T(2,128)(2,1)S(1)}, bf16[2,9216]{1,0:T(2,128)(2,1)}, u32[]{:S(2)}) copy-start(bf16[2,9216]{1,0:T(2,128)(2,1)} %pack.1.own_ref) | copy-start | bytes 110596
  6.6 9.3 %collective-permute-start.3 = (bf16[2,2,9216]{2,1,0:T(2,128)(2,1)S(1)}, bf16[2,2,9216]{2,1,0:T(2,128)(2,1)S(1)}, u32[]{:S(2)}, u32[]{:S(2)}) collective-permute-start(bf16[2,2,9216]{2,1,0:T(2,128)(2,1)S(1)} %merge.1.p0), channel_id=1, source_target_pairs={{0,12},{2,14},{4,0},{6,2},{8,4},{10,6},{12,8},{14,10},{1,13},{3,15... | collective-permute-start | bytes 221192 | tf_op jit(solution)/shard_map/ppermute | solution.py:345
  10.7 5.3 %collective-permute-start.2 = (bf16[2,2,9216]{2,1,0:T(2,128)(2,1)S(1)}, bf16[2,2,9216]{2,1,0:T(2,128)(2,1)S(1)}, u32[]{:S(2)}, u32[]{:S(2)}) collective-permute-start(bf16[2,2,9216]{2,1,0:T(2,128)(2,1)S(1)} %merge.1.p0), channel_id=1, source_target_pairs={{0,8},{2,10},{4,12},{6,14},{8,0},{10,2},{12,4},{14,6},{1,9},{3,11}... | collective-permute-start | bytes 221192 | tf_op jit(solution)/shard_map/ppermute | solution.py:345
  10.7 6.2 %collective-permute-start.1 = (bf16[2,2,9216]{2,1,0:T(2,128)(2,1)S(1)}, bf16[2,2,9216]{2,1,0:T(2,128)(2,1)S(1)}, u32[]{:S(2)}, u32[]{:S(2)}) collective-permute-start(bf16[2,2,9216]{2,1,0:T(2,128)(2,1)S(1)} %merge.1.p0), channel_id=1, source_target_pairs={{0,4},{2,6},{4,8},{6,10},{8,12},{10,14},{12,0},{14,2},{1,5},{3,7},... | collective-permute-start | bytes 221192 | tf_op jit(solution)/shard_map/ppermute | solution.py:345
  17.0 1.4 %collective-permute-start.5 = (bf16[16,4096]{1,0:T(8,128)(2,1)S(1)}, bf16[16,4096]{1,0:T(8,128)(2,1)S(1)}, u32[]{:S(2)}, u32[]{:S(2)}) collective-permute-start(bf16[16,4096]{1,0:T(8,128)(2,1)S(1)} %get-tuple-element.14.x_ref), channel_id=1, source_target_pairs={{0,1},{1,0},{2,3},{3,2},{4,5},{5,4},{6,7},{7,6},{8,9},{9,8},{10,11... | collective-permute-start | bytes 393224 | tf_op jit(solution)/shard_map/ppermute | solution.py:350
  20.5 15.1 %all-to-all-start = ((bf16[8,16,512]{2,1,0:T(8,128)(2,1)}), bf16[8,16,512]{2,1,0:T(8,128)(2,1)S(1)}, u32[]{:S(2)}, u32[]{:S(2)}) async-start(bf16[8,16,512]{2,1,0:T(8,128)(2,1)} %rotate_second.1), calls=%async_computation | async-start | bytes 262144 | tf_op jit(solution)/shard_map/all_to_all | solution.py:353
  34.3 1.3 %collective-permute-start.4 = (f32[16,1280]{1,0:T(8,128)S(1)}, f32[16,1280]{1,0:T(8,128)S(1)}, u32[]{:S(2)}, u32[]{:S(2)}) collective-permute-start(f32[16,1280]{1,0:T(8,128)S(1)} %rotate_grads.1.own_ref), channel_id=1, source_target_pairs={{0,1},{1,0},{2,3},{3,2},{4,5},{5,4},{6,7},{7,6},{8,9},{9,8},{10,11... | collective-permute-start | bytes 245768 | tf_op jit(solution)/shard_map/ppermute | solution.py:355

commit v4 on v3

--- a/solution.py
+++ b/solution.py
@@ -122,7 +122,7 @@
         pack_kernel,
         out_shape=jax.ShapeDtypeStruct((rows, width + grads.shape[1]), BF16),
         in_specs=[HBM, HBM],
-        out_specs=VMEM,
+        out_specs=HBM,
         scratch_shapes=[pltpu.SemaphoreType.DMA((2,))],
         cost_estimate=pl.CostEstimate(flops=0, bytes_accessed=80_000, transcendentals=0),
         name="pack",
@@ -208,10 +208,14 @@
     )(w)
 
 
+def row_dots(w_ref, x, first, last, columns=slice(None), rows=128):
+    return jnp.concatenate([dot(w_ref[i : i + rows, columns], x, NT) for i in range(first, last, rows)], axis=0)
+
+
 def half_dot(half, w_ref, x_ref):
     depth = x_ref.shape[1]
     columns = pl.ds(pl.multiple_of(half * depth, depth), depth)
-    return dot(w_ref[0, :, columns], x_ref[...], NT)
+    return row_dots(w_ref.at[0], x_ref[...], 0, w_ref.shape[1], columns)
 
 
 def rotate_first_kernel(w_ref, x_ref, o_ref):
@@ -253,28 +257,26 @@
     )(eigen_a, x, part, perm)
 
 
-def rotate_grads_kernel(ahead, w_ref, x_ref, o_ref, held, sems):
+def rotate_grads_kernel(w_ref, x_ref, o_ref, held, sems):
     parts = sems.shape[0]
     block = w_ref.shape[0] // parts
     spans = [slice(part * block, (part + 1) * block) for part in range(parts)]
     copies = [
         pltpu.make_async_copy(w_ref.at[rows, :], held.at[rows, :], sems.at[part]) for part, rows in enumerate(spans)
     ]
-    for part in range(ahead):
-        copies[part].start()
-    for part, rows in enumerate(spans):
-        copies[part].wait()
-        if part + ahead < parts:
-            copies[part + ahead].start()
-        o_ref[:, rows] = dot(held[rows, :], x_ref[...], NT).T
+    for copy in copies:
+        copy.start()
+    for copy, rows in zip(copies, spans):
+        copy.wait()
+        o_ref[:, rows] = row_dots(held, x_ref[...], rows.start, rows.stop).T
 
 
 def rotate_grads(eigen_s, x):
     features, depth = eigen_s.shape
     tokens = x.shape[0]
-    parts = features // 128
-    return pl.pallas_call(
-        functools.partial(rotate_grads_kernel, 3),
+    parts = features // 256
+    return pl.pallas_call(
+        rotate_grads_kernel,
         out_shape=jax.ShapeDtypeStruct((tokens, features), F32),
         in_specs=[HBM, VMEM],
         out_specs=VMEM,

time: 44 us -> 41.3 us (0.939)
  Pallas kernels: 26.7 us -> 24 us
    pallas_call x1, Pallas kernels: 9.73 us -> 6.22 us  [rotate_grads(): pl.pallas_call(rotate_grads_kernel, out_shape=jax.ShapeDtypeStruct((token...]
    pallas_call x1, Pallas kernels: 1.4 us -> 2.23 us  [pack(): pl.pallas_call(pack_kernel, out_shape=jax.ShapeDtypeStruct((rows, width +...]
  transfers between devices with their start and end apart: 7 -> 7, of which waited for: 5 -> 5; matrix products, arithmetic and copies ran while one was open for 0% -> 0% of each run, Pallas kernels for 35% -> 28%
where the time goes in v4:
time: 41.3 us; the launch traced here: 41 us
  Pallas kernels  24 us (58%)
  starting transfers between devices  12.4 us (30%)
  waiting for transfers between devices  3.72 us (9%)
  local copies, waits for them, and re-layouts  0.81 us (2%)
    pallas_call x1, Pallas kernels, correct(): pl.pallas_call(correct_kernel, out_shape=jax.ShapeDtypeStruct((rows, n_ro...  8.03 us
    pallas_call x1, Pallas kernels, rotate_grads(): pl.pallas_call(rotate_grads_kernel, out_shape=jax.ShapeDtypeStruct((token...  6.22 us
    ppermute x3, starting transfers between devices, few_tokens_body(): lax.ppermute(both, 'row', [(i, (i + 2 * k) % n_row) for i in range(n_row)])  5.14 us
    all_to_all x1, starting transfers between devices, few_tokens_body(): a_all = lax.all_to_all(copies, 'row', 0, 0)  4.08 us
    pallas_call x1, Pallas kernels, load(): pl.pallas_call(load_kernel, out_shape=jax.ShapeDtypeStruct(w.shape, w.dty...  3.39 us
    ppermute x1, starting transfers between devices, few_tokens_body(): beside = lax.ppermute(own, 'row', [(i, i ^ 1) for i in range(n_row)])  3 us
    pallas_call x1, Pallas kernels, pack(): pl.pallas_call(pack_kernel, out_shape=jax.ShapeDtypeStruct((rows, width +...  2.23 us
    pallas_call x1, Pallas kernels, rotate_acts(): pl.pallas_call(rotate_second_kernel, out_shape=jax.ShapeDtypeStruct((copi...  2 us
  transfers between devices with their start and end apart: 7, of which 5 were waited for; matrix products, arithmetic and copies ran while one was open for 0% of the time, Pallas kernels for 28%

profile of v4, /device:TPU:0, one launch (start us, length us, event | category | flops | bytes accessed | tf_op | source)
XLA Modules:
  0.0 41.0 jit_solution(15991607032275931634)
XLA Ops:
  0.0 2.2 %pack.1.own_ref = bf16[2,9216]{1,0:T(2,128)(2,1)} custom-call(bf16[2,4096]{1,0:T(2,128)(2,1)} %acts_ref.1, bf16[2,5120]{1,0:T(2,128)(2,1)} %grads_ref.1), custom_call_target="tpu_custom_call" | custom-call | bytes 80000 | tf_op jit(solution)/shard_map/pack/pallas_call | solution.py:121
  2.2 3.0 %collective-permute-start = (bf16[2,9216]{1,0:T(2,128)(2,1)}, bf16[2,9216]{1,0:T(2,128)(2,1)S(1)}, u32[]{:S(2)}, u32[]{:S(2)}) collective-permute-start(bf16[2,9216]{1,0:T(2,128)(2,1)} %pack.1.own_ref), channel_id=1, source_target_pairs={{0,2},{2,0},{4,6},{6,4},{8,10},{10,8},{12,14},{14,12},{1,3},{3,1},... | collective-permute-start | bytes 110600 | tf_op jit(solution)/shard_map/ppermute | solution.py:344
  5.3 0.8 %copy-done = bf16[2,9216]{1,0:T(2,128)(2,1)S(1)} copy-done((bf16[2,9216]{1,0:T(2,128)(2,1)S(1)}, bf16[2,9216]{1,0:T(2,128)(2,1)}, u32[]{:S(2)}) %copy-start) | copy-done | bytes 36888
  6.1 1.3 %collective-permute-done.beside_ref = bf16[2,9216]{1,0:T(2,128)(2,1)S(1)} collective-permute-done((bf16[2,9216]{1,0:T(2,128)(2,1)}, bf16[2,9216]{1,0:T(2,128)(2,1)S(1)}, u32[]{:S(2)}, u32[]{:S(2)}) %collective-permute-start) | collective-permute-done | bytes 36896 | tf_op jit(solution)/shard_map/ppermute | solution.py:344
  7.4 4.1 %collective-permute-start.3 = (bf16[2,2,9216]{2,1,0:T(2,128)(2,1)S(1)}, bf16[2,2,9216]{2,1,0:T(2,128)(2,1)S(1)}, u32[]{:S(2)}, u32[]{:S(2)}) collective-permute-start(bf16[2,2,9216]{2,1,0:T(2,128)(2,1)S(1)} %merge.1.p0), channel_id=1, source_target_pairs={{0,12},{2,14},{4,0},{6,2},{8,4},{10,6},{12,8},{14,10},{1,13},{3,15... | collective-permute-start | bytes 221192 | tf_op jit(solution)/shard_map/ppermute | solution.py:347
  11.5 0.0 collective-permute-start.2
  11.5 1.0 %collective-permute-start.1 = (bf16[2,2,9216]{2,1,0:T(2,128)(2,1)S(1)}, bf16[2,2,9216]{2,1,0:T(2,128)(2,1)S(1)}, u32[]{:S(2)}, u32[]{:S(2)}) collective-permute-start(bf16[2,2,9216]{2,1,0:T(2,128)(2,1)S(1)} %merge.1.p0), channel_id=1, source_target_pairs={{0,4},{2,6},{4,8},{6,10},{8,12},{10,14},{12,0},{14,2},{1,5},{3,7},... | collective-permute-start | bytes 221192 | tf_op jit(solution)/shard_map/ppermute | solution.py:347
  12.6 3.4 %load.1.basis_ref.w_ref = bf16[1,512,8192]{2,1,0:T(8,128)(2,1)S(1)} custom-call(bf16[1,512,8192]{2,1,0:T(8,128)(2,1)} %w_ref.2), custom_call_target="tpu_custom_call" | custom-call | bytes 8388608 | tf_op jit(solution)/shard_map/load/pallas_call | solution.py:199
  15.9 0.0 copy-done.2
  16.0 0.7 %pairs.1 = (bf16[80,16]{1,0:T(8,128)(2,1)S(1)}, bf16[80,16]{1,0:T(8,128)(2,1)S(1)}, bf16[80,16]{1,0:T(8,128)(2,1)S(1)}, bf16[80,16]{1,0:T(8,128)(2,1)S(1)}, bf16[16,16]{1,0:T(8,128)(2,1)S(1)}) custom-call(s32[1,12]{1,0:T(1,128)S(1)} %bitcast.2, s32[1,12]{1,0:T(1,128)S(1)} %bitcast.3), custom_call_target="tpu_custom_call" | custom-call | flops 2000000 | bytes 40000 | tf_op jit(solution)/shard_map/pairs/pallas_call | solution.py:96
  16.7 0.0 collective-permute-done.3.p3
  16.7 0.1 collective-permute-done.2.p2
  16.8 0.9 %collective-permute-done.1.p1 = bf16[2,2,9216]{2,1,0:T(2,128)(2,1)S(1)} collective-permute-done((bf16[2,2,9216]{2,1,0:T(2,128)(2,1)S(1)}, bf16[2,2,9216]{2,1,0:T(2,128)(2,1)S(1)}, u32[]{:S(2)}, u32[]{:S(2)}) %collective-permute-start.1) | collective-permute-done | bytes 73760 | tf_op jit(solution)/shard_map/ppermute | solution.py:347
  17.7 0.2 assemble.1
  17.9 0.1 collective-permute-start.5
  18.0 1.2 %rotate_first.1.part_ref = f32[512,16]{1,0:T(8,128)S(1)} custom-call(bf16[1,512,8192]{2,1,0:T(8,128)(2,1)S(1)} %load.1.basis_ref.w_ref, bf16[16,4096]{1,0:T(8,128)(2,1)S(1)} %get-tuple-element.14.x_ref), custom_call_target="tpu_custom_call" | custom-call | flops 1073741824 | bytes 4194304 | tf_op jit(solution)/shard_map/rotate_first/pallas_call | solution.py:240
  19.2 0.1 collective-permute-done.5.x_ref
  19.3 2.0 %rotate_second.1 = bf16[8,16,512]{2,1,0:T(8,128)(2,1)} custom-call(bf16[1,512,8192]{2,1,0:T(8,128)(2,1)S(1)} %load.1.basis_ref.w_ref, bf16[16,4096]{1,0:T(8,128)(2,1)S(1)} %collective-permute-done.5.x_ref, f32[512,16]{1,0:T(8,128)S(1)} %rotate_first.1.part_ref, bf16[16,16]{1,0:T(8,128)(2,1)S(1)} %get-tuple-element.12.perm_ref), custom_call_target="tpu_custom_call" | custom-call | flops 1073741824 | bytes 4194304 | tf_op jit(solution)/shard_map/rotate_second/pallas_call | solution.py:249
  21.3 4.1 %all-to-all-start = ((bf16[8,16,512]{2,1,0:T(8,128)(2,1)}), bf16[8,16,512]{2,1,0:T(8,128)(2,1)S(1)}, u32[]{:S(2)}, u32[]{:S(2)}) async-start(bf16[8,16,512]{2,1,0:T(8,128)(2,1)} %rotate_second.1), calls=%async_computation | async-start | bytes 262144 | tf_op jit(solution)/shard_map/all_to_all | solution.py:355
  25.4 6.2 %rotate_grads.1.own_ref = f32[16,1280]{1,0:T(8,128)S(1)} custom-call(bf16[1280,5120]{1,0:T(8,128)(2,1)} %w_ref.3, bf16[16,5120]{1,0:T(8,128)(2,1)S(1)} %get-tuple-element.13.x_ref), custom_call_target="tpu_custom_call" | custom-call | flops 3355443200 | bytes 13107200 | tf_op jit(solution)/shard_map/rotate_grads/pallas_call | solution.py:278
  31.6 0.1 collective-permute-start.4
  31.7 1.3 %collective-permute-done.4.other_ref = f32[16,1280]{1,0:T(8,128)S(1)} collective-permute-done((f32[16,1280]{1,0:T(8,128)S(1)}, f32[16,1280]{1,0:T(8,128)S(1)}, u32[]{:S(2)}, u32[]{:S(2)}) %collective-permute-start.4) | collective-permute-done | bytes 81952 | tf_op jit(solution)/shard_map/ppermute | solution.py:357
  32.9 0.0 all-to-all-done.a_ref
  32.9 8.0 %correct.1 = f32[1280,4096]{1,0:T(8,128)} custom-call(f32[16,1280]{1,0:T(8,128)S(1)} %rotate_grads.1.own_ref, f32[16,1280]{1,0:T(8,128)S(1)} %collective-permute-done.4.other_ref, bf16[8,16,512]{2,1,0:T(8,128)(2,1)S(1)} %all-to-all-done.a_ref, bf16[80,16]{1,0:T(8,128)(2,1)S(1)} %get-tuple-element.15.s1a_ref, bf16[80,16]{1,0:T(8,128)(2,1)S(1)} %get-tuple-element.16.s2a_ref, ...), custom_call_target="tpu_custom_call" | custom-call | flops 2684354560 | bytes 20971520 | tf_op jit(solution)/shard_map/correct/pallas_call | solution.py:320
  (6 shorter events, 0.0 us)
Async XLA Ops:
  0.0 15.9 %copy-start.2 = (s32[12]{0:T(128)S(1)}, s32[12]{0:T(128)}, u32[]{:S(2)}) copy-start(s32[12]{0:T(128)} %param.11) | copy-start | bytes 148
  0.0 16.0 %copy-start.1 = (s32[12]{0:T(128)S(1)}, s32[12]{0:T(128)}, u32[]{:S(2)}) copy-start(s32[12]{0:T(128)} %param.10) | copy-start | bytes 148
  2.2 5.2 %collective-permute-start = (bf16[2,9216]{1,0:T(2,128)(2,1)}, bf16[2,9216]{1,0:T(2,128)(2,1)S(1)}, u32[]{:S(2)}, u32[]{:S(2)}) collective-permute-start(bf16[2,9216]{1,0:T(2,128)(2,1)} %pack.1.own_ref), channel_id=1, source_target_pairs={{0,2},{2,0},{4,6},{6,4},{8,10},{10,8},{12,14},{14,12},{1,3},{3,1},... | collective-permute-start | bytes 110600 | tf_op jit(solution)/shard_map/ppermute | solution.py:344
  5.2 0.8 %copy-start = (bf16[2,9216]{1,0:T(2,128)(2,1)S(1)}, bf16[2,9216]{1,0:T(2,128)(2,1)}, u32[]{:S(2)}) copy-start(bf16[2,9216]{1,0:T(2,128)(2,1)} %pack.1.own_ref) | copy-start | bytes 110596
  7.4 9.3 %collective-permute-start.3 = (bf16[2,2,9216]{2,1,0:T(2,128)(2,1)S(1)}, bf16[2,2,9216]{2,1,0:T(2,128)(2,1)S(1)}, u32[]{:S(2)}, u32[]{:S(2)}) collective-permute-start(bf16[2,2,9216]{2,1,0:T(2,128)(2,1)S(1)} %merge.1.p0), channel_id=1, source_target_pairs={{0,12},{2,14},{4,0},{6,2},{8,4},{10,6},{12,8},{14,10},{1,13},{3,15... | collective-permute-start | bytes 221192 | tf_op jit(solution)/shard_map/ppermute | solution.py:347
  11.5 5.3 %collective-permute-start.2 = (bf16[2,2,9216]{2,1,0:T(2,128)(2,1)S(1)}, bf16[2,2,9216]{2,1,0:T(2,128)(2,1)S(1)}, u32[]{:S(2)}, u32[]{:S(2)}) collective-permute-start(bf16[2,2,9216]{2,1,0:T(2,128)(2,1)S(1)} %merge.1.p0), channel_id=1, source_target_pairs={{0,8},{2,10},{4,12},{6,14},{8,0},{10,2},{12,4},{14,6},{1,9},{3,11}... | collective-permute-start | bytes 221192 | tf_op jit(solution)/shard_map/ppermute | solution.py:347
  11.5 6.2 %collective-permute-start.1 = (bf16[2,2,9216]{2,1,0:T(2,128)(2,1)S(1)}, bf16[2,2,9216]{2,1,0:T(2,128)(2,1)S(1)}, u32[]{:S(2)}, u32[]{:S(2)}) collective-permute-start(bf16[2,2,9216]{2,1,0:T(2,128)(2,1)S(1)} %merge.1.p0), channel_id=1, source_target_pairs={{0,4},{2,6},{4,8},{6,10},{8,12},{10,14},{12,0},{14,2},{1,5},{3,7},... | collective-permute-start | bytes 221192 | tf_op jit(solution)/shard_map/ppermute | solution.py:347
  17.9 1.4 %collective-permute-start.5 = (bf16[16,4096]{1,0:T(8,128)(2,1)S(1)}, bf16[16,4096]{1,0:T(8,128)(2,1)S(1)}, u32[]{:S(2)}, u32[]{:S(2)}) collective-permute-start(bf16[16,4096]{1,0:T(8,128)(2,1)S(1)} %get-tuple-element.14.x_ref), channel_id=1, source_target_pairs={{0,1},{1,0},{2,3},{3,2},{4,5},{5,4},{6,7},{7,6},{8,9},{9,8},{10,11... | collective-permute-start | bytes 393224 | tf_op jit(solution)/shard_map/ppermute | solution.py:352
  21.3 11.6 %all-to-all-start = ((bf16[8,16,512]{2,1,0:T(8,128)(2,1)}), bf16[8,16,512]{2,1,0:T(8,128)(2,1)S(1)}, u32[]{:S(2)}, u32[]{:S(2)}) async-start(bf16[8,16,512]{2,1,0:T(8,128)(2,1)} %rotate_second.1), calls=%async_computation | async-start | bytes 262144 | tf_op jit(solution)/shard_map/all_to_all | solution.py:355
  31.6 1.3 %collective-permute-start.4 = (f32[16,1280]{1,0:T(8,128)S(1)}, f32[16,1280]{1,0:T(8,128)S(1)}, u32[]{:S(2)}, u32[]{:S(2)}) collective-permute-start(f32[16,1280]{1,0:T(8,128)S(1)} %rotate_grads.1.own_ref), channel_id=1, source_target_pairs={{0,1},{1,0},{2,3},{3,2},{4,5},{5,4},{6,7},{7,6},{8,9},{9,8},{10,11... | collective-permute-start | bytes 245768 | tf_op jit(solution)/shard_map/ppermute | solution.py:357

commit v5 on v4

--- a/solution.py
+++ b/solution.py
@@ -8,6 +8,7 @@
 
 N_SEQ = 6
 PAIR_ROWS = 80
+HEADS = (128, 128)
 BF16 = jnp.bfloat16
 F32 = jnp.float32
 I32 = jnp.int32
@@ -122,7 +123,7 @@
         pack_kernel,
         out_shape=jax.ShapeDtypeStruct((rows, width + grads.shape[1]), BF16),
         in_specs=[HBM, HBM],
-        out_specs=HBM,
+        out_specs=VMEM,
         scratch_shapes=[pltpu.SemaphoreType.DMA((2,))],
         cost_estimate=pl.CostEstimate(flops=0, bytes_accessed=80_000, transcendentals=0),
         name="pack",
@@ -218,75 +219,99 @@
     return row_dots(w_ref.at[0], x_ref[...], 0, w_ref.shape[1], columns)
 
 
-def rotate_first_kernel(w_ref, x_ref, o_ref):
+def fetch(s_ref, head_ref, first, sem):
+    return pltpu.make_async_copy(s_ref.at[first : first + head_ref.shape[0], :], head_ref, sem)
+
+
+def rotate_first_kernel(w_ref, x_ref, s_ref, o_ref, head_ref, sem):
+    copy = fetch(s_ref, head_ref, 0, sem)
+    copy.start()
     o_ref[...] = half_dot(lax.axis_index("col"), w_ref, x_ref)
-
-
-def rotate_second_kernel(w_ref, x_ref, part_ref, perm_ref, o_ref):
+    copy.wait()
+
+
+def rotate_second_kernel(w_ref, x_ref, part_ref, perm_ref, s_ref, o_ref, head_ref, sem):
+    copy = fetch(s_ref, head_ref, HEADS[0], sem)
+    copy.start()
     total = (half_dot(1 - lax.axis_index("col"), w_ref, x_ref) + part_ref[...]).astype(BF16)
     mine = dot(perm_ref[...], total, NT).astype(BF16)
     for row in range(o_ref.shape[0]):
         o_ref[row] = mine
-
-
-def rotate_acts(eigen_a, x, part=None, perm=None, copies=0):
+    copy.wait()
+
+
+def rotate_acts(eigen_a, x, eigen_s, part=None, perm=None, copies=0):
     _, features, _ = eigen_a.shape
     tokens, depth = x.shape
     cost = pl.CostEstimate(
         flops=2 * features * depth * 256, bytes_accessed=features * depth * 2, transcendentals=0
     )
-    params = pltpu.CompilerParams(vmem_limit_bytes=4 * MIB)
+    params = pltpu.CompilerParams(vmem_limit_bytes=34 * MIB)
+    scratch = [pltpu.SemaphoreType.DMA]
     if part is None:
         return pl.pallas_call(
             rotate_first_kernel,
-            out_shape=jax.ShapeDtypeStruct((features, tokens), F32),
-            in_specs=[VMEM, VMEM],
-            out_specs=VMEM,
+            out_shape=(
+                jax.ShapeDtypeStruct((features, tokens), F32),
+                jax.ShapeDtypeStruct((HEADS[0], eigen_s.shape[1]), BF16),
+            ),
+            in_specs=[VMEM, VMEM, HBM],
+            out_specs=(VMEM, VMEM),
+            scratch_shapes=scratch,
             compiler_params=params,
             cost_estimate=cost,
             name="rotate_first",
-        )(eigen_a, x)
+        )(eigen_a, x, eigen_s)
     return pl.pallas_call(
         rotate_second_kernel,
-        out_shape=jax.ShapeDtypeStruct((copies, tokens, features), BF16),
-        in_specs=[VMEM] * 4,
-        out_specs=VMEM,
+        out_shape=(
+            jax.ShapeDtypeStruct((copies, tokens, features), BF16),
+            jax.ShapeDtypeStruct((HEADS[1], eigen_s.shape[1]), BF16),
+        ),
+        in_specs=[VMEM] * 4 + [HBM],
+        out_specs=(VMEM, VMEM),
+        scratch_shapes=scratch,
         compiler_params=params,
         cost_estimate=cost,
         name="rotate_second",
-    )(eigen_a, x, part, perm)
-
-
-def rotate_grads_kernel(w_ref, x_ref, o_ref, held, sems):
+    )(eigen_a, x, part, perm, eigen_s)
+
+
+def rotate_grads_kernel(head0_ref, head1_ref, w_ref, x_ref, o_ref, held, sems):
+    first = sum(HEADS)
     parts = sems.shape[0]
-    block = w_ref.shape[0] // parts
+    block = held.shape[0] // parts
     spans = [slice(part * block, (part + 1) * block) for part in range(parts)]
     copies = [
-        pltpu.make_async_copy(w_ref.at[rows, :], held.at[rows, :], sems.at[part]) for part, rows in enumerate(spans)
+        pltpu.make_async_copy(w_ref.at[first + rows.start : first + rows.stop, :], held.at[rows, :], sems.at[part])
+        for part, rows in enumerate(spans)
     ]
     for copy in copies:
         copy.start()
+    o_ref[:, : HEADS[0]] = row_dots(head0_ref, x_ref[...], 0, HEADS[0]).T
+    o_ref[:, HEADS[0] : first] = row_dots(head1_ref, x_ref[...], 0, HEADS[1]).T
     for copy, rows in zip(copies, spans):
         copy.wait()
-        o_ref[:, rows] = row_dots(held, x_ref[...], rows.start, rows.stop).T
-
-
-def rotate_grads(eigen_s, x):
+        o_ref[:, first + rows.start : first + rows.stop] = row_dots(held, x_ref[...], rows.start, rows.stop).T
+
+
+def rotate_grads(heads, eigen_s, x):
     features, depth = eigen_s.shape
     tokens = x.shape[0]
-    parts = features // 256
+    rest = features - sum(HEADS)
+    parts = rest // 256
     return pl.pallas_call(
         rotate_grads_kernel,
         out_shape=jax.ShapeDtypeStruct((tokens, features), F32),
-        in_specs=[HBM, VMEM],
+        in_specs=[VMEM, VMEM, HBM, VMEM],
         out_specs=VMEM,
-        scratch_shapes=[pltpu.VMEM((features, depth), BF16), pltpu.SemaphoreType.DMA((parts,))],
-        compiler_params=pltpu.CompilerParams(vmem_limit_bytes=52 * MIB),
+        scratch_shapes=[pltpu.VMEM((rest, depth), BF16), pltpu.SemaphoreType.DMA((parts,))],
+        compiler_params=pltpu.CompilerParams(vmem_limit_bytes=44 * MIB),
         cost_estimate=pl.CostEstimate(
             flops=2 * features * depth * 256, bytes_accessed=features * depth * 2, transcendentals=0
         ),
         name="rotate_grads",
-    )(eigen_s, x)
+    )(*heads, eigen_s, x)
 
 
 def split(x):
@@ -350,10 +375,10 @@
     s1a, s2a, s1g, s2g, perm = make_pairs(doc_lengths, doc_plan, tokens)
     acts_own, grads_own = assemble(pieces, basis, perm, width)
     acts_other = lax.ppermute(acts_own, "col", [(0, 1), (1, 0)])
-    part = rotate_acts(basis, acts_own)
-    copies = rotate_acts(basis, acts_other, part, perm, n_row)
+    part, head0 = rotate_acts(basis, acts_own, eigen_s_rows)
+    copies, head1 = rotate_acts(basis, acts_other, eigen_s_rows, part, perm, n_row)
     a_all = lax.all_to_all(copies, "row", 0, 0)
-    g_own = rotate_grads(eigen_s_rows, grads_own)
+    g_own = rotate_grads((head0, head1), eigen_s_rows, grads_own)
     g_other = lax.ppermute(g_own, "col", [(0, 1), (1, 0)])
     return correct(g_own, g_other, a_all, s1a, s2a, s1g, s2g)
 
@@ -364,7 +389,8 @@
         tokens = n_row * acts.shape[0]
         most = tokens - (N_SEQ - 1)
         pairs = most * (most + 1) // 2 + N_SEQ - 1
-        few = n_row == 8 and acts.shape[0] == 2 and mesh.shape["col"] == 2 and pairs <= PAIR_ROWS
+        rows = rest[2].shape[0]
+        few = rows % 256 == 0 and rows > sum(HEADS) and n_row == 8 and acts.shape[0] == 2 and mesh.shape["col"] == 2 and pairs <= PAIR_ROWS
         return (few_tokens_body if few else general_body)(acts, *rest)
 
     return jax.shard_map(

time: 41.3 us -> 40.7 us (0.985)
  Pallas kernels: 24 us -> 22.8 us
    pallas_call x1, Pallas kernels: 2.23 us -> 1.38 us  [pack(): pl.pallas_call(pack_kernel, out_shape=jax.ShapeDtypeStruct((rows, width +...]
    all_to_all x1, waiting for transfers between devices: 0.01 us -> 0.44 us  [few_tokens_body(): a_all = lax.all_to_all(copies, 'row', 0, 0)]
where the time goes in v5:
time: 40.7 us; the launch traced here: 40.3 us
  Pallas kernels  22.8 us (56%)
  starting transfers between devices  12.8 us (31%)
  waiting for transfers between devices  3.72 us (9%)
  local copies, waits for them, and re-layouts  0.81 us (2%)
    pallas_call x1, Pallas kernels, correct(): pl.pallas_call(correct_kernel, out_shape=jax.ShapeDtypeStruct((rows, n_ro...  8.02 us
    pallas_call x1, Pallas kernels, rotate_grads(): pl.pallas_call(rotate_grads_kernel, out_shape=jax.ShapeDtypeStruct((token...  5.81 us
    ppermute x3, starting transfers between devices, few_tokens_body(): lax.ppermute(both, 'row', [(i, (i + 2 * k) % n_row) for i in range(n_row)])  5.2 us
    all_to_all x1, starting transfers between devices, few_tokens_body(): a_all = lax.all_to_all(copies, 'row', 0, 0)  4.06 us
    pallas_call x1, Pallas kernels, load(): pl.pallas_call(load_kernel, out_shape=jax.ShapeDtypeStruct(w.shape, w.dty...  3.39 us
    ppermute x1, starting transfers between devices, few_tokens_body(): beside = lax.ppermute(own, 'row', [(i, i ^ 1) for i in range(n_row)])  3 us
    pallas_call x1, Pallas kernels, rotate_acts(): pl.pallas_call(rotate_second_kernel, out_shape=(jax.ShapeDtypeStruct((cop...  2.02 us
    pallas_call x1, Pallas kernels, pack(): pl.pallas_call(pack_kernel, out_shape=jax.ShapeDtypeStruct((rows, width +...  1.38 us
  transfers between devices with their start and end apart: 7, of which 5 were waited for; matrix products, arithmetic and copies ran while one was open for 0% of the time, Pallas kernels for 28%

profile of v5, /device:TPU:0, one launch (start us, length us, event | category | flops | bytes accessed | tf_op | source)
XLA Modules:
  0.0 40.3 jit_solution(11570787170153274991)
XLA Ops:
  0.0 1.4 %pack.1.own_ref = bf16[2,9216]{1,0:T(2,128)(2,1)} custom-call(bf16[2,4096]{1,0:T(2,128)(2,1)} %acts_ref.1, bf16[2,5120]{1,0:T(2,128)(2,1)} %grads_ref.1), custom_call_target="tpu_custom_call" | custom-call | bytes 80000 | tf_op jit(solution)/shard_map/pack/pallas_call | solution.py:122
  1.4 3.0 %collective-permute-start = (bf16[2,9216]{1,0:T(2,128)(2,1)}, bf16[2,9216]{1,0:T(2,128)(2,1)S(1)}, u32[]{:S(2)}, u32[]{:S(2)}) collective-permute-start(bf16[2,9216]{1,0:T(2,128)(2,1)} %pack.1.own_ref), channel_id=1, source_target_pairs={{0,2},{2,0},{4,6},{6,4},{8,10},{10,8},{12,14},{14,12},{1,3},{3,1},... | collective-permute-start | bytes 110600 | tf_op jit(solution)/shard_map/ppermute | solution.py:369
  4.4 0.8 %copy-done = bf16[2,9216]{1,0:T(2,128)(2,1)S(1)} copy-done((bf16[2,9216]{1,0:T(2,128)(2,1)S(1)}, bf16[2,9216]{1,0:T(2,128)(2,1)}, u32[]{:S(2)}) %copy-start) | copy-done | bytes 36888
  5.2 1.3 %collective-permute-done.beside_ref = bf16[2,9216]{1,0:T(2,128)(2,1)S(1)} collective-permute-done((bf16[2,9216]{1,0:T(2,128)(2,1)}, bf16[2,9216]{1,0:T(2,128)(2,1)S(1)}, u32[]{:S(2)}, u32[]{:S(2)}) %collective-permute-start) | collective-permute-done | bytes 36896 | tf_op jit(solution)/shard_map/ppermute | solution.py:369
  6.5 0.0 copy-start.2
  6.6 4.2 %collective-permute-start.3 = (bf16[2,2,9216]{2,1,0:T(2,128)(2,1)S(1)}, bf16[2,2,9216]{2,1,0:T(2,128)(2,1)S(1)}, u32[]{:S(2)}, u32[]{:S(2)}) collective-permute-start(bf16[2,2,9216]{2,1,0:T(2,128)(2,1)S(1)} %merge.1.p0), channel_id=1, source_target_pairs={{0,12},{2,14},{4,0},{6,2},{8,4},{10,6},{12,8},{14,10},{1,13},{3,15... | collective-permute-start | bytes 221192 | tf_op jit(solution)/shard_map/ppermute | solution.py:372
  10.7 0.0 collective-permute-start.2
  10.7 1.0 %collective-permute-start.1 = (bf16[2,2,9216]{2,1,0:T(2,128)(2,1)S(1)}, bf16[2,2,9216]{2,1,0:T(2,128)(2,1)S(1)}, u32[]{:S(2)}, u32[]{:S(2)}) collective-permute-start(bf16[2,2,9216]{2,1,0:T(2,128)(2,1)S(1)} %merge.1.p0), channel_id=1, source_target_pairs={{0,4},{2,6},{4,8},{6,10},{8,12},{10,14},{12,0},{14,2},{1,5},{3,7},... | collective-permute-start | bytes 221192 | tf_op jit(solution)/shard_map/ppermute | solution.py:372
  11.8 3.4 %load.1.basis_ref.w_ref = bf16[1,512,8192]{2,1,0:T(8,128)(2,1)S(1)} custom-call(bf16[1,512,8192]{2,1,0:T(8,128)(2,1)} %w_ref.2), custom_call_target="tpu_custom_call" | custom-call | bytes 8388608 | tf_op jit(solution)/shard_map/load/pallas_call | solution.py:200
  15.2 0.7 %pairs.1 = (bf16[80,16]{1,0:T(8,128)(2,1)S(1)}, bf16[80,16]{1,0:T(8,128)(2,1)S(1)}, bf16[80,16]{1,0:T(8,128)(2,1)S(1)}, bf16[80,16]{1,0:T(8,128)(2,1)S(1)}, bf16[16,16]{1,0:T(8,128)(2,1)S(1)}) custom-call(s32[1,12]{1,0:T(1,128)S(1)} %bitcast.2, s32[1,12]{1,0:T(1,128)S(1)} %bitcast.3), custom_call_target="tpu_custom_call" | custom-call | flops 2000000 | bytes 40000 | tf_op jit(solution)/shard_map/pairs/pallas_call | solution.py:97
  15.9 0.0 collective-permute-done.3.p3
  15.9 0.1 collective-permute-done.2.p2
  16.0 0.9 %collective-permute-done.1.p1 = bf16[2,2,9216]{2,1,0:T(2,128)(2,1)S(1)} collective-permute-done((bf16[2,2,9216]{2,1,0:T(2,128)(2,1)S(1)}, bf16[2,2,9216]{2,1,0:T(2,128)(2,1)S(1)}, u32[]{:S(2)}, u32[]{:S(2)}) %collective-permute-start.1) | collective-permute-done | bytes 73760 | tf_op jit(solution)/shard_map/ppermute | solution.py:372
  16.9 0.2 assemble.1
  17.1 0.1 collective-permute-start.4
  17.2 1.3 %rotate_first.1 = (f32[512,16]{1,0:T(8,128)S(1)}, bf16[128,5120]{1,0:T(8,128)(2,1)S(1)}) custom-call(bf16[1,512,8192]{2,1,0:T(8,128)(2,1)S(1)} %load.1.basis_ref.w_ref, bf16[16,4096]{1,0:T(8,128)(2,1)S(1)} %get-tuple-element.17.x_ref, bf16[1280,5120]{1,0:T(8,128)(2,1)} %w_ref.3), custom_call_target="tpu_custom_call" | custom-call | flops 1073741824 | bytes 4194304 | tf_op jit(solution)/shard_map/rotate_first/pallas_call | solution.py:252
  18.5 0.0 collective-permute-done.4.x_ref
  18.5 2.0 %rotate_second.1 = (bf16[8,16,512]{2,1,0:T(8,128)(2,1)}, bf16[128,5120]{1,0:T(8,128)(2,1)S(1)}) custom-call(bf16[1,512,8192]{2,1,0:T(8,128)(2,1)S(1)} %load.1.basis_ref.w_ref, bf16[16,4096]{1,0:T(8,128)(2,1)S(1)} %collective-permute-done.4.x_ref, f32[512,16]{1,0:T(8,128)S(1)} %get-tuple-element.19.part_ref, bf16[16,16]{1,0:T(8,128)(2,1)S(1)} %get-tuple-element.16.perm_ref, ...), custom_call_target="tpu_custom_call" | custom-call | flops 1073741824 | bytes 4194304 | tf_op jit(solution)/shard_map/rotate_second/pallas_call | solution.py:265
  20.5 4.1 %all-to-all-start = ((bf16[8,16,512]{2,1,0:T(8,128)(2,1)}), bf16[8,16,512]{2,1,0:T(8,128)(2,1)S(1)}, u32[]{:S(2)}, u32[]{:S(2)}) async-start(bf16[8,16,512]{2,1,0:T(8,128)(2,1)} %get-tuple-element.22), calls=%async_computation | async-start | bytes 262144 | tf_op jit(solution)/shard_map/all_to_all | solution.py:380
  24.6 5.8 %rotate_grads.1.own_ref = f32[16,1280]{1,0:T(8,128)S(1)} custom-call(bf16[128,5120]{1,0:T(8,128)(2,1)S(1)} %get-tuple-element.18.head0_ref, bf16[128,5120]{1,0:T(8,128)(2,1)S(1)} %get-tuple-element.20.head1_ref, bf16[1280,5120]{1,0:T(8,128)(2,1)} %w_ref.3, bf16[16,5120]{1,0:T(8,128)(2,1)S(1)} %get-tuple-element.21.x_ref), custom_call_target="tpu_custom_call" | custom-call | flops 3355443200 | bytes 13107200 | tf_op jit(solution)/shard_map/rotate_grads/pallas_call | solution.py:303
  30.4 0.4 %collective-permute-start.5 = (f32[16,1280]{1,0:T(8,128)S(1)}, f32[16,1280]{1,0:T(8,128)S(1)}, u32[]{:S(2)}, u32[]{:S(2)}) collective-permute-start(f32[16,1280]{1,0:T(8,128)S(1)} %rotate_grads.1.own_ref), channel_id=1, source_target_pairs={{0,1},{1,0},{2,3},{3,2},{4,5},{5,4},{6,7},{7,6},{8,9},{9,8},{10,11... | collective-permute-start | bytes 245768 | tf_op jit(solution)/shard_map/ppermute | solution.py:382
  30.9 0.9 %collective-permute-done.5.other_ref = f32[16,1280]{1,0:T(8,128)S(1)} collective-permute-done((f32[16,1280]{1,0:T(8,128)S(1)}, f32[16,1280]{1,0:T(8,128)S(1)}, u32[]{:S(2)}, u32[]{:S(2)}) %collective-permute-start.5) | collective-permute-done | bytes 81952 | tf_op jit(solution)/shard_map/ppermute | solution.py:382
  31.8 0.4 %all-to-all-done.a_ref = bf16[8,16,512]{2,1,0:T(8,128)(2,1)S(1)} async-done(((bf16[8,16,512]{2,1,0:T(8,128)(2,1)}), bf16[8,16,512]{2,1,0:T(8,128)(2,1)S(1)}, u32[]{:S(2)}, u32[]{:S(2)}) %all-to-all-start) | async-done | bytes 131104 | tf_op jit(solution)/shard_map/all_to_all | solution.py:380
  32.2 8.0 %correct.1 = f32[1280,4096]{1,0:T(8,128)} custom-call(f32[16,1280]{1,0:T(8,128)S(1)} %rotate_grads.1.own_ref, f32[16,1280]{1,0:T(8,128)S(1)} %collective-permute-done.5.other_ref, bf16[8,16,512]{2,1,0:T(8,128)(2,1)S(1)} %all-to-all-done.a_ref, bf16[80,16]{1,0:T(8,128)(2,1)S(1)} %get-tuple-element.23.s1a_ref, bf16[80,16]{1,0:T(8,128)(2,1)S(1)} %get-tuple-element.24.s2a_ref, ...), custom_call_target="tpu_custom_call" | custom-call | flops 2684354560 | bytes 20971520 | tf_op jit(solution)/shard_map/correct/pallas_call | solution.py:345
  (6 shorter events, 0.0 us)
Async XLA Ops:
  1.4 5.2 %collective-permute-start = (bf16[2,9216]{1,0:T(2,128)(2,1)}, bf16[2,9216]{1,0:T(2,128)(2,1)S(1)}, u32[]{:S(2)}, u32[]{:S(2)}) collective-permute-start(bf16[2,9216]{1,0:T(2,128)(2,1)} %pack.1.own_ref), channel_id=1, source_target_pairs={{0,2},{2,0},{4,6},{6,4},{8,10},{10,8},{12,14},{14,12},{1,3},{3,1},... | collective-permute-start | bytes 110600 | tf_op jit(solution)/shard_map/ppermute | solution.py:369
  4.4 0.8 %copy-start = (bf16[2,9216]{1,0:T(2,128)(2,1)S(1)}, bf16[2,9216]{1,0:T(2,128)(2,1)}, u32[]{:S(2)}) copy-start(bf16[2,9216]{1,0:T(2,128)(2,1)} %pack.1.own_ref) | copy-start | bytes 110596
  6.5 8.6 %copy-start.1 = (s32[12]{0:T(128)S(1)}, s32[12]{0:T(128)}, u32[]{:S(2)}) copy-start(s32[12]{0:T(128)} %param.10) | copy-start | bytes 148
  6.5 8.6 %copy-start.2 = (s32[12]{0:T(128)S(1)}, s32[12]{0:T(128)}, u32[]{:S(2)}) copy-start(s32[12]{0:T(128)} %param.11) | copy-start | bytes 148
  6.6 9.3 %collective-permute-start.3 = (bf16[2,2,9216]{2,1,0:T(2,128)(2,1)S(1)}, bf16[2,2,9216]{2,1,0:T(2,128)(2,1)S(1)}, u32[]{:S(2)}, u32[]{:S(2)}) collective-permute-start(bf16[2,2,9216]{2,1,0:T(2,128)(2,1)S(1)} %merge.1.p0), channel_id=1, source_target_pairs={{0,12},{2,14},{4,0},{6,2},{8,4},{10,6},{12,8},{14,10},{1,13},{3,15... | collective-permute-start | bytes 221192 | tf_op jit(solution)/shard_map/ppermute | solution.py:372
  10.7 5.3 %collective-permute-start.2 = (bf16[2,2,9216]{2,1,0:T(2,128)(2,1)S(1)}, bf16[2,2,9216]{2,1,0:T(2,128)(2,1)S(1)}, u32[]{:S(2)}, u32[]{:S(2)}) collective-permute-start(bf16[2,2,9216]{2,1,0:T(2,128)(2,1)S(1)} %merge.1.p0), channel_id=1, source_target_pairs={{0,8},{2,10},{4,12},{6,14},{8,0},{10,2},{12,4},{14,6},{1,9},{3,11}... | collective-permute-start | bytes 221192 | tf_op jit(solution)/shard_map/ppermute | solution.py:372
  10.7 6.2 %collective-permute-start.1 = (bf16[2,2,9216]{2,1,0:T(2,128)(2,1)S(1)}, bf16[2,2,9216]{2,1,0:T(2,128)(2,1)S(1)}, u32[]{:S(2)}, u32[]{:S(2)}) collective-permute-start(bf16[2,2,9216]{2,1,0:T(2,128)(2,1)S(1)} %merge.1.p0), channel_id=1, source_target_pairs={{0,4},{2,6},{4,8},{6,10},{8,12},{10,14},{12,0},{14,2},{1,5},{3,7},... | collective-permute-start | bytes 221192 | tf_op jit(solution)/shard_map/ppermute | solution.py:372
  17.1 1.4 %collective-permute-start.4 = (bf16[16,4096]{1,0:T(8,128)(2,1)S(1)}, bf16[16,4096]{1,0:T(8,128)(2,1)S(1)}, u32[]{:S(2)}, u32[]{:S(2)}) collective-permute-start(bf16[16,4096]{1,0:T(8,128)(2,1)S(1)} %get-tuple-element.17.x_ref), channel_id=1, source_target_pairs={{0,1},{1,0},{2,3},{3,2},{4,5},{5,4},{6,7},{7,6},{8,9},{9,8},{10,11... | collective-permute-start | bytes 393224 | tf_op jit(solution)/shard_map/ppermute | solution.py:377
  20.5 11.7 %all-to-all-start = ((bf16[8,16,512]{2,1,0:T(8,128)(2,1)}), bf16[8,16,512]{2,1,0:T(8,128)(2,1)S(1)}, u32[]{:S(2)}, u32[]{:S(2)}) async-start(bf16[8,16,512]{2,1,0:T(8,128)(2,1)} %get-tuple-element.22), calls=%async_computation | async-start | bytes 262144 | tf_op jit(solution)/shard_map/all_to_all | solution.py:380
  30.4 1.4 %collective-permute-start.5 = (f32[16,1280]{1,0:T(8,128)S(1)}, f32[16,1280]{1,0:T(8,128)S(1)}, u32[]{:S(2)}, u32[]{:S(2)}) collective-permute-start(f32[16,1280]{1,0:T(8,128)S(1)} %rotate_grads.1.own_ref), channel_id=1, source_target_pairs={{0,1},{1,0},{2,3},{3,2},{4,5},{5,4},{6,7},{7,6},{8,9},{9,8},{10,11... | collective-permute-start | bytes 245768 | tf_op jit(solution)/shard_map/ppermute | solution.py:382

commit v6 on v5

--- a/solution.py
+++ b/solution.py
@@ -8,6 +8,7 @@
 
 N_SEQ = 6
 PAIR_ROWS = 80
+FIRST = 2
 HEADS = (128, 128)
 BF16 = jnp.bfloat16
 F32 = jnp.float32
@@ -286,12 +287,14 @@
         pltpu.make_async_copy(w_ref.at[first + rows.start : first + rows.stop, :], held.at[rows, :], sems.at[part])
         for part, rows in enumerate(spans)
     ]
-    for copy in copies:
+    for copy in copies[:2]:
         copy.start()
     o_ref[:, : HEADS[0]] = row_dots(head0_ref, x_ref[...], 0, HEADS[0]).T
     o_ref[:, HEADS[0] : first] = row_dots(head1_ref, x_ref[...], 0, HEADS[1]).T
-    for copy, rows in zip(copies, spans):
+    for part, (copy, rows) in enumerate(zip(copies, spans)):
         copy.wait()
+        if part + 2 < parts:
+            copies[part + 2].start()
         o_ref[:, first + rows.start : first + rows.stop] = row_dots(held, x_ref[...], rows.start, rows.stop).T
 
 
@@ -320,44 +323,67 @@
     return high, low
 
 
-def correct_kernel(own_ref, other_ref, a_ref, s1a_ref, s2a_ref, s1g_ref, s2g_ref, o_ref, buffer, g_pairs, sems):
+def pair_grads_kernel(own_ref, other_ref, s1_ref, s2_ref, o_ref):
     tokens = own_ref.shape[0]
+    g_rot = (own_ref[...] + other_ref[...]).astype(BF16)
+    product = dot(s1_ref[...], g_rot) * dot(s2_ref[...], g_rot) * (1.0 / tokens)
+    high, low = split(product)
+    o_ref[...] = jnp.concatenate([high, high, low], axis=0).T
+
+
+def pair_grads(own, other, s1, s2):
+    rows = own.shape[1]
+    return pl.pallas_call(
+        pair_grads_kernel,
+        out_shape=jax.ShapeDtypeStruct((rows, 3 * PAIR_ROWS), BF16),
+        in_specs=[VMEM] * 4,
+        out_specs=VMEM,
+        compiler_params=pltpu.CompilerParams(vmem_limit_bytes=6 * MIB),
+        cost_estimate=pl.CostEstimate(flops=2_000_000, bytes_accessed=2_000_000, transcendentals=0),
+        name="pair_grads",
+    )(own, other, s1, s2)
+
+
+def correct_kernel(g_ref, a_ref, s1_ref, s2_ref, o_ref, buffer, sems):
+    rows = g_ref.shape[0]
     n_block, _, width = a_ref.shape
-    g_rot = (own_ref[...] + other_ref[...]).astype(BF16)
-    product = dot(s1g_ref[...], g_rot) * dot(s2g_ref[...], g_rot) * (1.0 / tokens)
-    high, low = split(product)
-    g_pairs[...] = jnp.concatenate([high, high, low], axis=0).T
+    step = rows // (sems.shape[0] - n_block + 1)
     copies = []
     for block in range(n_block):
         a_rot = a_ref[block]
-        high, low = split(dot(s1a_ref[...], a_rot) * dot(s2a_ref[...], a_rot))
+        high, low = split(dot(s1_ref[...], a_rot) * dot(s2_ref[...], a_rot))
+        a_pairs = jnp.concatenate([high, low, high], axis=0)
         columns = slice(block * width, (block + 1) * width)
-        buffer[:, columns] = dot(g_pairs[...], jnp.concatenate([high, low, high], axis=0))
-        copies.append(pltpu.make_async_copy(buffer.at[:, columns], o_ref.at[:, columns], sems.at[block]))
-        copies[-1].start()
+        size = step if block == 0 else rows
+        for first in range(0, rows, size):
+            span = slice(first, first + size)
+            buffer[span, columns] = dot(g_ref[span, :], a_pairs)
+            copies.append(
+                pltpu.make_async_copy(buffer.at[span, columns], o_ref.at[span, columns], sems.at[len(copies)])
+            )
+            copies[-1].start()
     for copy in copies:
         copy.wait()
 
 
-def correct(own, other, a_all, s1a, s2a, s1g, s2g):
-    tokens, rows = own.shape
+def correct(g_pairs, a_all, s1, s2):
+    rows = g_pairs.shape[0]
     n_row, _, width = a_all.shape
     return pl.pallas_call(
         correct_kernel,
         out_shape=jax.ShapeDtypeStruct((rows, n_row * width), F32),
-        in_specs=[VMEM] * 7,
+        in_specs=[VMEM] * 4,
         out_specs=pl.BlockSpec(memory_space=pl.ANY),
         scratch_shapes=[
             pltpu.VMEM((rows, n_row * width), F32),
-            pltpu.VMEM((rows, 3 * PAIR_ROWS), BF16),
-            pltpu.SemaphoreType.DMA((n_row,)),
+            pltpu.SemaphoreType.DMA((n_row + FIRST - 1,)),
         ],
         compiler_params=pltpu.CompilerParams(vmem_limit_bytes=32 * MIB),
         cost_estimate=pl.CostEstimate(
             flops=2 * rows * n_row * width * 256, bytes_accessed=rows * n_row * width * 4, transcendentals=0
         ),
         name="correct",
-    )(own, other, a_all, s1a, s2a, s1g, s2g)
+    )(g_pairs, a_all, s1, s2)
 
 
 def few_tokens_body(acts, grads, eigen_a, eigen_s_rows, doc_lengths, doc_plan):
@@ -380,7 +406,7 @@
     a_all = lax.all_to_all(copies, "row", 0, 0)
     g_own = rotate_grads((head0, head1), eigen_s_rows, grads_own)
     g_other = lax.ppermute(g_own, "col", [(0, 1), (1, 0)])
-    return correct(g_own, g_other, a_all, s1a, s2a, s1g, s2g)
+    return correct(pair_grads(g_own, g_other, s1g, s2g), a_all, s1a, s2a)
 
 
 def solution(mesh):

time: 40.7 us -> 40.4 us (level)
    pallas_call x0 -> x1, Pallas kernels: none -> 0.42 us  [pair_grads(): pl.pallas_call(pair_grads_kernel, out_shape=jax.ShapeDtypeStruct((rows, 3...]
where the time goes in v6:
time: 40.4 us; the launch traced here: 40 us
  Pallas kernels  22.6 us (56%)
  starting transfers between devices  12.8 us (32%)
  waiting for transfers between devices  3.69 us (9%)
  local copies, waits for them, and re-layouts  0.81 us (2%)
    pallas_call x1, Pallas kernels, correct(): pl.pallas_call(correct_kernel, out_shape=jax.ShapeDtypeStruct((rows, n_ro...  7.73 us
    pallas_call x1, Pallas kernels, rotate_grads(): pl.pallas_call(rotate_grads_kernel, out_shape=jax.ShapeDtypeStruct((token...  5.41 us
    ppermute x3, starting transfers between devices, few_tokens_body(): lax.ppermute(both, 'row', [(i, (i + 2 * k) % n_row) for i in range(n_row)])  5.2 us
    all_to_all x1, starting transfers between devices, few_tokens_body(): a_all = lax.all_to_all(copies, 'row', 0, 0)  4.06 us
    pallas_call x1, Pallas kernels, load(): pl.pallas_call(load_kernel, out_shape=jax.ShapeDtypeStruct(w.shape, w.dty...  3.39 us
    ppermute x1, starting transfers between devices, few_tokens_body(): beside = lax.ppermute(own, 'row', [(i, i ^ 1) for i in range(n_row)])  3 us
    pallas_call x1, Pallas kernels, rotate_acts(): pl.pallas_call(rotate_second_kernel, out_shape=(jax.ShapeDtypeStruct((cop...  2.02 us
    pallas_call x1, Pallas kernels, pack(): pl.pallas_call(pack_kernel, out_shape=jax.ShapeDtypeStruct((rows, width +...  1.38 us
  transfers between devices with their start and end apart: 7, of which 5 were waited for; matrix products, arithmetic and copies ran while one was open for 0% of the time, Pallas kernels for 28%

profile of v6, /device:TPU:0, one launch (start us, length us, event | category | flops | bytes accessed | tf_op | source)
XLA Modules:
  0.0 40.0 jit_solution(16210679569394114570)
XLA Ops:
  0.0 1.4 %pack.1.own_ref = bf16[2,9216]{1,0:T(2,128)(2,1)} custom-call(bf16[2,4096]{1,0:T(2,128)(2,1)} %acts_ref.1, bf16[2,5120]{1,0:T(2,128)(2,1)} %grads_ref.1), custom_call_target="tpu_custom_call" | custom-call | bytes 80000 | tf_op jit(solution)/shard_map/pack/pallas_call | solution.py:123
  1.4 3.0 %collective-permute-start = (bf16[2,9216]{1,0:T(2,128)(2,1)}, bf16[2,9216]{1,0:T(2,128)(2,1)S(1)}, u32[]{:S(2)}, u32[]{:S(2)}) collective-permute-start(bf16[2,9216]{1,0:T(2,128)(2,1)} %pack.1.own_ref), channel_id=1, source_target_pairs={{0,2},{2,0},{4,6},{6,4},{8,10},{10,8},{12,14},{14,12},{1,3},{3,1},... | collective-permute-start | bytes 110600 | tf_op jit(solution)/shard_map/ppermute | solution.py:395
  4.4 0.8 %copy-done = bf16[2,9216]{1,0:T(2,128)(2,1)S(1)} copy-done((bf16[2,9216]{1,0:T(2,128)(2,1)S(1)}, bf16[2,9216]{1,0:T(2,128)(2,1)}, u32[]{:S(2)}) %copy-start) | copy-done | bytes 36888
  5.2 1.3 %collective-permute-done.beside_ref = bf16[2,9216]{1,0:T(2,128)(2,1)S(1)} collective-permute-done((bf16[2,9216]{1,0:T(2,128)(2,1)}, bf16[2,9216]{1,0:T(2,128)(2,1)S(1)}, u32[]{:S(2)}, u32[]{:S(2)}) %collective-permute-start) | collective-permute-done | bytes 36896 | tf_op jit(solution)/shard_map/ppermute | solution.py:395
  6.5 0.0 copy-start.2
  6.6 4.2 %collective-permute-start.3 = (bf16[2,2,9216]{2,1,0:T(2,128)(2,1)S(1)}, bf16[2,2,9216]{2,1,0:T(2,128)(2,1)S(1)}, u32[]{:S(2)}, u32[]{:S(2)}) collective-permute-start(bf16[2,2,9216]{2,1,0:T(2,128)(2,1)S(1)} %merge.1.p0), channel_id=1, source_target_pairs={{0,12},{2,14},{4,0},{6,2},{8,4},{10,6},{12,8},{14,10},{1,13},{3,15... | collective-permute-start | bytes 221192 | tf_op jit(solution)/shard_map/ppermute | solution.py:398
  10.7 0.0 collective-permute-start.2
  10.7 1.0 %collective-permute-start.1 = (bf16[2,2,9216]{2,1,0:T(2,128)(2,1)S(1)}, bf16[2,2,9216]{2,1,0:T(2,128)(2,1)S(1)}, u32[]{:S(2)}, u32[]{:S(2)}) collective-permute-start(bf16[2,2,9216]{2,1,0:T(2,128)(2,1)S(1)} %merge.1.p0), channel_id=1, source_target_pairs={{0,4},{2,6},{4,8},{6,10},{8,12},{10,14},{12,0},{14,2},{1,5},{3,7},... | collective-permute-start | bytes 221192 | tf_op jit(solution)/shard_map/ppermute | solution.py:398
  11.8 3.4 %load.1.basis_ref.w_ref = bf16[1,512,8192]{2,1,0:T(8,128)(2,1)S(1)} custom-call(bf16[1,512,8192]{2,1,0:T(8,128)(2,1)} %w_ref.2), custom_call_target="tpu_custom_call" | custom-call | bytes 8388608 | tf_op jit(solution)/shard_map/load/pallas_call | solution.py:201
  15.2 0.7 %pairs.1 = (bf16[80,16]{1,0:T(8,128)(2,1)S(1)}, bf16[80,16]{1,0:T(8,128)(2,1)S(1)}, bf16[80,16]{1,0:T(8,128)(2,1)S(1)}, bf16[80,16]{1,0:T(8,128)(2,1)S(1)}, bf16[16,16]{1,0:T(8,128)(2,1)S(1)}) custom-call(s32[1,12]{1,0:T(1,128)S(1)} %bitcast.2, s32[1,12]{1,0:T(1,128)S(1)} %bitcast.3), custom_call_target="tpu_custom_call" | custom-call | flops 2000000 | bytes 40000 | tf_op jit(solution)/shard_map/pairs/pallas_call | solution.py:98
  15.9 0.0 collective-permute-done.3.p3
  15.9 0.1 collective-permute-done.2.p2
  16.0 0.9 %collective-permute-done.1.p1 = bf16[2,2,9216]{2,1,0:T(2,128)(2,1)S(1)} collective-permute-done((bf16[2,2,9216]{2,1,0:T(2,128)(2,1)S(1)}, bf16[2,2,9216]{2,1,0:T(2,128)(2,1)S(1)}, u32[]{:S(2)}, u32[]{:S(2)}) %collective-permute-start.1) | collective-permute-done | bytes 73760 | tf_op jit(solution)/shard_map/ppermute | solution.py:398
  16.9 0.2 assemble.1
  17.1 0.1 collective-permute-start.4
  17.2 1.3 %rotate_first.1 = (f32[512,16]{1,0:T(8,128)S(1)}, bf16[128,5120]{1,0:T(8,128)(2,1)S(1)}) custom-call(bf16[1,512,8192]{2,1,0:T(8,128)(2,1)S(1)} %load.1.basis_ref.w_ref, bf16[16,4096]{1,0:T(8,128)(2,1)S(1)} %get-tuple-element.17.x_ref, bf16[1280,5120]{1,0:T(8,128)(2,1)} %w_ref.3), custom_call_target="tpu_custom_call" | custom-call | flops 1073741824 | bytes 4194304 | tf_op jit(solution)/shard_map/rotate_first/pallas_call | solution.py:253
  18.5 2.0 %rotate_second.1 = (bf16[8,16,512]{2,1,0:T(8,128)(2,1)}, bf16[128,5120]{1,0:T(8,128)(2,1)S(1)}) custom-call(bf16[1,512,8192]{2,1,0:T(8,128)(2,1)S(1)} %load.1.basis_ref.w_ref, bf16[16,4096]{1,0:T(8,128)(2,1)S(1)} %collective-permute-done.4.x_ref, f32[512,16]{1,0:T(8,128)S(1)} %get-tuple-element.19.part_ref, bf16[16,16]{1,0:T(8,128)(2,1)S(1)} %get-tuple-element.16.perm_ref, ...), custom_call_target="tpu_custom_call" | custom-call | flops 1073741824 | bytes 4194304 | tf_op jit(solution)/shard_map/rotate_second/pallas_call | solution.py:266
  20.5 4.1 %all-to-all-start = ((bf16[8,16,512]{2,1,0:T(8,128)(2,1)}), bf16[8,16,512]{2,1,0:T(8,128)(2,1)S(1)}, u32[]{:S(2)}, u32[]{:S(2)}) async-start(bf16[8,16,512]{2,1,0:T(8,128)(2,1)} %get-tuple-element.24), calls=%async_computation | async-start | bytes 262144 | tf_op jit(solution)/shard_map/all_to_all | solution.py:406
  24.6 5.4 %rotate_grads.1.own_ref = f32[16,1280]{1,0:T(8,128)S(1)} custom-call(bf16[128,5120]{1,0:T(8,128)(2,1)S(1)} %get-tuple-element.18.head0_ref, bf16[128,5120]{1,0:T(8,128)(2,1)S(1)} %get-tuple-element.20.head1_ref, bf16[1280,5120]{1,0:T(8,128)(2,1)} %w_ref.3, bf16[16,5120]{1,0:T(8,128)(2,1)S(1)} %get-tuple-element.21.x_ref), custom_call_target="tpu_custom_call" | custom-call | flops 3355443200 | bytes 13107200 | tf_op jit(solution)/shard_map/rotate_grads/pallas_call | solution.py:306
  30.0 0.4 %collective-permute-start.5 = (f32[16,1280]{1,0:T(8,128)S(1)}, f32[16,1280]{1,0:T(8,128)S(1)}, u32[]{:S(2)}, u32[]{:S(2)}) collective-permute-start(f32[16,1280]{1,0:T(8,128)S(1)} %rotate_grads.1.own_ref), channel_id=1, source_target_pairs={{0,1},{1,0},{2,3},{3,2},{4,5},{5,4},{6,7},{7,6},{8,9},{9,8},{10,11... | collective-permute-start | bytes 245768 | tf_op jit(solution)/shard_map/ppermute | solution.py:408
  30.5 0.9 %collective-permute-done.5.other_ref = f32[16,1280]{1,0:T(8,128)S(1)} collective-permute-done((f32[16,1280]{1,0:T(8,128)S(1)}, f32[16,1280]{1,0:T(8,128)S(1)}, u32[]{:S(2)}, u32[]{:S(2)}) %collective-permute-start.5) | collective-permute-done | bytes 81952 | tf_op jit(solution)/shard_map/ppermute | solution.py:408
  31.4 0.4 %pair_grads.1.g_ref = bf16[1280,240]{1,0:T(8,128)(2,1)S(1)} custom-call(f32[16,1280]{1,0:T(8,128)S(1)} %rotate_grads.1.own_ref, f32[16,1280]{1,0:T(8,128)S(1)} %collective-permute-done.5.other_ref, bf16[80,16]{1,0:T(8,128)(2,1)S(1)} %get-tuple-element.22.s1_ref, bf16[80,16]{1,0:T(8,128)(2,1)S(1)} %get-tuple-element.23.s2_ref), custom_call_target="tpu_custom_call" | custom-call | flops 2000000 | bytes 2000000 | tf_op jit(solution)/shard_map/pair_grads/pallas_call | solution.py:336
  31.8 0.4 %all-to-all-done.a_ref = bf16[8,16,512]{2,1,0:T(8,128)(2,1)S(1)} async-done(((bf16[8,16,512]{2,1,0:T(8,128)(2,1)}), bf16[8,16,512]{2,1,0:T(8,128)(2,1)S(1)}, u32[]{:S(2)}, u32[]{:S(2)}) %all-to-all-start) | async-done | bytes 131104 | tf_op jit(solution)/shard_map/all_to_all | solution.py:406
  32.2 7.7 %correct.1 = f32[1280,4096]{1,0:T(8,128)} custom-call(bf16[1280,240]{1,0:T(8,128)(2,1)S(1)} %pair_grads.1.g_ref, bf16[8,16,512]{2,1,0:T(8,128)(2,1)S(1)} %all-to-all-done.a_ref, bf16[80,16]{1,0:T(8,128)(2,1)S(1)} %get-tuple-element.25.s1_ref, bf16[80,16]{1,0:T(8,128)(2,1)S(1)} %get-tuple-element.26.s2_ref), custom_call_target="tpu_custom_call" | custom-call | flops 2684354560 | bytes 20971520 | tf_op jit(solution)/shard_map/correct/pallas_call | solution.py:372
  (7 shorter events, 0.0 us)
Async XLA Ops:
  1.4 5.2 %collective-permute-start = (bf16[2,9216]{1,0:T(2,128)(2,1)}, bf16[2,9216]{1,0:T(2,128)(2,1)S(1)}, u32[]{:S(2)}, u32[]{:S(2)}) collective-permute-start(bf16[2,9216]{1,0:T(2,128)(2,1)} %pack.1.own_ref), channel_id=1, source_target_pairs={{0,2},{2,0},{4,6},{6,4},{8,10},{10,8},{12,14},{14,12},{1,3},{3,1},... | collective-permute-start | bytes 110600 | tf_op jit(solution)/shard_map/ppermute | solution.py:395
  4.4 0.8 %copy-start = (bf16[2,9216]{1,0:T(2,128)(2,1)S(1)}, bf16[2,9216]{1,0:T(2,128)(2,1)}, u32[]{:S(2)}) copy-start(bf16[2,9216]{1,0:T(2,128)(2,1)} %pack.1.own_ref) | copy-start | bytes 110596
  6.5 8.6 %copy-start.1 = (s32[12]{0:T(128)S(1)}, s32[12]{0:T(128)}, u32[]{:S(2)}) copy-start(s32[12]{0:T(128)} %param.10) | copy-start | bytes 148
  6.5 8.6 %copy-start.2 = (s32[12]{0:T(128)S(1)}, s32[12]{0:T(128)}, u32[]{:S(2)}) copy-start(s32[12]{0:T(128)} %param.11) | copy-start | bytes 148
  6.6 9.3 %collective-permute-start.3 = (bf16[2,2,9216]{2,1,0:T(2,128)(2,1)S(1)}, bf16[2,2,9216]{2,1,0:T(2,128)(2,1)S(1)}, u32[]{:S(2)}, u32[]{:S(2)}) collective-permute-start(bf16[2,2,9216]{2,1,0:T(2,128)(2,1)S(1)} %merge.1.p0), channel_id=1, source_target_pairs={{0,12},{2,14},{4,0},{6,2},{8,4},{10,6},{12,8},{14,10},{1,13},{3,15... | collective-permute-start | bytes 221192 | tf_op jit(solution)/shard_map/ppermute | solution.py:398
  10.7 5.3 %collective-permute-start.2 = (bf16[2,2,9216]{2,1,0:T(2,128)(2,1)S(1)}, bf16[2,2,9216]{2,1,0:T(2,128)(2,1)S(1)}, u32[]{:S(2)}, u32[]{:S(2)}) collective-permute-start(bf16[2,2,9216]{2,1,0:T(2,128)(2,1)S(1)} %merge.1.p0), channel_id=1, source_target_pairs={{0,8},{2,10},{4,12},{6,14},{8,0},{10,2},{12,4},{14,6},{1,9},{3,11}... | collective-permute-start | bytes 221192 | tf_op jit(solution)/shard_map/ppermute | solution.py:398
  10.7 6.2 %collective-permute-start.1 = (bf16[2,2,9216]{2,1,0:T(2,128)(2,1)S(1)}, bf16[2,2,9216]{2,1,0:T(2,128)(2,1)S(1)}, u32[]{:S(2)}, u32[]{:S(2)}) collective-permute-start(bf16[2,2,9216]{2,1,0:T(2,128)(2,1)S(1)} %merge.1.p0), channel_id=1, source_target_pairs={{0,4},{2,6},{4,8},{6,10},{8,12},{10,14},{12,0},{14,2},{1,5},{3,7},... | collective-permute-start | bytes 221192 | tf_op jit(solution)/shard_map/ppermute | solution.py:398
  17.1 1.4 %collective-permute-start.4 = (bf16[16,4096]{1,0:T(8,128)(2,1)S(1)}, bf16[16,4096]{1,0:T(8,128)(2,1)S(1)}, u32[]{:S(2)}, u32[]{:S(2)}) collective-permute-start(bf16[16,4096]{1,0:T(8,128)(2,1)S(1)} %get-tuple-element.17.x_ref), channel_id=1, source_target_pairs={{0,1},{1,0},{2,3},{3,2},{4,5},{5,4},{6,7},{7,6},{8,9},{9,8},{10,11... | collective-permute-start | bytes 393224 | tf_op jit(solution)/shard_map/ppermute | solution.py:403
  20.5 11.7 %all-to-all-start = ((bf16[8,16,512]{2,1,0:T(8,128)(2,1)}), bf16[8,16,512]{2,1,0:T(8,128)(2,1)S(1)}, u32[]{:S(2)}, u32[]{:S(2)}) async-start(bf16[8,16,512]{2,1,0:T(8,128)(2,1)} %get-tuple-element.24), calls=%async_computation | async-start | bytes 262144 | tf_op jit(solution)/shard_map/all_to_all | solution.py:406
  30.0 1.4 %collective-permute-start.5 = (f32[16,1280]{1,0:T(8,128)S(1)}, f32[16,1280]{1,0:T(8,128)S(1)}, u32[]{:S(2)}, u32[]{:S(2)}) collective-permute-start(f32[16,1280]{1,0:T(8,128)S(1)} %rotate_grads.1.own_ref), channel_id=1, source_target_pairs={{0,1},{1,0},{2,3},{3,2},{4,5},{5,4},{6,7},{7,6},{8,9},{9,8},{10,11... | collective-permute-start | bytes 245768 | tf_op jit(solution)/shard_map/ppermute | solution.py:408

commit v7 on v6

--- a/solution.py
+++ b/solution.py
@@ -52,17 +52,18 @@
     return correction / total_tokens
 
 
-def pairs_kernel(len_ref, plan_ref, s1a_ref, s2a_ref, s1g_ref, s2g_ref, perm_ref):
-    docs = len_ref.shape[1]
+def pairs_kernel(docs_ref, s1a_ref, s2a_ref, s1g_ref, s2g_ref, perm_ref):
+    docs = docs_ref.shape[1]
+    lengths, plan = docs_ref[0:1], docs_ref[1:2]
     tokens = perm_ref.shape[0]
     grid_pairs = tokens * tokens
     me = lax.axis_index("row")
     upper = (iota((docs, docs), 0) <= iota((docs, docs), 1)).astype(F32)
-    ends = dot(jnp.broadcast_to(len_ref[...].astype(F32), (8, docs)), upper)[0:1]
+    ends = dot(jnp.broadcast_to(lengths.astype(F32), (8, docs)), upper)[0:1]
     position = iota((tokens, docs), 0).astype(F32)
     doc = jnp.sum((ends <= position).astype(F32), axis=1, keepdims=True)
     onehot = doc == iota((tokens, docs), 1).astype(F32)
-    seq = jnp.sum(jnp.where(onehot, plan_ref[...].astype(F32), 0.0), axis=1, keepdims=True)
+    seq = jnp.sum(jnp.where(onehot, plan.astype(F32), 0.0), axis=1, keepdims=True)
     p_lane = iota((tokens, grid_pairs), 1)
     t_sub = iota((tokens, grid_pairs), 0)
     first = lax.div(p_lane, tokens)
@@ -84,7 +85,7 @@
     s2 = dot(pick, jnp.where(is_second, 1.0, 0.0).astype(BF16)).astype(BF16)
     token = iota((tokens, tokens), 0)
     slot = iota((tokens, tokens), 1)
-    source = ((me + 8 - 2 * (slot >> 2)) & 7) ^ ((slot >> 1) & 1)
+    source = me ^ (2 * (slot >> 2)) ^ ((slot >> 1) & 1)
     perm = (token == 2 * source + (slot & 1)).astype(BF16)
     s1a_ref[...] = s1
     s2a_ref[...] = s2
@@ -98,12 +99,12 @@
     return pl.pallas_call(
         pairs_kernel,
         out_shape=(sel, sel, sel, sel, jax.ShapeDtypeStruct((tokens, tokens), BF16)),
-        in_specs=[VMEM, VMEM],
+        in_specs=[VMEM],
         out_specs=(VMEM,) * 5,
         compiler_params=pltpu.CompilerParams(vmem_limit_bytes=2 * MIB),
         cost_estimate=pl.CostEstimate(flops=2_000_000, bytes_accessed=40_000, transcendentals=0),
         name="pairs",
-    )(doc_lengths[None, :], doc_plan[None, :])
+    )(jnp.stack([doc_lengths, doc_plan]))
 
 
 def pack_kernel(acts_ref, grads_ref, o_ref, sems):
@@ -126,7 +127,7 @@
         in_specs=[HBM, HBM],
         out_specs=VMEM,
         scratch_shapes=[pltpu.SemaphoreType.DMA((2,))],
-        cost_estimate=pl.CostEstimate(flops=0, bytes_accessed=80_000, transcendentals=0),
+        cost_estimate=pl.CostEstimate(flops=0, bytes_accessed=2_000_000, transcendentals=0),
         name="pack",
     )(acts, grads)
 
@@ -147,21 +148,21 @@
     )(own)
 
 
-def merge_kernel(own_ref, beside_ref, o_ref):
+def merge_kernel(own_ref, beside_ref, perm_ref, o_ref):
     o_ref[0] = own_ref[...]
     o_ref[1] = beside_ref[...]
 
 
-def merge(own, beside):
+def merge(own, beside, perm):
     return pl.pallas_call(
         merge_kernel,
         out_shape=jax.ShapeDtypeStruct((2,) + own.shape, BF16),
-        in_specs=[VMEM] * 2,
+        in_specs=[VMEM] * 3,
         out_specs=VMEM,
         compiler_params=pltpu.CompilerParams(vmem_limit_bytes=2 * MIB),
         cost_estimate=pl.CostEstimate(flops=10_000, bytes_accessed=150_000, transcendentals=0),
         name="merge",
-    )(own, beside)
+    )(own, beside, perm)
 
 
 def assemble_kernel(width, p0, p1, p2, p3, basis_ref, perm_ref, acts_ref, grads_ref):
@@ -391,14 +392,14 @@
     tokens = n_row * acts.shape[0]
     width = acts.shape[1]
 
+    s1a, s2a, s1g, s2g, perm = make_pairs(doc_lengths, doc_plan, tokens)
     own = pack(acts, grads)
     beside = lax.ppermute(own, "row", [(i, i ^ 1) for i in range(n_row)])
-    both = merge(stage(own), beside)
+    both = merge(stage(own), beside, perm)
     pieces = [both] + [
-        lax.ppermute(both, "row", [(i, (i + 2 * k) % n_row) for i in range(n_row)]) for k in range(1, 4)
+        lax.ppermute(both, "row", [(i, i ^ (2 * k)) for i in range(n_row)]) for k in range(1, 4)
     ]
     basis = load(eigen_a)
-    s1a, s2a, s1g, s2g, perm = make_pairs(doc_lengths, doc_plan, tokens)
     acts_own, grads_own = assemble(pieces, basis, perm, width)
     acts_other = lax.ppermute(acts_own, "col", [(0, 1), (1, 0)])
     part, head0 = rotate_acts(basis, acts_own, eigen_s_rows)

time: 40.4 us -> 40.2 us (level)
  other arithmetic: 0 us -> 0.68 us
  waiting for transfers between devices: 3.69 us -> 3.19 us
    ppermute x1, waiting for transfers between devices: 1.34 us -> 0.01 us  [few_tokens_body(): beside = lax.ppermute(own, 'row', [(i, i ^ 1) for i in range(n_row)])]
    another operation x0 -> x1, other arithmetic: none -> 0.68 us  [make_pairs(): jnp.stack([doc_lengths, doc_plan])]
    ppermute x3, waiting for transfers between devices: 1.01 us -> 1.67 us  [few_tokens_body(): lax.ppermute(both, 'row', [(i, i ^ 2 * k) for i in range(n_row)])]
    ppermute x3, starting transfers between devices: 5.2 us -> 4.74 us  [few_tokens_body(): lax.ppermute(both, 'row', [(i, i ^ 2 * k) for i in range(n_row)])]
    unnamed x6 -> x2, local copies, waits for them, and re-layouts: 0.81 us -> 0.77 us
  transfers between devices with their start and end apart: 7 -> 7, of which waited for: 5 -> 3; matrix products, arithmetic and copies ran while one was open for 0% -> 2% of each run, Pallas kernels for 28% -> 28%
where the time goes in v7:
time: 40.2 us; the launch traced here: 39.7 us
  Pallas kernels  22.6 us (56%)
  starting transfers between devices  12.4 us (31%)
  waiting for transfers between devices  3.19 us (8%)
  local copies, waits for them, and re-layouts  0.77 us (2%)
  other arithmetic  0.68 us (2%)
    pallas_call x1, Pallas kernels, correct(): pl.pallas_call(correct_kernel, out_shape=jax.ShapeDtypeStruct((rows, n_ro...  7.72 us
    pallas_call x1, Pallas kernels, rotate_grads(): pl.pallas_call(rotate_grads_kernel, out_shape=jax.ShapeDtypeStruct((token...  5.41 us
    ppermute x3, starting transfers between devices, few_tokens_body(): lax.ppermute(both, 'row', [(i, i ^ 2 * k) for i in range(n_row)])  4.74 us
    all_to_all x1, starting transfers between devices, few_tokens_body(): a_all = lax.all_to_all(copies, 'row', 0, 0)  4.32 us
    pallas_call x1, Pallas kernels, load(): pl.pallas_call(load_kernel, out_shape=jax.ShapeDtypeStruct(w.shape, w.dty...  3.39 us
    ppermute x1, starting transfers between devices, few_tokens_body(): beside = lax.ppermute(own, 'row', [(i, i ^ 1) for i in range(n_row)])  3 us
    pallas_call x1, Pallas kernels, rotate_acts(): pl.pallas_call(rotate_second_kernel, out_shape=(jax.ShapeDtypeStruct((cop...  2.02 us
    ppermute x3, waiting for transfers between devices, few_tokens_body(): lax.ppermute(both, 'row', [(i, i ^ 2 * k) for i in range(n_row)])  1.67 us
  transfers between devices with their start and end apart: 7, of which 3 were waited for; matrix products, arithmetic and copies ran while one was open for 2% of the time, Pallas kernels for 28%

profile of v7, /device:TPU:0, one launch (start us, length us, event | category | flops | bytes accessed | tf_op | source)
XLA Modules:
  0.0 39.7 jit_solution(10859654223915705329)
XLA Ops:
  0.0 1.4 %pack.1.own_ref = bf16[2,9216]{1,0:T(2,128)(2,1)} custom-call(bf16[2,4096]{1,0:T(2,128)(2,1)} %acts_ref.1, bf16[2,5120]{1,0:T(2,128)(2,1)} %grads_ref.1), custom_call_target="tpu_custom_call" | custom-call | bytes 2000000 | tf_op jit(solution)/shard_map/pack/pallas_call | solution.py:124
  1.4 3.0 %collective-permute-start = (bf16[2,9216]{1,0:T(2,128)(2,1)}, bf16[2,9216]{1,0:T(2,128)(2,1)S(1)}, u32[]{:S(2)}, u32[]{:S(2)}) collective-permute-start(bf16[2,9216]{1,0:T(2,128)(2,1)} %pack.1.own_ref), channel_id=1, source_target_pairs={{0,2},{2,0},{4,6},{6,4},{8,10},{10,8},{12,14},{14,12},{1,3},{3,1},... | collective-permute-start | bytes 110600 | tf_op jit(solution)/shard_map/ppermute | solution.py:397
  4.4 0.7 %pad_add_fusion.docs_ref = s32[2,12]{1,0:T(2,128)S(1)} fusion(s32[1,12]{1,0:T(1,128)} %bitcast.2, s32[1,12]{1,0:T(1,128)} %bitcast.3), kind=kLoop, calls=%fused_computation | loop fusion | flops 24 | bytes 192 | tf_op jit(solution)/shard_map/stack | solution.py:107
  5.1 0.8 %copy-done = bf16[2,9216]{1,0:T(2,128)(2,1)S(1)} copy-done((bf16[2,9216]{1,0:T(2,128)(2,1)S(1)}, bf16[2,9216]{1,0:T(2,128)(2,1)}, u32[]{:S(2)}) %copy-start) | copy-done | bytes 36888
  5.8 0.7 %pairs.1 = (bf16[80,16]{1,0:T(8,128)(2,1)S(1)}, bf16[80,16]{1,0:T(8,128)(2,1)S(1)}, bf16[80,16]{1,0:T(8,128)(2,1)S(1)}, bf16[80,16]{1,0:T(8,128)(2,1)S(1)}, bf16[16,16]{1,0:T(8,128)(2,1)S(1)}) custom-call(s32[2,12]{1,0:T(2,128)S(1)} %pad_add_fusion.docs_ref), custom_call_target="tpu_custom_call" | custom-call | flops 2000000 | bytes 40000 | tf_op jit(solution)/shard_map/pairs/pallas_call | solution.py:99
  6.5 0.0 collective-permute-done.beside_ref
  6.6 4.1 %collective-permute-start.3 = (bf16[2,2,9216]{2,1,0:T(2,128)(2,1)S(1)}, bf16[2,2,9216]{2,1,0:T(2,128)(2,1)S(1)}, u32[]{:S(2)}, u32[]{:S(2)}) collective-permute-start(bf16[2,2,9216]{2,1,0:T(2,128)(2,1)S(1)} %merge.1.p0), channel_id=1, source_target_pairs={{0,12},{2,14},{4,8},{6,10},{8,4},{10,6},{12,0},{14,2},{1,13},{3,15... | collective-permute-start | bytes 221192 | tf_op jit(solution)/shard_map/ppermute | solution.py:400
  10.7 0.0 collective-permute-start.2
  10.7 0.6 %collective-permute-start.1 = (bf16[2,2,9216]{2,1,0:T(2,128)(2,1)S(1)}, bf16[2,2,9216]{2,1,0:T(2,128)(2,1)S(1)}, u32[]{:S(2)}, u32[]{:S(2)}) collective-permute-start(bf16[2,2,9216]{2,1,0:T(2,128)(2,1)S(1)} %merge.1.p0), channel_id=1, source_target_pairs={{0,4},{2,6},{4,0},{6,2},{8,12},{10,14},{12,8},{14,10},{1,5},{3,7},... | collective-permute-start | bytes 221192 | tf_op jit(solution)/shard_map/ppermute | solution.py:400
  11.3 3.4 %load.1.basis_ref.w_ref = bf16[1,512,8192]{2,1,0:T(8,128)(2,1)S(1)} custom-call(bf16[1,512,8192]{2,1,0:T(8,128)(2,1)} %w_ref.2), custom_call_target="tpu_custom_call" | custom-call | bytes 8388608 | tf_op jit(solution)/shard_map/load/pallas_call | solution.py:202
  14.7 0.0 collective-permute-done.3.p3
  14.7 1.7 %collective-permute-done.2.p2 = bf16[2,2,9216]{2,1,0:T(2,128)(2,1)S(1)} collective-permute-done((bf16[2,2,9216]{2,1,0:T(2,128)(2,1)S(1)}, bf16[2,2,9216]{2,1,0:T(2,128)(2,1)S(1)}, u32[]{:S(2)}, u32[]{:S(2)}) %collective-permute-start.2) | collective-permute-done | bytes 73760 | tf_op jit(solution)/shard_map/ppermute | solution.py:400
  16.4 0.0 collective-permute-done.1.p1
  16.4 0.2 assemble.1
  16.6 0.1 collective-permute-start.4
  16.7 1.3 %rotate_first.1 = (f32[512,16]{1,0:T(8,128)S(1)}, bf16[128,5120]{1,0:T(8,128)(2,1)S(1)}) custom-call(bf16[1,512,8192]{2,1,0:T(8,128)(2,1)S(1)} %load.1.basis_ref.w_ref, bf16[16,4096]{1,0:T(8,128)(2,1)S(1)} %get-tuple-element.17.x_ref, bf16[1280,5120]{1,0:T(8,128)(2,1)} %w_ref.3), custom_call_target="tpu_custom_call" | custom-call | flops 1073741824 | bytes 4194304 | tf_op jit(solution)/shard_map/rotate_first/pallas_call | solution.py:254
  18.0 2.0 %rotate_second.1 = (bf16[8,16,512]{2,1,0:T(8,128)(2,1)}, bf16[128,5120]{1,0:T(8,128)(2,1)S(1)}) custom-call(bf16[1,512,8192]{2,1,0:T(8,128)(2,1)S(1)} %load.1.basis_ref.w_ref, bf16[16,4096]{1,0:T(8,128)(2,1)S(1)} %collective-permute-done.4.x_ref, f32[512,16]{1,0:T(8,128)S(1)} %get-tuple-element.19.part_ref, bf16[16,16]{1,0:T(8,128)(2,1)S(1)} %get-tuple-element.16.perm_ref, ...), custom_call_target="tpu_custom_call" | custom-call | flops 1073741824 | bytes 4194304 | tf_op jit(solution)/shard_map/rotate_second/pallas_call | solution.py:267
  20.0 4.3 %all-to-all-start = ((bf16[8,16,512]{2,1,0:T(8,128)(2,1)}), bf16[8,16,512]{2,1,0:T(8,128)(2,1)S(1)}, u32[]{:S(2)}, u32[]{:S(2)}) async-start(bf16[8,16,512]{2,1,0:T(8,128)(2,1)} %get-tuple-element.24), calls=%async_computation | async-start | bytes 262144 | tf_op jit(solution)/shard_map/all_to_all | solution.py:407
  24.4 5.4 %rotate_grads.1.own_ref = f32[16,1280]{1,0:T(8,128)S(1)} custom-call(bf16[128,5120]{1,0:T(8,128)(2,1)S(1)} %get-tuple-element.18.head0_ref, bf16[128,5120]{1,0:T(8,128)(2,1)S(1)} %get-tuple-element.20.head1_ref, bf16[1280,5120]{1,0:T(8,128)(2,1)} %w_ref.3, bf16[16,5120]{1,0:T(8,128)(2,1)S(1)} %get-tuple-element.21.x_ref), custom_call_target="tpu_custom_call" | custom-call | flops 3355443200 | bytes 13107200 | tf_op jit(solution)/shard_map/rotate_grads/pallas_call | solution.py:307
  29.8 0.3 collective-permute-start.5
  30.1 1.1 %collective-permute-done.5.other_ref = f32[16,1280]{1,0:T(8,128)S(1)} collective-permute-done((f32[16,1280]{1,0:T(8,128)S(1)}, f32[16,1280]{1,0:T(8,128)S(1)}, u32[]{:S(2)}, u32[]{:S(2)}) %collective-permute-start.5) | collective-permute-done | bytes 81952 | tf_op jit(solution)/shard_map/ppermute | solution.py:409
  31.1 0.4 %pair_grads.1.g_ref = bf16[1280,240]{1,0:T(8,128)(2,1)S(1)} custom-call(f32[16,1280]{1,0:T(8,128)S(1)} %rotate_grads.1.own_ref, f32[16,1280]{1,0:T(8,128)S(1)} %collective-permute-done.5.other_ref, bf16[80,16]{1,0:T(8,128)(2,1)S(1)} %get-tuple-element.22.s1_ref, bf16[80,16]{1,0:T(8,128)(2,1)S(1)} %get-tuple-element.23.s2_ref), custom_call_target="tpu_custom_call" | custom-call | flops 2000000 | bytes 2000000 | tf_op jit(solution)/shard_map/pair_grads/pallas_call | solution.py:337
  31.5 0.5 %all-to-all-done.a_ref = bf16[8,16,512]{2,1,0:T(8,128)(2,1)S(1)} async-done(((bf16[8,16,512]{2,1,0:T(8,128)(2,1)}), bf16[8,16,512]{2,1,0:T(8,128)(2,1)S(1)}, u32[]{:S(2)}, u32[]{:S(2)}) %all-to-all-start) | async-done | bytes 131104 | tf_op jit(solution)/shard_map/all_to_all | solution.py:407
  32.0 7.7 %correct.1 = f32[1280,4096]{1,0:T(8,128)} custom-call(bf16[1280,240]{1,0:T(8,128)(2,1)S(1)} %pair_grads.1.g_ref, bf16[8,16,512]{2,1,0:T(8,128)(2,1)S(1)} %all-to-all-done.a_ref, bf16[80,16]{1,0:T(8,128)(2,1)S(1)} %get-tuple-element.25.s1_ref, bf16[80,16]{1,0:T(8,128)(2,1)S(1)} %get-tuple-element.26.s2_ref), custom_call_target="tpu_custom_call" | custom-call | flops 2684354560 | bytes 20971520 | tf_op jit(solution)/shard_map/correct/pallas_call | solution.py:373
  (4 shorter events, 0.0 us)
Async XLA Ops:
  1.4 5.2 %collective-permute-start = (bf16[2,9216]{1,0:T(2,128)(2,1)}, bf16[2,9216]{1,0:T(2,128)(2,1)S(1)}, u32[]{:S(2)}, u32[]{:S(2)}) collective-permute-start(bf16[2,9216]{1,0:T(2,128)(2,1)} %pack.1.own_ref), channel_id=1, source_target_pairs={{0,2},{2,0},{4,6},{6,4},{8,10},{10,8},{12,14},{14,12},{1,3},{3,1},... | collective-permute-start | bytes 110600 | tf_op jit(solution)/shard_map/ppermute | solution.py:397
  5.1 0.8 %copy-start = (bf16[2,9216]{1,0:T(2,128)(2,1)S(1)}, bf16[2,9216]{1,0:T(2,128)(2,1)}, u32[]{:S(2)}) copy-start(bf16[2,9216]{1,0:T(2,128)(2,1)} %pack.1.own_ref) | copy-start | bytes 110596
  6.6 8.1 %collective-permute-start.3 = (bf16[2,2,9216]{2,1,0:T(2,128)(2,1)S(1)}, bf16[2,2,9216]{2,1,0:T(2,128)(2,1)S(1)}, u32[]{:S(2)}, u32[]{:S(2)}) collective-permute-start(bf16[2,2,9216]{2,1,0:T(2,128)(2,1)S(1)} %merge.1.p0), channel_id=1, source_target_pairs={{0,12},{2,14},{4,8},{6,10},{8,4},{10,6},{12,0},{14,2},{1,13},{3,15... | collective-permute-start | bytes 221192 | tf_op jit(solution)/shard_map/ppermute | solution.py:400
  10.7 5.7 %collective-permute-start.2 = (bf16[2,2,9216]{2,1,0:T(2,128)(2,1)S(1)}, bf16[2,2,9216]{2,1,0:T(2,128)(2,1)S(1)}, u32[]{:S(2)}, u32[]{:S(2)}) collective-permute-start(bf16[2,2,9216]{2,1,0:T(2,128)(2,1)S(1)} %merge.1.p0), channel_id=1, source_target_pairs={{0,8},{2,10},{4,12},{6,14},{8,0},{10,2},{12,4},{14,6},{1,9},{3,11}... | collective-permute-start | bytes 221192 | tf_op jit(solution)/shard_map/ppermute | solution.py:400
  10.7 5.7 %collective-permute-start.1 = (bf16[2,2,9216]{2,1,0:T(2,128)(2,1)S(1)}, bf16[2,2,9216]{2,1,0:T(2,128)(2,1)S(1)}, u32[]{:S(2)}, u32[]{:S(2)}) collective-permute-start(bf16[2,2,9216]{2,1,0:T(2,128)(2,1)S(1)} %merge.1.p0), channel_id=1, source_target_pairs={{0,4},{2,6},{4,0},{6,2},{8,12},{10,14},{12,8},{14,10},{1,5},{3,7},... | collective-permute-start | bytes 221192 | tf_op jit(solution)/shard_map/ppermute | solution.py:400
  16.6 1.4 %collective-permute-start.4 = (bf16[16,4096]{1,0:T(8,128)(2,1)S(1)}, bf16[16,4096]{1,0:T(8,128)(2,1)S(1)}, u32[]{:S(2)}, u32[]{:S(2)}) collective-permute-start(bf16[16,4096]{1,0:T(8,128)(2,1)S(1)} %get-tuple-element.17.x_ref), channel_id=1, source_target_pairs={{0,1},{1,0},{2,3},{3,2},{4,5},{5,4},{6,7},{7,6},{8,9},{9,8},{10,11... | collective-permute-start | bytes 393224 | tf_op jit(solution)/shard_map/ppermute | solution.py:404
  20.0 12.0 %all-to-all-start = ((bf16[8,16,512]{2,1,0:T(8,128)(2,1)}), bf16[8,16,512]{2,1,0:T(8,128)(2,1)S(1)}, u32[]{:S(2)}, u32[]{:S(2)}) async-start(bf16[8,16,512]{2,1,0:T(8,128)(2,1)} %get-tuple-element.24), calls=%async_computation | async-start | bytes 262144 | tf_op jit(solution)/shard_map/all_to_all | solution.py:407
  29.8 1.3 %collective-permute-start.5 = (f32[16,1280]{1,0:T(8,128)S(1)}, f32[16,1280]{1,0:T(8,128)S(1)}, u32[]{:S(2)}, u32[]{:S(2)}) collective-permute-start(f32[16,1280]{1,0:T(8,128)S(1)} %rotate_grads.1.own_ref), channel_id=1, source_target_pairs={{0,1},{1,0},{2,3},{3,2},{4,5},{5,4},{6,7},{7,6},{8,9},{9,8},{10,11... | collective-permute-start | bytes 245768 | tf_op jit(solution)/shard_map/ppermute | solution.py:409

commit v8 on v7

--- a/solution.py
+++ b/solution.py
@@ -107,47 +107,6 @@
     )(jnp.stack([doc_lengths, doc_plan]))
 
 
-def pack_kernel(acts_ref, grads_ref, o_ref, sems):
-    width = acts_ref.shape[1]
-    copies = (
-        pltpu.make_async_copy(acts_ref, o_ref.at[:, :width], sems.at[0]),
-        pltpu.make_async_copy(grads_ref, o_ref.at[:, width:], sems.at[1]),
-    )
-    for copy in copies:
-        copy.start()
-    for copy in copies:
-        copy.wait()
-
-
-def pack(acts, grads):
-    rows, width = acts.shape
-    return pl.pallas_call(
-        pack_kernel,
-        out_shape=jax.ShapeDtypeStruct((rows, width + grads.shape[1]), BF16),
-        in_specs=[HBM, HBM],
-        out_specs=VMEM,
-        scratch_shapes=[pltpu.SemaphoreType.DMA((2,))],
-        cost_estimate=pl.CostEstimate(flops=0, bytes_accessed=2_000_000, transcendentals=0),
-        name="pack",
-    )(acts, grads)
-
-
-def stage_kernel(own_ref, o_ref):
-    o_ref[...] = own_ref[...]
-
-
-def stage(own):
-    return pl.pallas_call(
-        stage_kernel,
-        out_shape=jax.ShapeDtypeStruct(own.shape, BF16),
-        in_specs=[VMEM],
-        out_specs=VMEM,
-        compiler_params=pltpu.CompilerParams(vmem_limit_bytes=2 * MIB),
-        cost_estimate=pl.CostEstimate(flops=10_000, bytes_accessed=2_000_000, transcendentals=0),
-        name="stage",
-    )(own)
-
-
 def merge_kernel(own_ref, beside_ref, perm_ref, o_ref):
     o_ref[0] = own_ref[...]
     o_ref[1] = beside_ref[...]
@@ -393,9 +352,9 @@
     width = acts.shape[1]
 
     s1a, s2a, s1g, s2g, perm = make_pairs(doc_lengths, doc_plan, tokens)
-    own = pack(acts, grads)
+    own = jnp.concatenate([acts, grads], axis=1)
     beside = lax.ppermute(own, "row", [(i, i ^ 1) for i in range(n_row)])
-    both = merge(stage(own), beside, perm)
+    both = merge(own, beside, perm)
     pieces = [both] + [
         lax.ppermute(both, "row", [(i, i ^ (2 * k)) for i in range(n_row)]) for k in range(1, 4)
     ]

time: 40.2 us -> 40 us (level)
  Pallas kernels: 22.6 us -> 21.2 us
  local copies, waits for them, and re-layouts: 0.77 us -> 1.48 us
    pallas_call x2 -> x0, Pallas kernels: 1.38 us -> none  [the longest x1 1.38 us: pack(): pl.pallas_call(pack_kernel, out_shape=jax.ShapeDtypeStruct((rows, width +...]
    concatenate x0 -> x1, local copies, waits for them, and re-layouts: none -> 0.75 us  [few_tokens_body(): own = jnp.concatenate([acts, grads], axis=1)]
    ppermute x1, waiting for transfers between devices: 0.01 us -> 0.55 us  [few_tokens_body(): beside = lax.ppermute(own, 'row', [(i, i ^ 1) for i in range(n_row)])]
  transfers between devices with their start and end apart: 7 -> 7, of which waited for: 3 -> 4; matrix products, arithmetic and copies ran while one was open for 2% -> 2% of each run, Pallas kernels for 28% -> 28%
where the time goes in v8:
time: 40 us; the launch traced here: 39.6 us
  Pallas kernels  21.2 us (53%)
  starting transfers between devices  12.7 us (32%)
  waiting for transfers between devices  3.47 us (9%)
  local copies, waits for them, and re-layouts  1.48 us (4%)
  other arithmetic  0.68 us (2%)
    pallas_call x1, Pallas kernels, correct(): pl.pallas_call(correct_kernel, out_shape=jax.ShapeDtypeStruct((rows, n_ro...  7.72 us
    pallas_call x1, Pallas kernels, rotate_grads(): pl.pallas_call(rotate_grads_kernel, out_shape=jax.ShapeDtypeStruct((token...  5.41 us
    ppermute x3, starting transfers between devices, few_tokens_body(): lax.ppermute(both, 'row', [(i, i ^ 2 * k) for i in range(n_row)])  4.77 us
    all_to_all x1, starting transfers between devices, few_tokens_body(): a_all = lax.all_to_all(copies, 'row', 0, 0)  4.42 us
    pallas_call x1, Pallas kernels, load(): pl.pallas_call(load_kernel, out_shape=jax.ShapeDtypeStruct(w.shape, w.dty...  3.39 us
    ppermute x1, starting transfers between devices, few_tokens_body(): beside = lax.ppermute(own, 'row', [(i, i ^ 1) for i in range(n_row)])  3 us
    pallas_call x1, Pallas kernels, rotate_acts(): pl.pallas_call(rotate_second_kernel, out_shape=(jax.ShapeDtypeStruct((cop...  2.03 us
    ppermute x3, waiting for transfers between devices, few_tokens_body(): lax.ppermute(both, 'row', [(i, i ^ 2 * k) for i in range(n_row)])  1.58 us
  transfers between devices with their start and end apart: 7, of which 4 were waited for; matrix products, arithmetic and copies ran while one was open for 2% of the time, Pallas kernels for 28%

profile of v8, /device:TPU:0, one launch (start us, length us, event | category | flops | bytes accessed | tf_op | source)
XLA Modules:
  0.0 39.6 jit_solution(2468947127662912926)
XLA Ops:
  0.0 0.7 %constant_dynamic-update-slice_fusion.1 = bf16[2,9216]{1,0:T(2,128)(2,1)S(1)} fusion(bf16[2,4096]{1,0:T(2,128)(2,1)} %param.6), kind=kLoop, calls=%fused_computation.1 | loop fusion | bytes 32768
  0.7 0.8 %constant_dynamic-update-slice_fusion.own_ref = bf16[2,9216]{1,0:T(2,128)(2,1)S(1)} fusion(bf16[2,9216]{1,0:T(2,128)(2,1)S(1)} %constant_dynamic-update-slice_fusion.1, bf16[2,5120]{1,0:T(2,128)(2,1)} %param.7), kind=kLoop, calls=%fused_computation | loop fusion | bytes 40960 | tf_op jit(solution)/shard_map/concatenate | solution.py:355
  1.5 3.0 %collective-permute-start = (bf16[2,9216]{1,0:T(2,128)(2,1)S(1)}, bf16[2,9216]{1,0:T(2,128)(2,1)S(1)}, u32[]{:S(2)}, u32[]{:S(2)}) collective-permute-start(bf16[2,9216]{1,0:T(2,128)(2,1)S(1)} %constant_dynamic-update-slice_fusion.own_ref), channel_id=1, source_target_pairs={{0,2},{2,0},{4,6},{6,4},{8,10},{10,8},{12,14},{14,12},{1,3},{3,1},... | collective-permute-start | bytes 110600 | tf_op jit(solution)/shard_map/ppermute | solution.py:356
  4.5 0.7 %pad_add_fusion.docs_ref = s32[2,12]{1,0:T(2,128)S(1)} fusion(s32[1,12]{1,0:T(1,128)} %bitcast.2, s32[1,12]{1,0:T(1,128)} %bitcast.3), kind=kLoop, calls=%fused_computation.2 | loop fusion | flops 24 | bytes 192 | tf_op jit(solution)/shard_map/stack | solution.py:107
  5.2 0.7 %pairs.1 = (bf16[80,16]{1,0:T(8,128)(2,1)S(1)}, bf16[80,16]{1,0:T(8,128)(2,1)S(1)}, bf16[80,16]{1,0:T(8,128)(2,1)S(1)}, bf16[80,16]{1,0:T(8,128)(2,1)S(1)}, bf16[16,16]{1,0:T(8,128)(2,1)S(1)}) custom-call(s32[2,12]{1,0:T(2,128)S(1)} %pad_add_fusion.docs_ref), custom_call_target="tpu_custom_call" | custom-call | flops 2000000 | bytes 40000 | tf_op jit(solution)/shard_map/pairs/pallas_call | solution.py:99
  5.9 0.6 %collective-permute-done.beside_ref = bf16[2,9216]{1,0:T(2,128)(2,1)S(1)} collective-permute-done((bf16[2,9216]{1,0:T(2,128)(2,1)S(1)}, bf16[2,9216]{1,0:T(2,128)(2,1)S(1)}, u32[]{:S(2)}, u32[]{:S(2)}) %collective-permute-start) | collective-permute-done | bytes 36896 | tf_op jit(solution)/shard_map/ppermute | solution.py:356
  6.4 4.1 %collective-permute-start.3 = (bf16[2,2,9216]{2,1,0:T(2,128)(2,1)S(1)}, bf16[2,2,9216]{2,1,0:T(2,128)(2,1)S(1)}, u32[]{:S(2)}, u32[]{:S(2)}) collective-permute-start(bf16[2,2,9216]{2,1,0:T(2,128)(2,1)S(1)} %merge.1.p0), channel_id=1, source_target_pairs={{0,12},{2,14},{4,8},{6,10},{8,4},{10,6},{12,0},{14,2},{1,13},{3,15... | collective-permute-start | bytes 221192 | tf_op jit(solution)/shard_map/ppermute | solution.py:359
  10.6 0.6 %collective-permute-start.1 = (bf16[2,2,9216]{2,1,0:T(2,128)(2,1)S(1)}, bf16[2,2,9216]{2,1,0:T(2,128)(2,1)S(1)}, u32[]{:S(2)}, u32[]{:S(2)}) collective-permute-start(bf16[2,2,9216]{2,1,0:T(2,128)(2,1)S(1)} %merge.1.p0), channel_id=1, source_target_pairs={{0,4},{2,6},{4,0},{6,2},{8,12},{10,14},{12,8},{14,10},{1,5},{3,7},... | collective-permute-start | bytes 221192 | tf_op jit(solution)/shard_map/ppermute | solution.py:359
  11.2 3.4 %load.1.basis_ref.w_ref = bf16[1,512,8192]{2,1,0:T(8,128)(2,1)S(1)} custom-call(bf16[1,512,8192]{2,1,0:T(8,128)(2,1)} %w_ref.2), custom_call_target="tpu_custom_call" | custom-call | bytes 8388608 | tf_op jit(solution)/shard_map/load/pallas_call | solution.py:161
  14.6 0.0 collective-permute-done.3.p3
  14.6 1.6 %collective-permute-done.2.p2 = bf16[2,2,9216]{2,1,0:T(2,128)(2,1)S(1)} collective-permute-done((bf16[2,2,9216]{2,1,0:T(2,128)(2,1)S(1)}, bf16[2,2,9216]{2,1,0:T(2,128)(2,1)S(1)}, u32[]{:S(2)}, u32[]{:S(2)}) %collective-permute-start.2) | collective-permute-done | bytes 73760 | tf_op jit(solution)/shard_map/ppermute | solution.py:359
  16.2 0.0 collective-permute-done.1.p1
  16.2 0.2 assemble.1
  16.4 0.1 collective-permute-start.4
  16.5 1.3 %rotate_first.1 = (f32[512,16]{1,0:T(8,128)S(1)}, bf16[128,5120]{1,0:T(8,128)(2,1)S(1)}) custom-call(bf16[1,512,8192]{2,1,0:T(8,128)(2,1)S(1)} %load.1.basis_ref.w_ref, bf16[16,4096]{1,0:T(8,128)(2,1)S(1)} %get-tuple-element.17.x_ref, bf16[1280,5120]{1,0:T(8,128)(2,1)} %w_ref.3), custom_call_target="tpu_custom_call" | custom-call | flops 1073741824 | bytes 4194304 | tf_op jit(solution)/shard_map/rotate_first/pallas_call | solution.py:213
  17.8 0.0 collective-permute-done.4.x_ref
  17.8 2.0 %rotate_second.1 = (bf16[8,16,512]{2,1,0:T(8,128)(2,1)}, bf16[128,5120]{1,0:T(8,128)(2,1)S(1)}) custom-call(bf16[1,512,8192]{2,1,0:T(8,128)(2,1)S(1)} %load.1.basis_ref.w_ref, bf16[16,4096]{1,0:T(8,128)(2,1)S(1)} %collective-permute-done.4.x_ref, f32[512,16]{1,0:T(8,128)S(1)} %get-tuple-element.19.part_ref, bf16[16,16]{1,0:T(8,128)(2,1)S(1)} %get-tuple-element.16.perm_ref, ...), custom_call_target="tpu_custom_call" | custom-call | flops 1073741824 | bytes 4194304 | tf_op jit(solution)/shard_map/rotate_second/pallas_call | solution.py:226
  19.9 4.4 %all-to-all-start = ((bf16[8,16,512]{2,1,0:T(8,128)(2,1)}), bf16[8,16,512]{2,1,0:T(8,128)(2,1)S(1)}, u32[]{:S(2)}, u32[]{:S(2)}) async-start(bf16[8,16,512]{2,1,0:T(8,128)(2,1)} %get-tuple-element.24), calls=%async_computation | async-start | bytes 262144 | tf_op jit(solution)/shard_map/all_to_all | solution.py:366
  24.3 5.4 %rotate_grads.1.own_ref = f32[16,1280]{1,0:T(8,128)S(1)} custom-call(bf16[128,5120]{1,0:T(8,128)(2,1)S(1)} %get-tuple-element.18.head0_ref, bf16[128,5120]{1,0:T(8,128)(2,1)S(1)} %get-tuple-element.20.head1_ref, bf16[1280,5120]{1,0:T(8,128)(2,1)} %w_ref.3, bf16[16,5120]{1,0:T(8,128)(2,1)S(1)} %get-tuple-element.21.x_ref), custom_call_target="tpu_custom_call" | custom-call | flops 3355443200 | bytes 13107200 | tf_op jit(solution)/shard_map/rotate_grads/pallas_call | solution.py:266
  29.7 0.4 %collective-permute-start.5 = (f32[16,1280]{1,0:T(8,128)S(1)}, f32[16,1280]{1,0:T(8,128)S(1)}, u32[]{:S(2)}, u32[]{:S(2)}) collective-permute-start(f32[16,1280]{1,0:T(8,128)S(1)} %rotate_grads.1.own_ref), channel_id=1, source_target_pairs={{0,1},{1,0},{2,3},{3,2},{4,5},{5,4},{6,7},{7,6},{8,9},{9,8},{10,11... | collective-permute-start | bytes 245768 | tf_op jit(solution)/shard_map/ppermute | solution.py:368
  30.1 0.9 %collective-permute-done.5.other_ref = f32[16,1280]{1,0:T(8,128)S(1)} collective-permute-done((f32[16,1280]{1,0:T(8,128)S(1)}, f32[16,1280]{1,0:T(8,128)S(1)}, u32[]{:S(2)}, u32[]{:S(2)}) %collective-permute-start.5) | collective-permute-done | bytes 81952 | tf_op jit(solution)/shard_map/ppermute | solution.py:368
  31.1 0.4 %pair_grads.1.g_ref = bf16[1280,240]{1,0:T(8,128)(2,1)S(1)} custom-call(f32[16,1280]{1,0:T(8,128)S(1)} %rotate_grads.1.own_ref, f32[16,1280]{1,0:T(8,128)S(1)} %collective-permute-done.5.other_ref, bf16[80,16]{1,0:T(8,128)(2,1)S(1)} %get-tuple-element.22.s1_ref, bf16[80,16]{1,0:T(8,128)(2,1)S(1)} %get-tuple-element.23.s2_ref), custom_call_target="tpu_custom_call" | custom-call | flops 2000000 | bytes 2000000 | tf_op jit(solution)/shard_map/pair_grads/pallas_call | solution.py:296
  31.5 0.4 %all-to-all-done.a_ref = bf16[8,16,512]{2,1,0:T(8,128)(2,1)S(1)} async-done(((bf16[8,16,512]{2,1,0:T(8,128)(2,1)}), bf16[8,16,512]{2,1,0:T(8,128)(2,1)S(1)}, u32[]{:S(2)}, u32[]{:S(2)}) %all-to-all-start) | async-done | bytes 131104 | tf_op jit(solution)/shard_map/all_to_all | solution.py:366
  31.9 7.7 %correct.1 = f32[1280,4096]{1,0:T(8,128)} custom-call(bf16[1280,240]{1,0:T(8,128)(2,1)S(1)} %pair_grads.1.g_ref, bf16[8,16,512]{2,1,0:T(8,128)(2,1)S(1)} %all-to-all-done.a_ref, bf16[80,16]{1,0:T(8,128)(2,1)S(1)} %get-tuple-element.25.s1_ref, bf16[80,16]{1,0:T(8,128)(2,1)S(1)} %get-tuple-element.26.s2_ref), custom_call_target="tpu_custom_call" | custom-call | flops 2684354560 | bytes 20971520 | tf_op jit(solution)/shard_map/correct/pallas_call | solution.py:332
  (2 shorter events, 0.0 us)
Async XLA Ops:
  1.5 4.9 %collective-permute-start = (bf16[2,9216]{1,0:T(2,128)(2,1)S(1)}, bf16[2,9216]{1,0:T(2,128)(2,1)S(1)}, u32[]{:S(2)}, u32[]{:S(2)}) collective-permute-start(bf16[2,9216]{1,0:T(2,128)(2,1)S(1)} %constant_dynamic-update-slice_fusion.own_ref), channel_id=1, source_target_pairs={{0,2},{2,0},{4,6},{6,4},{8,10},{10,8},{12,14},{14,12},{1,3},{3,1},... | collective-permute-start | bytes 110600 | tf_op jit(solution)/shard_map/ppermute | solution.py:356
  6.4 8.2 %collective-permute-start.3 = (bf16[2,2,9216]{2,1,0:T(2,128)(2,1)S(1)}, bf16[2,2,9216]{2,1,0:T(2,128)(2,1)S(1)}, u32[]{:S(2)}, u32[]{:S(2)}) collective-permute-start(bf16[2,2,9216]{2,1,0:T(2,128)(2,1)S(1)} %merge.1.p0), channel_id=1, source_target_pairs={{0,12},{2,14},{4,8},{6,10},{8,4},{10,6},{12,0},{14,2},{1,13},{3,15... | collective-permute-start | bytes 221192 | tf_op jit(solution)/shard_map/ppermute | solution.py:359
  10.6 5.6 %collective-permute-start.2 = (bf16[2,2,9216]{2,1,0:T(2,128)(2,1)S(1)}, bf16[2,2,9216]{2,1,0:T(2,128)(2,1)S(1)}, u32[]{:S(2)}, u32[]{:S(2)}) collective-permute-start(bf16[2,2,9216]{2,1,0:T(2,128)(2,1)S(1)} %merge.1.p0), channel_id=1, source_target_pairs={{0,8},{2,10},{4,12},{6,14},{8,0},{10,2},{12,4},{14,6},{1,9},{3,11}... | collective-permute-start | bytes 221192 | tf_op jit(solution)/shard_map/ppermute | solution.py:359
  10.6 5.6 %collective-permute-start.1 = (bf16[2,2,9216]{2,1,0:T(2,128)(2,1)S(1)}, bf16[2,2,9216]{2,1,0:T(2,128)(2,1)S(1)}, u32[]{:S(2)}, u32[]{:S(2)}) collective-permute-start(bf16[2,2,9216]{2,1,0:T(2,128)(2,1)S(1)} %merge.1.p0), channel_id=1, source_target_pairs={{0,4},{2,6},{4,0},{6,2},{8,12},{10,14},{12,8},{14,10},{1,5},{3,7},... | collective-permute-start | bytes 221192 | tf_op jit(solution)/shard_map/ppermute | solution.py:359
  16.4 1.4 %collective-permute-start.4 = (bf16[16,4096]{1,0:T(8,128)(2,1)S(1)}, bf16[16,4096]{1,0:T(8,128)(2,1)S(1)}, u32[]{:S(2)}, u32[]{:S(2)}) collective-permute-start(bf16[16,4096]{1,0:T(8,128)(2,1)S(1)} %get-tuple-element.17.x_ref), channel_id=1, source_target_pairs={{0,1},{1,0},{2,3},{3,2},{4,5},{5,4},{6,7},{7,6},{8,9},{9,8},{10,11... | collective-permute-start | bytes 393224 | tf_op jit(solution)/shard_map/ppermute | solution.py:363
  19.9 12.0 %all-to-all-start = ((bf16[8,16,512]{2,1,0:T(8,128)(2,1)}), bf16[8,16,512]{2,1,0:T(8,128)(2,1)S(1)}, u32[]{:S(2)}, u32[]{:S(2)}) async-start(bf16[8,16,512]{2,1,0:T(8,128)(2,1)} %get-tuple-element.24), calls=%async_computation | async-start | bytes 262144 | tf_op jit(solution)/shard_map/all_to_all | solution.py:366
  29.7 1.4 %collective-permute-start.5 = (f32[16,1280]{1,0:T(8,128)S(1)}, f32[16,1280]{1,0:T(8,128)S(1)}, u32[]{:S(2)}, u32[]{:S(2)}) collective-permute-start(f32[16,1280]{1,0:T(8,128)S(1)} %rotate_grads.1.own_ref), channel_id=1, source_target_pairs={{0,1},{1,0},{2,3},{3,2},{4,5},{5,4},{6,7},{7,6},{8,9},{9,8},{10,11... | collective-permute-start | bytes 245768 | tf_op jit(solution)/shard_map/ppermute | solution.py:368
